TPU v7x, 512 devices: a whole 4x8x8 slice. The times are simulated.
512 devices in a mesh: pb: 8 (over z), kv: 8 (over x, y_lo), ha: 8 (over y_hi, core).
Axes of the slice: x: 4, y: 8 (y_hi: 4, y_lo: 2; y = y_hi * 2 + y_lo), z: 8, core: 2. Of those that a mesh axis runs over, the one named last changes fastest.
Arguments:
- queries: bfloat16 [16384, 8192], P(('pb', 'kv', 'ha')), may hold values from -15 to 15
- keyvals: bfloat16 [2, 16384, 1024], P(None, ('pb', 'kv', 'ha')), may hold values from -6 to 6
- block_index: int32 [128, 16], P(('pb', 'kv')), may hold values from 0 to 127, as said below
- block_count: int32 [128], P(('pb', 'kv')), may hold values from 1 to 16, as said below
Outputs:
- attended: bfloat16 [16384, 8192], P(('pb', 'kv', 'ha'))
Inputs may be any that keep to these rules, and one draw needn't show every extreme that they name: `block_index`: row i lists block_count[i] distinct blocks: first i, then i - 1 down to i - 2 where these are 0 or more, then blocks j <= i - 3 with j % 2 == 0, the largest such j first whenever one exists; the slots past the count hold i. `block_count`: some row uses all 16 slots.
All inputs are finite; a program needn't handle non-finite values.
Results may differ from a plain program's by a relative error of at most 0.0035.
Values may be sent and summed in bfloat16 or wider, within the bound.
No kernel may reach another device: no remote copies, remote signals or barrier semaphores. Data moves between devices by JAX's collectives and lax.ppermute only.
A program may use at most 64 MiB of HBM per device.

v0:
```python
import math

import jax
import jax.numpy as jnp
from jax import lax
from jax.sharding import PartitionSpec as P

HEAD_SIZE = 128
BLOCK_POSITIONS = 128
LOCAL = 3
MAXB = 16


per_group = 4


def passed_along(array, axis, by):
    size = lax.axis_size(axis)
    pairs = [(i, i + by) for i in range(size) if 0 <= i + by < size]
    return lax.ppermute(array, axis, pairs)


def body(queries, keyvals, block_index, block_count):
    moved_q, moved_kv = (
        lax.all_to_all(queries[None], "ha", split_axis=2, concat_axis=1, tiled=True),
        lax.all_to_all(keyvals, "ha", split_axis=2, concat_axis=1, tiled=True),
    )
    local_q = moved_q[0]
    tokens = local_q.shape[0]
    blocks = tokens // BLOCK_POSITIONS
    feature_columns = moved_kv.shape[2]
    kv_heads = feature_columns // HEAD_SIZE
    query_head_group = local_q.shape[1] // HEAD_SIZE // kv_heads
    shards = lax.axis_size(("pb", "kv"))
    first_block = lax.axis_index(("pb", "kv")) * blocks
    earlier = passed_along(moved_kv, ("pb", "kv"), 1)
    nearby = jnp.concatenate([earlier, moved_kv], axis=1)
    qnumber = first_block + jnp.arange(blocks, dtype=jnp.int32)
    distant = qnumber[:, None] - block_index >= LOCAL
    near_row = jnp.clip(block_index - first_block + LOCAL - 1, 0, LOCAL - 2 + blocks)
    owner_shard = block_index // blocks
    summary = moved_kv[:, :BLOCK_POSITIONS, :]
    gathered = lax.all_gather(summary, ("pb", "kv"), axis=1, tiled=True)
    lookup = jnp.concatenate([nearby, gathered], axis=1).reshape(
        2, LOCAL - 1 + blocks + shards, BLOCK_POSITIONS, feature_columns
    )
    table_row = jnp.where(distant, LOCAL - 1 + blocks + owner_shard, near_row)
    picked = jnp.take(lookup, table_row.reshape(-1), axis=1)
    picked = picked.reshape(2, blocks, MAXB, BLOCK_POSITIONS, feature_columns)
    score_scale = 1.0 / math.sqrt(HEAD_SIZE)
    qgroups = local_q.reshape(blocks, BLOCK_POSITIONS, kv_heads, query_head_group, HEAD_SIZE)
    sections = MAXB // per_group
    key_slot = jnp.arange(per_group * BLOCK_POSITIONS, dtype=jnp.int32)
    slot_of = key_slot // BLOCK_POSITIONS
    key_cell = key_slot % BLOCK_POSITIONS
    query_rows_ids = jnp.arange(BLOCK_POSITIONS, dtype=jnp.int32)

    def attend(inputs):
        query_rows, listed, listed_count, block_number = inputs
        local_index = block_number - first_block
        chosen = lax.dynamic_index_in_dim(picked, local_index, 1, keepdims=False)
        key_sets = chosen[0].reshape(sections, per_group * BLOCK_POSITIONS, kv_heads, HEAD_SIZE)
        value_sets = chosen[1].reshape(sections, per_group * BLOCK_POSITIONS, kv_heads, HEAD_SIZE)

        def section_scores(section):
            return (
                jnp.einsum(
                    "rgzd,kgd->gzrk",
                    query_rows,
                    key_sets[section],
                    preferred_element_type=jnp.float32,
                )
                * score_scale
            )

        def section_mask(section):
            listed_here = jnp.repeat(
                listed[section * per_group : (section + 1) * per_group], BLOCK_POSITIONS
            )
            slot_ok = section * per_group + slot_of < listed_count
            before = listed_here < block_number
            return slot_ok[None, :] & (
                before[None, :] | (key_cell[None, :] <= query_rows_ids[:, None])
            )

        row_peak = jnp.full((kv_heads, query_head_group, BLOCK_POSITIONS), -1e30, jnp.float32)
        for section in range(sections):
            masked = jnp.where(section_mask(section), section_scores(section), -1e30)
            row_peak = jnp.maximum(row_peak, jnp.max(masked, axis=-1))
        state = (
            jnp.zeros((kv_heads, query_head_group, BLOCK_POSITIONS), jnp.float32),
            jnp.zeros((BLOCK_POSITIONS, kv_heads, query_head_group, HEAD_SIZE), jnp.float32),
        )
        for section in range(sections):
            sum_totals, sum_numerator = state
            allowed = section_mask(section)
            weights = jnp.where(
                allowed, jnp.exp(section_scores(section) - row_peak[..., None]), 0.0
            )
            sum_totals = sum_totals + jnp.sum(weights, axis=-1)
            rounded = weights.astype(jnp.bfloat16)
            sum_numerator = sum_numerator + jnp.einsum(
                "gzrk,kgd->rgzd", rounded, value_sets[section], preferred_element_type=jnp.float32
            )
            state = (sum_totals, sum_numerator)
        totals, numerator = state
        output = numerator / jnp.transpose(totals, (2, 0, 1))[..., None]
        return output.astype(jnp.bfloat16).reshape(
            BLOCK_POSITIONS, kv_heads * query_head_group * HEAD_SIZE
        )

    result = lax.map(attend, (qgroups, block_index, block_count, qnumber))
    result = result.reshape(tokens, kv_heads * query_head_group * HEAD_SIZE)
    return lax.all_to_all(result, "ha", split_axis=0, concat_axis=1, tiled=True)


def solution(mesh):
    in_specs = (
        P(("pb", "kv", "ha"), None),
        P(None, ("pb", "kv", "ha"), None),
        P(("pb", "kv"), None),
        P(("pb", "kv")),
    )
    out_specs = P(("pb", "kv", "ha"), None)
    return jax.shard_map(body, mesh=mesh, in_specs=in_specs, out_specs=out_specs, check_vma=False)
```

profile of v0, /device:TPU:1, one launch (start us, length us, event | category | flops | bytes accessed | tf_op | source)
XLA Modules:
  0.0 406.0 jit_solution(11080000458962600864)
XLA Ops:
  6.5 1.3 copy.64
  8.3 17.3 %all_to_all.52 = bf16[8,2,4096]{2,1,0:T(2,128)(2,1)S(1)} all-to-all(bf16[8,2,4096]{2,1,0:T(2,128)(2,1)S(1)} %reshape.325), channel_id=1, replica_groups=mesh['pb'=8,'kv'=8,'ha'=8] {'ha'}, dimensions={0} | all-to-all | bytes 262144 | tf_op jit(solution)/shard_map/all_to_all | solution.py:26
  26.9 6.7 %copy.68 = bf16[1,32,8192]{1,0,2:T(2,128)(2,1)} copy(bf16[1,32,8192]{2,1,0:T(8,128)(2,1)S(1)} %bitcast.306) | data formatting | bytes 1048576 | tf_op jit(solution)/shard_map/broadcast_in_dim | solution.py:25
  34.2 45.2 %reduce.8 = bf16[8192,32]{1,0:T(8,128)(2,1)S(1)} reduce(bf16[8192,1,32]{2,1,0:T(2,128)(2,1)} %bitcast.283, bf16[]{:T(256)} %broadcast.226), dimensions={1}, to_apply=%bitcast.182.reduce_sub_computation | reduce | bytes 1048578
  79.4 2.7 reshape.327
  82.0 4.6 %all-to-all-start.1 = ((bf16[8,2,16384]{2,1,0:T(2,128)(2,1)}), bf16[8,2,16384]{2,1,0:T(2,128)(2,1)S(1)}, u32[]{:S(2)}, u32[]{:S(2)}) async-start(bf16[8,2,16384]{2,1,0:T(2,128)(2,1)} %reshape.327), calls=%async_computation.1 | async-start | bytes 1048576 | tf_op jit(solution)/shard_map/all_to_all | solution.py:25
  86.8 2.3 collective-permute-start
  89.2 17.0 %all-to-all-done.1 = bf16[8,2,16384]{2,1,0:T(2,128)(2,1)S(1)} async-done(((bf16[8,2,16384]{2,1,0:T(2,128)(2,1)}), bf16[8,2,16384]{2,1,0:T(2,128)(2,1)S(1)}, u32[]{:S(2)}, u32[]{:S(2)}) %all-to-all-start.1) | async-done | bytes 524320 | tf_op jit(solution)/shard_map/all_to_all | solution.py:25
  106.2 4.5 %reshape.328 = bf16[8192,1,32]{2,1,0:T(2,128)(2,1)} reshape(bf16[8,2,16384]{2,1,0:T(2,128)(2,1)S(1)} %all-to-all-done.1) | data formatting | bytes 1048576
  110.7 8.0 %copy.69 = bf16[1,32,8192]{2,1,0:T(8,128)(2,1)S(1)} copy(bf16[1,32,8192]{1,0,2:T(2,128)(2,1)} %bitcast.284) | data formatting | bytes 1048576 | tf_op jit(solution)/shard_map/all_to_all | solution.py:25
  119.5 179.3 %all-gather.2.cloned.1.call-done = bf16[2,8192,128]{2,1,0:T(8,128)(2,1)} async-done(((bf16[2,128,128]{2,1,0:T(8,128)(2,1)}), bf16[2,8192,128]{2,1,0:T(8,128)(2,1)}) %all-gather.2.cloned.1.call-update) | async-done | bytes 4194320 | tf_op jit(solution)/shard_map/all_gather | solution.py:43
  298.8 4.1 pad_maximum_fusion
  302.9 4.4 %gather_fusion = bf16[32,2,128,128]{3,2,1,0:T(8,128)(2,1)} fusion(bf16[2,68,128,128]{3,2,1,0:T(8,128)(2,1)} %bitcast.291, s32[1024]{0:T(1024)S(1)} %pad_clamp_fusion), kind=kCustom, calls=%fused_computation | custom fusion | bytes 4194432 | tf_op jit(solution)/shard_map/jit(_take)/gather | solution.py:48
  307.3 1.9 copy_select_fusion
  309.1 24.5 %while.12 = (s32[]{:T(128)}, bf16[2,128,1024]{2,1,0:T(8,128)(2,1)}, s32[2]{0:T(128)S(1)}, s32[]{:T(128)}, bf16[2,2,16,128,128]{4,3,2,1,0:T(8,128)(2,1)S(1)}, /*i...) while((s32[]{:T(128)}, bf16[2,128,1024]{2,1,0:T(8,128)(2,1)}, ...), condition=%wide.region_9.10_spmd.clone.clone, body=%wide.region_0.9_spmd.clone.clone.sunk | while | flops 1098069504 | bytes 35500564 | solution.py:112
  310.7 0.8 compare_bitcast_fusion.5
  313.6 1.0 fusion.135
  318.2 1.7 fusion.141
  322.9 0.8 compare_bitcast_fusion.5
  325.9 1.0 fusion.135
  330.4 1.7 fusion.141
  332.9 0.7 constant_dynamic-update-slice_fusion.2
  333.6 64.7 %all_to_all.53 = bf16[8,32,1024]{2,1,0:T(8,128)(2,1)S(1)} all-to-all(bf16[8,32,1024]{2,1,0:T(8,128)(2,1)} %bitcast.307), channel_id=1, replica_groups=mesh['pb'=8,'kv'=8,'ha'=8] {'ha'}, dimensions={0} | all-to-all | bytes 1048576 | tf_op jit(solution)/shard_map/all_to_all | solution.py:114
  398.3 0.8 copy.87
  (67 shorter events, 18.3 us)
Async XLA Ops:
  6.5 20.4 %copy-start = (bf16[32,8192]{1,0:T(8,128)(2,1)S(1)}, bf16[32,8192]{1,0:T(8,128)(2,1)}, u32[]{:S(2)}) copy-start(bf16[32,8192]{1,0:T(8,128)(2,1)} %param.6) | copy-start | bytes 1572868
  6.5 292.3 %all-gather.2.cloned.1.call-start = ((), (), s32[]{:S(2)}) async-start(), calls=%async_computation.3 | async-start | bytes 4259840 | tf_op jit(solution)/shard_map/all_gather | solution.py:43
  79.4 7.3 %copy-start.1 = (s32[2,16]{1,0:T(2,128)S(1)}, s32[2,16]{1,0:T(2,128)}, u32[]{:S(2)}) copy-start(s32[2,16]{1,0:T(2,128)} %param.8) | copy-start | bytes 388
  82.0 24.2 %all-to-all-start.1 = ((bf16[8,2,16384]{2,1,0:T(2,128)(2,1)}), bf16[8,2,16384]{2,1,0:T(2,128)(2,1)S(1)}, u32[]{:S(2)}, u32[]{:S(2)}) async-start(bf16[8,2,16384]{2,1,0:T(2,128)(2,1)} %reshape.327), calls=%async_computation.1 | async-start | bytes 1048576 | tf_op jit(solution)/shard_map/all_to_all | solution.py:25
  86.8 32.6 %collective-permute-start = (bf16[2,256,128]{2,1,0:T(8,128)(2,1)S(1)}, bf16[2,256,128]{2,1,0:T(8,128)(2,1)S(1)}, u32[]{:S(2)}, u32[]{:S(2)}) collective-permute-start(bf16[2,256,128]{2,1,0:T(8,128)(2,1)S(1)} %bitcast.304), channel_id=1, source_target_pairs={{0,8},{8,16},{16,24},{24,32},{32,40},{40,48},{48,56},{56,64},{64,7... | collective-permute-start | bytes 393224 | tf_op jit(solution)/shard_map/ppermute | solution.py:20
  307.3 1.9 copy-start.2
Sparse Core Ops, SparseCore 0:
  27.0 271.7 all-gather.1
where the time goes:
time: 407 us; the launch traced here: 406 us
  waiting for transfers between devices  196 us (48%)
  blocking collectives  82 us (20%)
  other arithmetic  61 us (15%)
  local copies, waits for them, and re-layouts  36.4 us (9%)
  between operations  13.5 us (3%)
  matrix products  8.02 us (2%)
  starting transfers between devices  6.95 us (2%)
    all_gather x1, waiting for transfers between devices, body(): gathered = lax.all_gather(summary, ('pb', 'kv'), axis=1, tiled=True)  179 us
    all_to_all x1, blocking collectives, body(): return lax.all_to_all(result, 'ha', split_axis=0, concat_axis=1, tiled=True)  64.7 us
    unnamed x1, other arithmetic  45.2 us
    all_to_all x1, blocking collectives, body(): lax.all_to_all(keyvals, 'ha', split_axis=2, concat_axis=1, tiled=True)  17.3 us
    all_to_all x1, waiting for transfers between devices, body(): lax.all_to_all(queries[None], 'ha', split_axis=2, concat_axis=1, tiled=True)  17 us
    unnamed x14, local copies, waits for them, and re-layouts  10.1 us
    all_to_all x3, local copies, waits for them, and re-layouts, body(): lax.all_to_all(queries[None], 'ha', split_axis=2, concat_axis=1, tiled=True)  8.3 us
  transfers between devices with their start and end apart: 3, of which 2 were waited for; matrix products, arithmetic and copies ran while one was open for 17% of the time, Pallas kernels for 0%

commit v1 on v0

v1 whole, which is shorter than its diff:
```python
import math

import jax
import jax.numpy as jnp
from jax import lax
from jax.experimental import pallas as pl
from jax.experimental.pallas import tpu as pltpu
from jax.sharding import Mesh, PartitionSpec as P

HEAD_SIZE = 128
BLOCK_POSITIONS = 128
MAXB = 16
KEYS = MAXB * BLOCK_POSITIONS
HALF = BLOCK_POSITIONS // 2
STRIP = 32
GROUP = 8
ROWS = GROUP * STRIP
ODD = 3
NEGATIVE = -1e30
FACTOR = math.log2(math.e) / math.sqrt(HEAD_SIZE)
Z, X, YLO, YHI, CORE = "z", "x", "ylo", "yhi", "core"
RING = (YLO, YHI)


def attend(meta, lists, other_lists, q_ref, *refs):
    columns, odds = refs[:10], refs[10:12]
    out_ref, table, keys, values, scores, weights, sems = refs[12:]
    z, x, ylo, core = meta[0], meta[1], meta[2], meta[3]
    evens = table.shape[1] - ODD
    per_column = evens // 4
    copies = []

    def bring(source, target):
        copy = pltpu.make_async_copy(source, target, sems.at[len(copies)])
        copy.start()
        copies.append(copy)

    for rc in range(2):
        own, left, right, far_a, far_b = columns[rc * 5 : rc * 5 + 5]
        bring(own, table.at[rc, pl.ds(0, per_column)])
        bring(right, table.at[rc, pl.ds(per_column, per_column)])
        bring(far_a, table.at[rc, pl.ds(2 * per_column, per_column // 2)])
        bring(far_b, table.at[rc, pl.ds(2 * per_column + per_column // 2, per_column // 2)])
        bring(left, table.at[rc, pl.ds(3 * per_column, per_column)])
        bring(odds[rc], table.at[rc, pl.ds(evens, ODD)])
    for copy in copies:
        copy.wait()

    pair = z * 4 + x
    cell = lax.broadcasted_iota(jnp.int32, (ROWS, BLOCK_POSITIONS), 1)
    row = lax.broadcasted_iota(jnp.int32, (ROWS, BLOCK_POSITIONS), 0)
    cell_core = jnp.bitwise_xor(cell // HALF, core)
    key_position = (cell % HALF) // STRIP * HALF + cell_core * STRIP + cell % STRIP
    row_position = core * STRIP + row % STRIP

    def one_block(b, carry):
        mine = (b // 2) == ylo
        inside = b % 2
        count = jnp.where(mine, lists[inside, MAXB], other_lists[inside, MAXB])
        for e in range(MAXB):
            j = jnp.where(mine, lists[inside, e], other_lists[inside, e])
            relative = jnp.bitwise_and(j // 4 - x, 3)
            even_row = relative * per_column + (j // 16) * 2 + (j // 2) % 2
            odd_row = evens + jnp.clip((j - 4 * pair + 1) // 2, 0, ODD - 1)
            t = jnp.where(j % 2 == 0, even_row, odd_row)
            for rc in range(2):
                span = pl.ds(e * BLOCK_POSITIONS + rc * HALF, HALF)
                keys[span, :] = table[rc, t, 0]
                values[span, :] = table[rc, t, 1]
        for strip in range(2):
            source = 2 * b + strip
            q = jnp.concatenate(
                [q_ref[source, :, h * HEAD_SIZE : (h + 1) * HEAD_SIZE] for h in range(GROUP)], axis=0
            )
            peak = jnp.full((ROWS, BLOCK_POSITIONS), NEGATIVE, jnp.float32)
            for g in range(MAXB // 2):
                s = lax.dot_general(
                    q,
                    keys[g * 256 : (g + 1) * 256, :],
                    (((1,), (1,)), ((), ())),
                    preferred_element_type=jnp.float32,
                )
                for half in range(2):
                    e = 2 * g + half
                    part = s[:, half * 128 : (half + 1) * 128]
                    if e == 0:
                        part = jnp.where(key_position <= row_position + strip * HALF, part, NEGATIVE)
                    else:
                        part = jnp.where(e < count, part, NEGATIVE)
                    scores[strip, :, e * 128 : (e + 1) * 128] = part
                    peak = jnp.maximum(peak, part)
            top = jnp.max(peak, axis=1, keepdims=True) * FACTOR
            total = jnp.zeros((ROWS, BLOCK_POSITIONS), jnp.float32)
            for e in range(MAXB):
                span = slice(e * 128, (e + 1) * 128)
                w = jnp.exp2(scores[strip, :, span] * FACTOR - top)
                total = total + w
                weights[strip, :, span] = w.astype(jnp.bfloat16)
            numerator = jnp.dot(weights[strip], values[...], preferred_element_type=jnp.float32)
            result = numerator / jnp.sum(total, axis=1, keepdims=True)
            result = result.astype(jnp.bfloat16)
            for h in range(GROUP):
                out_ref[source, :, h * HEAD_SIZE : (h + 1) * HEAD_SIZE] = result[h * STRIP : (h + 1) * STRIP]
        return carry

    lax.fori_loop(0, 4, one_block, 0)


def attention(meta, lists, other_lists, q, columns, odds, interpret=False):
    evens = 4 * columns[0].shape[0]
    smem = pl.BlockSpec(memory_space=pltpu.SMEM)
    vmem = pl.BlockSpec(memory_space=pltpu.VMEM)
    hbm = pl.BlockSpec(memory_space=pl.ANY)
    return pl.pallas_call(
        attend,
        out_shape=jax.ShapeDtypeStruct(q.shape, q.dtype),
        in_specs=[smem, smem, smem, vmem] + [hbm] * 12,
        out_specs=vmem,
        scratch_shapes=[
            pltpu.VMEM((2, evens + ODD, 2, HALF, HEAD_SIZE), jnp.bfloat16),
            pltpu.VMEM((KEYS, HEAD_SIZE), jnp.bfloat16),
            pltpu.VMEM((KEYS, HEAD_SIZE), jnp.bfloat16),
            pltpu.VMEM((2, ROWS, KEYS), jnp.float32),
            pltpu.VMEM((2, ROWS, KEYS), jnp.bfloat16),
            pltpu.SemaphoreType.DMA((12,)),
        ],
        compiler_params=pltpu.CompilerParams(vmem_limit_bytes=40 * 2**20),
        interpret=interpret,
    )(meta, lists, other_lists, q, *columns, *odds)


def shift(array, axis, by):
    size = lax.axis_size(axis)
    return lax.ppermute(array, axis, [(i, (i + by) % size) for i in range(size)])


def swap(array, axis):
    return lax.ppermute(array, axis, [(0, 1), (1, 0)])


def body(queries, keyvals, block_index, block_count):
    lists = jnp.concatenate([block_index, block_count[:, None]], axis=1)
    other_lists = swap(lists, YLO)
    meta = jnp.stack([lax.axis_index(a) for a in (Z, X, YLO, CORE)]).astype(jnp.int32)
    heads = lax.axis_size(RING)

    sent = keyvals.reshape(2, STRIP, heads, HEAD_SIZE).transpose(2, 0, 1, 3)
    local = lax.all_to_all(sent, RING, split_axis=0, concat_axis=0, tiled=True)
    local = local.reshape(4, 2, 2, STRIP, HEAD_SIZE).transpose(0, 2, 1, 3, 4)
    local = local.reshape(4, 2, HALF, HEAD_SIZE)

    summary = jnp.stack([local[0], local[2]])
    gathered = lax.all_gather(summary, Z, axis=0, tiled=True)
    sent_q = queries.reshape(STRIP, heads, GROUP * HEAD_SIZE).transpose(1, 0, 2)
    q = lax.all_to_all(sent_q, RING, split_axis=0, concat_axis=0, tiled=True)

    middle = gathered.shape[0] // 2
    left = shift(gathered, X, 1)
    right = shift(gathered, X, -1)
    far_a = shift(left[:middle], X, 1)
    far_b = shift(right[middle:], X, -1)
    pairs = lax.axis_size((Z, X))
    before = lax.ppermute(local[3], (Z, X), [(i, i + 1) for i in range(pairs - 1)])
    odd = jnp.stack([before, local[1], local[3]])

    columns = [gathered, left, right, far_a, far_b]
    columns += [swap(column, CORE) for column in columns]
    odds = [odd, swap(odd, CORE)]
    result = attention(meta, lists, other_lists, q, columns, odds)
    result = lax.all_to_all(result, RING, split_axis=0, concat_axis=0, tiled=True)
    return result.transpose(1, 0, 2).reshape(STRIP, heads * GROUP * HEAD_SIZE)


def solution(mesh):
    pb, kv, ha = mesh.devices.shape
    fine = Mesh(mesh.devices.reshape(pb, kv // 2, 2, ha // 2, 2), (Z, X, YLO, YHI, CORE))
    rows = (Z, X, YLO, YHI, CORE)
    shard = (Z, X, YLO)
    return jax.shard_map(
        body,
        mesh=fine,
        in_specs=(P(rows, None), P(None, rows, None), P(shard, None), P(shard)),
        out_specs=P(rows, None),
        check_vma=False,
    )
```

time: 407 us -> 129 us (0.32)
  the two profiles are of different devices: /device:TPU:1 before, /device:TPU:8 now
where the time goes in v1:
time: 129 us
  blocking collectives  70.7 us (55%)
  starting transfers between devices  36 us (28%)
  Pallas kernels  11.7 us (9%)
  waiting for transfers between devices  5.61 us (4%)
  local copies, waits for them, and re-layouts  4.31 us (3%)
    all_gather x1, blocking collectives, body(): gathered = lax.all_gather(summary, Z, axis=0, tiled=True)  31.1 us
    all_to_all x1, blocking collectives, body(): lax.all_to_all(result, RING, split_axis=0, concat_axis=0, tiled=True)  23.8 us
    all_to_all x1, blocking collectives, body(): local = lax.all_to_all(sent, RING, split_axis=0, concat_axis=0, tiled=True)  15.8 us
    ppermute x4, starting transfers between devices, shift(): lax.ppermute(array, axis, [(i, (i + by) % size) for i in range(size)])  15.2 us
    ppermute x7, starting transfers between devices, swap(): return lax.ppermute(array, axis, [(0, 1), (1, 0)])  14.4 us
    pallas_call x1, Pallas kernels, attention(): pl.pallas_call(attend, out_shape=jax.ShapeDtypeStruct(q.shape, q.dtype),...  11.7 us
    all_to_all x1, starting transfers between devices, body(): q = lax.all_to_all(sent_q, RING, split_axis=0, concat_axis=0, tiled=True)  3.72 us
    ppermute x1, starting transfers between devices, body(): lax.ppermute(local[3], (Z, X), [(i, i + 1) for i in range(pairs - 1)])  2.65 us
  transfers between devices with their start and end apart: 13, of which 3 were waited for; matrix products, arithmetic and copies ran while one was open for 1% of the time, Pallas kernels for 0%

profile of v1, /device:TPU:8, one launch (start us, length us, event | category | flops | bytes accessed | tf_op | source)
XLA Modules:
  0.0 128.7 jit_solution(3113294355736568853)
XLA Ops:
  0.0 0.9 copy.41
  1.0 15.8 %all_to_all.15 = bf16[8,2,32,128]{3,2,1,0:T(8,128)(2,1)S(1)} all-to-all(bf16[8,2,32,128]{3,2,1,0:T(8,128)(2,1)S(1)} %copy.32), channel_id=1, replica_groups=mesh['z'=8,'x'=4,'ylo'=2,'yhi'=4,'core'=2] {'ylo','yhi'}, dimensions={0} | all-to-all | bytes 262144 | tf_op jit(solution)/shard_map/all_to_all | solution.py:148
  16.8 31.1 %all_gather.3.refs_0_ = bf16[16,2,64,128]{3,2,1,0:T(8,128)(2,1)S(1)} all-gather(bf16[2,2,64,128]{3,2,1,0:T(8,128)(2,1)S(1)} %pad_maximum_fusion.1), channel_id=1, replica_groups=mesh['z'=8,'x'=4,'ylo'=2,'yhi'=4,'core'=2] {'z'}, dimensions={0}, use_global_device_ids=true | all-gather | bytes 589824 | tf_op jit(solution)/shard_map/all_gather | solution.py:153
  47.9 4.7 %collective-permute-start.2 = (bf16[16,2,64,128]{3,2,1,0:T(8,128)(2,1)S(1)}, bf16[16,2,64,128]{3,2,1,0:T(8,128)(2,1)S(1)}, u32[]{:S(2)}, u32[]{:S(2)}) collective-permute-start(bf16[16,2,64,128]{3,2,1,0:T(8,128)(2,1)S(1)} %all_gather.3.refs_0_), channel_id=1, source_target_pairs={{0,48},{16,0},{32,16},{48,32},{1,49},{17,1},{33,17},{49,33},{2,50}... | collective-permute-start | bytes 1572872 | tf_op jit(solution)/shard_map/ppermute | solution.py:134
  52.6 1.9 %collective-permute-start.1 = (bf16[16,2,64,128]{3,2,1,0:T(8,128)(2,1)S(1)}, bf16[16,2,64,128]{3,2,1,0:T(8,128)(2,1)S(1)}, u32[]{:S(2)}, u32[]{:S(2)}) collective-permute-start(bf16[16,2,64,128]{3,2,1,0:T(8,128)(2,1)S(1)} %all_gather.3.refs_0_), channel_id=1, source_target_pairs={{0,16},{16,32},{32,48},{48,0},{1,17},{17,33},{33,49},{49,1},{2,18}... | collective-permute-start | bytes 1572872 | tf_op jit(solution)/shard_map/ppermute | solution.py:134
  54.5 0.8 copy.43
  55.3 3.7 %all-to-all-start = ((bf16[8,32,1024]{2,1,0:T(8,128)(2,1)}), bf16[8,32,1024]{2,1,0:T(8,128)(2,1)S(1)}, u32[]{:S(2)}, u32[]{:S(2)}) async-start(bf16[8,32,1024]{2,1,0:T(8,128)(2,1)} %bitcast.30), calls=%async_computation | async-start | bytes 1048576 | tf_op jit(solution)/shard_map/all_to_all | solution.py:155
  59.1 2.7 %collective-permute-start.10 = (bf16[2,64,128]{2,1,0:T(8,128)(2,1)S(1)}, bf16[2,64,128]{2,1,0:T(8,128)(2,1)S(1)}, u32[]{:S(2)}, u32[]{:S(2)}) collective-permute-start(bf16[2,64,128]{2,1,0:T(8,128)(2,1)S(1)} %bitcast.37), channel_id=1, source_target_pairs={{0,16},{16,32},{32,48},{48,64},{64,80},{80,96},{96,112},{112,128},... | collective-permute-start | bytes 98312 | tf_op jit(solution)/shard_map/ppermute | solution.py:163
  61.8 1.5 %collective-permute-done.10 = bf16[2,64,128]{2,1,0:T(8,128)(2,1)S(1)} collective-permute-done((bf16[2,64,128]{2,1,0:T(8,128)(2,1)S(1)}, bf16[2,64,128]{2,1,0:T(8,128)(2,1)S(1)}, u32[]{:S(2)}, u32[]{:S(2)}) %collective-permute-start.10) | collective-permute-done | bytes 32800 | tf_op jit(solution)/shard_map/ppermute | solution.py:163
  63.3 1.9 %collective-permute-start.11 = (bf16[3,2,64,128]{3,2,1,0:T(8,128)(2,1)S(1)}, bf16[3,2,64,128]{3,2,1,0:T(8,128)(2,1)S(1)}, u32[]{:S(2)}, u32[]{:S(2)}) collective-permute-start(bf16[3,2,64,128]{3,2,1,0:T(8,128)(2,1)S(1)} %pad_maximum_fusion.refs_10_), channel_id=1, source_target_pairs={{0,1},{1,0},{2,3},{3,2},{4,5},{5,4},{6,7},{7,6},{8,9},{9,8},{10,11... | collective-permute-start | bytes 294920 | tf_op jit(solution)/shard_map/ppermute | solution.py:138
  65.3 2.0 %collective-permute-start = (s32[2,17]{1,0:T(2,128)S(1)}, s32[2,17]{1,0:T(2,128)S(1)}, u32[]{:S(2)}, u32[]{:S(2)}) collective-permute-start(s32[2,17]{1,0:T(2,128)S(1)} %pad_add_fusion.lists), channel_id=1, source_target_pairs={{0,8},{8,0},{1,9},{9,1},{2,10},{10,2},{3,11},{11,3},{4,12},{12,4},... | collective-permute-start | bytes 416 | tf_op jit(solution)/shard_map/ppermute | solution.py:138
  67.3 2.3 %collective-permute-start.5 = (bf16[16,2,64,128]{3,2,1,0:T(8,128)(2,1)S(1)}, bf16[16,2,64,128]{3,2,1,0:T(8,128)(2,1)S(1)}, u32[]{:S(2)}, u32[]{:S(2)}) collective-permute-start(bf16[16,2,64,128]{3,2,1,0:T(8,128)(2,1)S(1)} %all_gather.3.refs_0_), channel_id=1, source_target_pairs={{0,1},{1,0},{2,3},{3,2},{4,5},{5,4},{6,7},{7,6},{8,9},{9,8},{10,11... | collective-permute-start | bytes 1572872 | tf_op jit(solution)/shard_map/ppermute | solution.py:138
  69.7 6.7 %collective-permute-start.4 = (bf16[8,2,64,128]{3,2,1,0:T(8,128)(2,1)S(1)}, bf16[8,2,64,128]{3,2,1,0:T(8,128)(2,1)S(1)}, u32[]{:S(2)}, u32[]{:S(2)}) collective-permute-start(bf16[8,2,64,128]{3,2,1,0:T(8,128)(2,1)S(1)} %slice.44), channel_id=1, source_target_pairs={{0,48},{16,0},{32,16},{48,32},{1,49},{17,1},{33,17},{49,33},{2,50}... | collective-permute-start | bytes 786440 | tf_op jit(solution)/shard_map/ppermute | solution.py:134
  76.5 1.9 %collective-permute-start.3 = (bf16[8,2,64,128]{3,2,1,0:T(8,128)(2,1)S(1)}, bf16[8,2,64,128]{3,2,1,0:T(8,128)(2,1)}, u32[]{:S(2)}, u32[]{:S(2)}) collective-permute-start(bf16[8,2,64,128]{3,2,1,0:T(8,128)(2,1)S(1)} %slice.43), channel_id=1, source_target_pairs={{0,16},{16,32},{32,48},{48,0},{1,17},{17,33},{33,49},{49,1},{2,18}... | collective-permute-start | bytes 786440 | tf_op jit(solution)/shard_map/ppermute | solution.py:134
  78.4 1.9 %collective-permute-start.7 = (bf16[16,2,64,128]{3,2,1,0:T(8,128)(2,1)S(1)}, bf16[16,2,64,128]{3,2,1,0:T(8,128)(2,1)S(1)}, u32[]{:S(2)}, u32[]{:S(2)}) collective-permute-start(bf16[16,2,64,128]{3,2,1,0:T(8,128)(2,1)S(1)} %collective-permute-done.2.refs_2_), channel_id=1, source_target_pairs={{0,1},{1,0},{2,3},{3,2},{4,5},{5,4},{6,7},{7,6},{8,9},{9,8},{10,11... | collective-permute-start | bytes 1572872 | tf_op jit(solution)/shard_map/ppermute | solution.py:138
  81.0 2.4 %collective-permute-start.6 = (bf16[16,2,64,128]{3,2,1,0:T(8,128)(2,1)S(1)}, bf16[16,2,64,128]{3,2,1,0:T(8,128)(2,1)}, u32[]{:S(2)}, u32[]{:S(2)}) collective-permute-start(bf16[16,2,64,128]{3,2,1,0:T(8,128)(2,1)S(1)} %collective-permute-done.1.refs_1_), channel_id=1, source_target_pairs={{0,1},{1,0},{2,3},{3,2},{4,5},{5,4},{6,7},{7,6},{8,9},{9,8},{10,11... | collective-permute-start | bytes 1572872 | tf_op jit(solution)/shard_map/ppermute | solution.py:138
  83.4 1.9 %collective-permute-start.9 = (bf16[8,2,64,128]{3,2,1,0:T(8,128)(2,1)S(1)}, bf16[8,2,64,128]{3,2,1,0:T(8,128)(2,1)}, u32[]{:S(2)}, u32[]{:S(2)}) collective-permute-start(bf16[8,2,64,128]{3,2,1,0:T(8,128)(2,1)S(1)} %collective-permute-done.4.refs_4_), channel_id=1, source_target_pairs={{0,1},{1,0},{2,3},{3,2},{4,5},{5,4},{6,7},{7,6},{8,9},{9,8},{10,11... | collective-permute-start | bytes 786440 | tf_op jit(solution)/shard_map/ppermute | solution.py:138
  85.3 2.4 %collective-permute-done.3.refs_3_ = bf16[8,2,64,128]{3,2,1,0:T(8,128)(2,1)} collective-permute-done((bf16[8,2,64,128]{3,2,1,0:T(8,128)(2,1)S(1)}, bf16[8,2,64,128]{3,2,1,0:T(8,128)(2,1)}, u32[]{:S(2)}, u32[]{:S(2)}) %collective-permute-start.3) | collective-permute-done | bytes 262176 | tf_op jit(solution)/shard_map/ppermute | solution.py:134
  87.7 1.9 %collective-permute-start.8 = (bf16[8,2,64,128]{3,2,1,0:T(8,128)(2,1)}, bf16[8,2,64,128]{3,2,1,0:T(8,128)(2,1)}, u32[]{:S(2)}, u32[]{:S(2)}) collective-permute-start(bf16[8,2,64,128]{3,2,1,0:T(8,128)(2,1)} %collective-permute-done.3.refs_3_), channel_id=1, source_target_pairs={{0,1},{1,0},{2,3},{3,2},{4,5},{5,4},{6,7},{7,6},{8,9},{9,8},{10,11... | collective-permute-start | bytes 786440 | tf_op jit(solution)/shard_map/ppermute | solution.py:138
  89.7 1.7 %collective-permute-done.8.refs_8_ = bf16[8,2,64,128]{3,2,1,0:T(8,128)(2,1)} collective-permute-done((bf16[8,2,64,128]{3,2,1,0:T(8,128)(2,1)}, bf16[8,2,64,128]{3,2,1,0:T(8,128)(2,1)}, u32[]{:S(2)}, u32[]{:S(2)}) %collective-permute-start.8) | collective-permute-done | bytes 262176 | tf_op jit(solution)/shard_map/ppermute | solution.py:138
  91.5 0.9 copy-done.1
  92.4 11.7 %shard_map.46 = bf16[8,32,1024]{2,1,0:T(8,128)(2,1)S(1)} custom-call(s32[4]{0:T(128)S(1)} %pad_add_fusion.1.meta, s32[2,17]{1,0:T(2,128)S(1)} %pad_add_fusion.lists, s32[2,17]{1,0:T(2,128)S(1)} %collective-permute-done.other_lists, bf16[8,32,1024]{2,1,0:T(8,128)(2,1)S(1)} %all-to-all-done.q_ref, bf16[16,2,64,128]{3,2,1,0:T(8,128)(2,1)S(1)} %all_gather.3.refs_0_, ...), custom_call_target="tpu_custom_call" | custom-call | tf_op jit(solution)/shard_map/pallas_call | solution.py:114
  104.1 23.8 %all_to_all.16 = bf16[8,32,1024]{2,1,0:T(8,128)(2,1)S(1)} all-to-all(bf16[8,32,1024]{2,1,0:T(8,128)(2,1)S(1)} %shard_map.46), channel_id=1, replica_groups=mesh['z'=8,'x'=4,'ylo'=2,'yhi'=4,'core'=2] {'ylo','yhi'}, dimensions={0} | all-to-all | bytes 1048576 | tf_op jit(solution)/shard_map/all_to_all | solution.py:170
  127.9 0.8 copy.40
  (33 shorter events, 1.0 us)
Async XLA Ops:
  16.8 37.7 %copy-start.2 = (bf16[32,8192]{1,0:T(8,128)(2,1)S(1)}, bf16[32,8192]{1,0:T(8,128)(2,1)}, u32[]{:S(2)}) copy-start(bf16[32,8192]{1,0:T(8,128)(2,1)} %param.4) | copy-start | bytes 1572868
  47.9 21.8 %collective-permute-start.2 = (bf16[16,2,64,128]{3,2,1,0:T(8,128)(2,1)S(1)}, bf16[16,2,64,128]{3,2,1,0:T(8,128)(2,1)S(1)}, u32[]{:S(2)}, u32[]{:S(2)}) collective-permute-start(bf16[16,2,64,128]{3,2,1,0:T(8,128)(2,1)S(1)} %all_gather.3.refs_0_), channel_id=1, source_target_pairs={{0,48},{16,0},{32,16},{48,32},{1,49},{17,1},{33,17},{49,33},{2,50}... | collective-permute-start | bytes 1572872 | tf_op jit(solution)/shard_map/ppermute | solution.py:134
  52.6 23.9 %collective-permute-start.1 = (bf16[16,2,64,128]{3,2,1,0:T(8,128)(2,1)S(1)}, bf16[16,2,64,128]{3,2,1,0:T(8,128)(2,1)S(1)}, u32[]{:S(2)}, u32[]{:S(2)}) collective-permute-start(bf16[16,2,64,128]{3,2,1,0:T(8,128)(2,1)S(1)} %all_gather.3.refs_0_), channel_id=1, source_target_pairs={{0,16},{16,32},{32,48},{48,0},{1,17},{17,33},{33,49},{49,1},{2,18}... | collective-permute-start | bytes 1572872 | tf_op jit(solution)/shard_map/ppermute | solution.py:134
  55.3 34.4 %all-to-all-start = ((bf16[8,32,1024]{2,1,0:T(8,128)(2,1)}), bf16[8,32,1024]{2,1,0:T(8,128)(2,1)S(1)}, u32[]{:S(2)}, u32[]{:S(2)}) async-start(bf16[8,32,1024]{2,1,0:T(8,128)(2,1)} %bitcast.30), calls=%async_computation | async-start | bytes 1048576 | tf_op jit(solution)/shard_map/all_to_all | solution.py:155
  59.1 2.7 %copy-start.4 = (s32[2]{0:T(128)S(1)}, s32[2]{0:T(128)}, u32[]{:S(2)}) copy-start(s32[2]{0:T(128)} %param.7) | copy-start | bytes 28
  59.1 4.2 %collective-permute-start.10 = (bf16[2,64,128]{2,1,0:T(8,128)(2,1)S(1)}, bf16[2,64,128]{2,1,0:T(8,128)(2,1)S(1)}, u32[]{:S(2)}, u32[]{:S(2)}) collective-permute-start(bf16[2,64,128]{2,1,0:T(8,128)(2,1)S(1)} %bitcast.37), channel_id=1, source_target_pairs={{0,16},{16,32},{32,48},{48,64},{64,80},{80,96},{96,112},{112,128},... | collective-permute-start | bytes 98312 | tf_op jit(solution)/shard_map/ppermute | solution.py:163
  63.3 1.9 %copy-start.3 = (s32[2,16]{1,0:T(2,128)S(1)}, s32[2,16]{1,0:T(2,128)}, u32[]{:S(2)}) copy-start(s32[2,16]{1,0:T(2,128)} %param.6) | copy-start | bytes 388
  63.3 17.0 %collective-permute-start.11 = (bf16[3,2,64,128]{3,2,1,0:T(8,128)(2,1)S(1)}, bf16[3,2,64,128]{3,2,1,0:T(8,128)(2,1)S(1)}, u32[]{:S(2)}, u32[]{:S(2)}) collective-permute-start(bf16[3,2,64,128]{3,2,1,0:T(8,128)(2,1)S(1)} %pad_maximum_fusion.refs_10_), channel_id=1, source_target_pairs={{0,1},{1,0},{2,3},{3,2},{4,5},{5,4},{6,7},{7,6},{8,9},{9,8},{10,11... | collective-permute-start | bytes 294920 | tf_op jit(solution)/shard_map/ppermute | solution.py:138
  65.3 13.0 %collective-permute-start = (s32[2,17]{1,0:T(2,128)S(1)}, s32[2,17]{1,0:T(2,128)S(1)}, u32[]{:S(2)}, u32[]{:S(2)}) collective-permute-start(s32[2,17]{1,0:T(2,128)S(1)} %pad_add_fusion.lists), channel_id=1, source_target_pairs={{0,8},{8,0},{1,9},{9,1},{2,10},{10,2},{3,11},{11,3},{4,12},{12,4},... | collective-permute-start | bytes 416 | tf_op jit(solution)/shard_map/ppermute | solution.py:138
  67.3 22.4 %collective-permute-start.5 = (bf16[16,2,64,128]{3,2,1,0:T(8,128)(2,1)S(1)}, bf16[16,2,64,128]{3,2,1,0:T(8,128)(2,1)S(1)}, u32[]{:S(2)}, u32[]{:S(2)}) collective-permute-start(bf16[16,2,64,128]{3,2,1,0:T(8,128)(2,1)S(1)} %all_gather.3.refs_0_), channel_id=1, source_target_pairs={{0,1},{1,0},{2,3},{3,2},{4,5},{5,4},{6,7},{7,6},{8,9},{9,8},{10,11... | collective-permute-start | bytes 1572872 | tf_op jit(solution)/shard_map/ppermute | solution.py:138
  69.7 13.7 %collective-permute-start.4 = (bf16[8,2,64,128]{3,2,1,0:T(8,128)(2,1)S(1)}, bf16[8,2,64,128]{3,2,1,0:T(8,128)(2,1)S(1)}, u32[]{:S(2)}, u32[]{:S(2)}) collective-permute-start(bf16[8,2,64,128]{3,2,1,0:T(8,128)(2,1)S(1)} %slice.44), channel_id=1, source_target_pairs={{0,48},{16,0},{32,16},{48,32},{1,49},{17,1},{33,17},{49,33},{2,50}... | collective-permute-start | bytes 786440 | tf_op jit(solution)/shard_map/ppermute | solution.py:134
  76.5 11.2 %collective-permute-start.3 = (bf16[8,2,64,128]{3,2,1,0:T(8,128)(2,1)S(1)}, bf16[8,2,64,128]{3,2,1,0:T(8,128)(2,1)}, u32[]{:S(2)}, u32[]{:S(2)}) collective-permute-start(bf16[8,2,64,128]{3,2,1,0:T(8,128)(2,1)S(1)} %slice.43), channel_id=1, source_target_pairs={{0,16},{16,32},{32,48},{48,0},{1,17},{17,33},{33,49},{49,1},{2,18}... | collective-permute-start | bytes 786440 | tf_op jit(solution)/shard_map/ppermute | solution.py:134
  78.4 11.3 %collective-permute-start.7 = (bf16[16,2,64,128]{3,2,1,0:T(8,128)(2,1)S(1)}, bf16[16,2,64,128]{3,2,1,0:T(8,128)(2,1)S(1)}, u32[]{:S(2)}, u32[]{:S(2)}) collective-permute-start(bf16[16,2,64,128]{3,2,1,0:T(8,128)(2,1)S(1)} %collective-permute-done.2.refs_2_), channel_id=1, source_target_pairs={{0,1},{1,0},{2,3},{3,2},{4,5},{5,4},{6,7},{7,6},{8,9},{9,8},{10,11... | collective-permute-start | bytes 1572872 | tf_op jit(solution)/shard_map/ppermute | solution.py:138
  80.3 0.6 copy-start
  81.0 10.5 %collective-permute-start.6 = (bf16[16,2,64,128]{3,2,1,0:T(8,128)(2,1)S(1)}, bf16[16,2,64,128]{3,2,1,0:T(8,128)(2,1)}, u32[]{:S(2)}, u32[]{:S(2)}) collective-permute-start(bf16[16,2,64,128]{3,2,1,0:T(8,128)(2,1)S(1)} %collective-permute-done.1.refs_1_), channel_id=1, source_target_pairs={{0,1},{1,0},{2,3},{3,2},{4,5},{5,4},{6,7},{7,6},{8,9},{9,8},{10,11... | collective-permute-start | bytes 1572872 | tf_op jit(solution)/shard_map/ppermute | solution.py:138
  83.4 6.3 %collective-permute-start.9 = (bf16[8,2,64,128]{3,2,1,0:T(8,128)(2,1)S(1)}, bf16[8,2,64,128]{3,2,1,0:T(8,128)(2,1)}, u32[]{:S(2)}, u32[]{:S(2)}) collective-permute-start(bf16[8,2,64,128]{3,2,1,0:T(8,128)(2,1)S(1)} %collective-permute-done.4.refs_4_), channel_id=1, source_target_pairs={{0,1},{1,0},{2,3},{3,2},{4,5},{5,4},{6,7},{7,6},{8,9},{9,8},{10,11... | collective-permute-start | bytes 786440 | tf_op jit(solution)/shard_map/ppermute | solution.py:138
  87.7 3.8 %collective-permute-start.8 = (bf16[8,2,64,128]{3,2,1,0:T(8,128)(2,1)}, bf16[8,2,64,128]{3,2,1,0:T(8,128)(2,1)}, u32[]{:S(2)}, u32[]{:S(2)}) collective-permute-start(bf16[8,2,64,128]{3,2,1,0:T(8,128)(2,1)} %collective-permute-done.3.refs_3_), channel_id=1, source_target_pairs={{0,1},{1,0},{2,3},{3,2},{4,5},{5,4},{6,7},{7,6},{8,9},{9,8},{10,11... | collective-permute-start | bytes 786440 | tf_op jit(solution)/shard_map/ppermute | solution.py:138
  91.5 0.9 copy-start.1

commit v2 on v1

v2 whole, which is shorter than its diff:
```python
import math

import jax
import jax.numpy as jnp
from jax import lax
from jax.experimental import pallas as pl
from jax.experimental.pallas import tpu as pltpu
from jax.sharding import Mesh, PartitionSpec as P

HEAD_SIZE = 128
BLOCK_POSITIONS = 128
MAXB = 16
KEYS = MAXB * BLOCK_POSITIONS
HALF = BLOCK_POSITIONS // 2
STRIP = 32
GROUP = 8
HALF_ROWS = GROUP * STRIP
ODD = 3
NEGATIVE = -1e30
FACTOR = math.log2(math.e) / math.sqrt(HEAD_SIZE)
Z, X, YLO, YHI, CORE = "z", "x", "ylo", "yhi", "core"
RING = (YLO, YHI)


def attend(meta, lists, other_lists, q_ref, *refs):
    columns, odds = refs[:8], refs[8:10]
    out_ref, table, qs, keys, values, scores, weights, sems = refs[10], refs[11], *(
        refs[12 + 2 * i : 14 + 2 * i] for i in range(4)
    ), refs[20], refs[21]
    z, x, ylo, core, me = (meta[i] for i in range(5))
    evens = table.shape[1] - ODD
    per_column = evens // 4
    copies = []

    def bring(source, target):
        copy = pltpu.make_async_copy(source, target, sems.at[len(copies)])
        copy.start()
        copies.append(copy)

    for rc in range(2):
        side = jnp.bitwise_xor(core, rc)
        for source, relative in zip(columns[rc * 4 : rc * 4 + 4], (0, 3 - 2 * side, 1 + 2 * side, 2)):
            bring(source, table.at[rc, pl.ds(relative * per_column, per_column)])
        bring(odds[rc], table.at[rc, pl.ds(evens, ODD)])
    for copy in copies:
        copy.wait()

    pair = z * 4 + x
    cell = lax.broadcasted_iota(jnp.int32, (HALF_ROWS, BLOCK_POSITIONS), 1)
    row = lax.broadcasted_iota(jnp.int32, (HALF_ROWS, BLOCK_POSITIONS), 0)
    cell_core = jnp.bitwise_xor(cell // HALF, core)
    key_position = (cell % HALF) // STRIP * HALF + cell_core * STRIP + cell % STRIP
    row_position = core * STRIP + row % STRIP

    def entry(b, e):
        return jnp.where(b // 2 == ylo, lists[b % 2, e], other_lists[b % 2, e])

    def prepare(b, slot):
        for e in range(MAXB):
            j = entry(b, e)
            relative = jnp.bitwise_and(j // 4 - x, 3)
            odd_row = evens + jnp.clip((j - 4 * pair + 1) // 2, 0, ODD - 1)
            for rc in range(2):
                upward = jnp.bitwise_and(z - j // 16, 7)
                distance = jnp.where(core == rc, upward, jnp.bitwise_and(8 - upward, 7))
                place = jnp.bitwise_and(distance, 1) * 4 + jnp.bitwise_and(distance, 2) + distance // 4
                even_row = relative * per_column + place * 2 + (j // 2) % 2
                t = jnp.where(j % 2 == 0, even_row, odd_row)
                span = pl.ds(e * BLOCK_POSITIONS + rc * HALF, HALF)
                keys[slot][span, :] = table[rc, t, 0]
                values[slot][span, :] = table[rc, t, 1]
        for strip in range(2):
            for h in range(GROUP):
                qs[slot][pl.ds((strip * GROUP + h) * STRIP, STRIP), :] = q_ref[
                    2 * b + strip, :, h * HEAD_SIZE : (h + 1) * HEAD_SIZE
                ]

    def score(slot, g, count):
        s = lax.dot_general(
            qs[slot][...],
            keys[slot][g * 256 : (g + 1) * 256, :],
            (((1,), (1,)), ((), ())),
            preferred_element_type=jnp.float32,
        )
        for e in (2 * g, 2 * g + 1):
            for strip in range(2):
                lines = slice(strip * HALF_ROWS, (strip + 1) * HALF_ROWS)
                part = s[lines, (e % 2) * 128 : (e % 2 + 1) * 128]
                keep = key_position <= row_position + strip * HALF if e == 0 else e < count
                scores[slot][lines, e * 128 : (e + 1) * 128] = jnp.where(keep, part, NEGATIVE)

    def finish(b, slot, later):
        for strip in range(2):
            lines = slice(strip * HALF_ROWS, (strip + 1) * HALF_ROWS)
            peak = scores[slot][lines, 0:128]
            for e in range(1, MAXB):
                peak = jnp.maximum(peak, scores[slot][lines, e * 128 : (e + 1) * 128])
            top = jnp.max(peak, axis=1, keepdims=True) * FACTOR
            total = jnp.zeros((HALF_ROWS, BLOCK_POSITIONS), jnp.float32)
            for e in range(MAXB):
                if e % 4 == 0 and later is not None:
                    score(1 - slot, strip * 4 + e // 4, later)
                span = slice(e * 128, (e + 1) * 128)
                w = jnp.exp2(scores[slot][lines, span] * FACTOR - top)
                total = total + w
                weights[lines, span] = w.astype(jnp.bfloat16)
            numerator = jnp.dot(weights[lines, :], values[slot][...], preferred_element_type=jnp.float32)
            result = (numerator / jnp.sum(total, axis=1, keepdims=True)).astype(jnp.bfloat16)
            place = jnp.bitwise_xor(2 * b + strip, me)
            for h in range(GROUP):
                out_ref[place, :, h * HEAD_SIZE : (h + 1) * HEAD_SIZE] = result[h * STRIP : (h + 1) * STRIP]

    prepare(0, 0)
    for g in range(MAXB // 2):
        score(0, g, entry(0, MAXB))

    def step(i, carry):
        b = 2 * i
        prepare(b + 1, 1)
        finish(b, 0, entry(b + 1, MAXB))
        after = jnp.minimum(b + 2, 3)
        prepare(after, 0)
        finish(b + 1, 1, entry(after, MAXB))
        return carry

    lax.fori_loop(0, 2, step, 0)


def attention(meta, lists, other_lists, q, columns, odds, interpret=False):
    evens = 4 * columns[0].shape[0]
    smem = pl.BlockSpec(memory_space=pltpu.SMEM)
    vmem = pl.BlockSpec(memory_space=pltpu.VMEM)
    hbm = pl.BlockSpec(memory_space=pl.ANY)
    return pl.pallas_call(
        attend,
        out_shape=jax.ShapeDtypeStruct(q.shape, q.dtype),
        in_specs=[smem, smem, smem, vmem] + [hbm] * 10,
        out_specs=vmem,
        scratch_shapes=[pltpu.VMEM((2, evens + ODD, 2, HALF, HEAD_SIZE), jnp.bfloat16)]
        + [pltpu.VMEM((2 * HALF_ROWS, HEAD_SIZE), jnp.bfloat16)] * 2
        + [pltpu.VMEM((KEYS, HEAD_SIZE), jnp.bfloat16)] * 4
        + [pltpu.VMEM((2 * HALF_ROWS, KEYS), jnp.float32)] * 2
        + [pltpu.VMEM((2 * HALF_ROWS, KEYS), jnp.bfloat16), pltpu.SemaphoreType.DMA((10,))],
        compiler_params=pltpu.CompilerParams(vmem_limit_bytes=40 * 2**20),
        cost_estimate=pl.CostEstimate(flops=2**31, bytes_accessed=8 * 2**20, transcendentals=2**22),
        interpret=interpret,
    )(meta, lists, other_lists, q, *columns, *odds)


def assemble_kernel(meta, *refs):
    out_ref = refs[-1]
    for k, ref in enumerate(refs[:-1]):
        column = jnp.bitwise_xor(meta[4], k) * ref.shape[1]
        out_ref[:, pl.ds(pl.multiple_of(column, ref.shape[1]), ref.shape[1])] = ref[...]


def assemble(meta, pieces, interpret=False):
    rows, width = pieces[0].shape
    vmem = pl.BlockSpec(memory_space=pltpu.VMEM)
    return pl.pallas_call(
        assemble_kernel,
        out_shape=jax.ShapeDtypeStruct((rows, width * len(pieces)), pieces[0].dtype),
        in_specs=[pl.BlockSpec(memory_space=pltpu.SMEM)] + [vmem] * len(pieces),
        out_specs=vmem,
        interpret=interpret,
    )(meta, *pieces)


def swap(array, axis):
    return lax.ppermute(array, axis, [(0, 1), (1, 0)])


def around(array, axis, by):
    size = lax.axis_size(axis)
    pairs = [(2 * i + c, 2 * ((i + (by, -by)[c]) % size) + c) for i in range(size) for c in range(2)]
    return lax.ppermute(array, (axis, CORE), pairs)


def body(queries, keyvals, block_index, block_count):
    lists = jnp.concatenate([block_index, block_count[:, None]], axis=1)
    other_lists = swap(lists, YLO)
    meta = jnp.stack([lax.axis_index(a) for a in (Z, X, YLO, CORE, RING)]).astype(jnp.int32)
    heads = lax.axis_size(RING)

    sent = keyvals.reshape(2, STRIP, heads, HEAD_SIZE).transpose(2, 0, 1, 3)
    local = lax.all_to_all(sent, RING, split_axis=0, concat_axis=0, tiled=True)
    local, queries = lax.optimization_barrier((local, queries))
    local = local.reshape(4, 2, 2, STRIP, HEAD_SIZE).transpose(0, 2, 1, 3, 4)
    local = local.reshape(4, 2, HALF, HEAD_SIZE)
    sent_q = queries.reshape(STRIP, heads, GROUP * HEAD_SIZE).transpose(1, 0, 2)
    q = lax.all_to_all(sent_q, RING, split_axis=0, concat_axis=0, tiled=True)
    pairs = lax.axis_size((Z, X))
    before = lax.ppermute(local[3], (Z, X), [(i, i + 1) for i in range(pairs - 1)])
    odd = jnp.stack([before, local[1], local[3]])
    other_odd = swap(odd, CORE)

    gathered = jnp.stack([local[0], local[2]])
    for by in (4, 2, 1):
        gathered = jnp.concatenate([gathered, around(gathered, Z, by)])

    first = around(gathered, X, 1)
    own_swapped = swap(gathered, CORE)
    first, gathered, other_odd, other_lists, own_swapped, q = lax.optimization_barrier(
        (first, gathered, other_odd, other_lists, own_swapped, q)
    )
    far = around(first, X, 1)
    second = around(gathered, X, -1)

    columns = [gathered, first, second, far, own_swapped]
    columns += [swap(column, CORE) for column in columns[1:4]]
    result = attention(meta, lists, other_lists, q, columns, [odd, other_odd])
    pieces = [result[0]]
    for k in range(1, heads):
        pieces.append(lax.ppermute(result[k], RING, [(i, i ^ k) for i in range(heads)]))
    return assemble(meta, pieces)


def solution(mesh):
    pb, kv, ha = mesh.devices.shape
    fine = Mesh(mesh.devices.reshape(pb, kv // 2, 2, ha // 2, 2), (Z, X, YLO, YHI, CORE))
    rows = (Z, X, YLO, YHI, CORE)
    shard = (Z, X, YLO)
    return jax.shard_map(
        body,
        mesh=fine,
        in_specs=(P(rows, None), P(None, rows, None), P(shard, None), P(shard)),
        out_specs=P(rows, None),
        check_vma=False,
    )
```

time: 129 us -> 144 us (1.12)
  the two profiles are of different devices: /device:TPU:8 before, /device:TPU:7 now
where the time goes in v2:
time: 144 us; the launch traced here: 143 us
  starting transfers between devices  94.5 us (66%)
  waiting for transfers between devices  16.5 us (11%)
  Pallas kernels  14.6 us (10%)
  blocking collectives  13.8 us (10%)
  local copies, waits for them, and re-layouts  3.37 us (2%)
    ppermute x6, starting transfers between devices, swap(): return lax.ppermute(array, axis, [(0, 1), (1, 0)])  31.1 us
    ppermute x6, starting transfers between devices, around(): return lax.ppermute(array, (axis, CORE), pairs)  29.9 us
    ppermute x7, starting transfers between devices, body(): lax.ppermute(result[k], RING, [(i, i ^ k) for i in range(heads)])  25.7 us
    all_to_all x1, blocking collectives, body(): local = lax.all_to_all(sent, RING, split_axis=0, concat_axis=0, tiled=True)  13.8 us
    pallas_call x1, Pallas kernels, attention(): pl.pallas_call(attend, out_shape=jax.ShapeDtypeStruct(q.shape, q.dtype),...  12.7 us
    ppermute x6, waiting for transfers between devices, around(): return lax.ppermute(array, (axis, CORE), pairs)  6.57 us
    ppermute x7, waiting for transfers between devices, body(): lax.ppermute(result[k], RING, [(i, i ^ k) for i in range(heads)])  5.91 us
    ppermute x1, starting transfers between devices, body(): lax.ppermute(local[3], (Z, X), [(i, i + 1) for i in range(pairs - 1)])  4.29 us
  transfers between devices with their start and end apart: 21, of which 8 were waited for; matrix products, arithmetic and copies ran while one was open for 1% of the time, Pallas kernels for 0%

profile of v2, /device:TPU:7, one launch (start us, length us, event | category | flops | bytes accessed | tf_op | source)
XLA Modules:
  0.0 143.3 jit_solution(4617789170830733570)
XLA Ops:
  1.0 13.8 %all_to_all.10 = bf16[8,2,32,128]{3,2,1,0:T(8,128)(2,1)S(1)} all-to-all(bf16[8,2,32,128]{3,2,1,0:T(8,128)(2,1)S(1)} %copy.22), channel_id=1, replica_groups=mesh['z'=8,'x'=4,'ylo'=2,'yhi'=4,'core'=2] {'ylo','yhi'}, dimensions={0} | all-to-all | bytes 262144 | tf_op jit(solution)/shard_map/all_to_all | solution.py:186
  14.8 10.6 %collective-permute-start = (bf16[2,2,64,128]{3,2,1,0:T(8,128)(2,1)S(1)}, bf16[2,2,64,128]{3,2,1,0:T(8,128)(2,1)S(1)}, u32[]{:S(2)}, u32[]{:S(2)}) collective-permute-start(bf16[2,2,64,128]{3,2,1,0:T(8,128)(2,1)S(1)} %pad_maximum_fusion.3), channel_id=1, source_target_pairs={{0,256},{1,257},{64,320},{65,321},{128,384},{129,385},{192,448},{1... | collective-permute-start | bytes 196616 | tf_op jit(solution)/shard_map/ppermute | solution.py:176
  27.2 7.8 %collective-permute-start.1 = (bf16[4,2,64,128]{3,2,1,0:T(8,128)(2,1)S(1)}, bf16[4,2,64,128]{3,2,1,0:T(8,128)(2,1)S(1)}, u32[]{:S(2)}, u32[]{:S(2)}) collective-permute-start(bf16[4,2,64,128]{3,2,1,0:T(8,128)(2,1)S(1)} %pad_maximum_fusion.1), channel_id=1, source_target_pairs={{0,128},{1,385},{64,192},{65,449},{128,256},{129,1},{192,320},{193... | collective-permute-start | bytes 393224 | tf_op jit(solution)/shard_map/ppermute | solution.py:176
  35.8 3.5 %all-to-all-start.1 = ((bf16[8,32,1024]{2,1,0:T(8,128)(2,1)}), bf16[8,32,1024]{2,1,0:T(8,128)(2,1)S(1)}, u32[]{:S(2)}, u32[]{:S(2)}) async-start(bf16[8,32,1024]{2,1,0:T(8,128)(2,1)} %bitcast.44), calls=%async_computation.1 | async-start | bytes 1048576 | tf_op jit(solution)/shard_map/all_to_all | solution.py:191
  39.4 3.7 %collective-permute-start.2 = (bf16[8,2,64,128]{3,2,1,0:T(8,128)(2,1)S(1)}, bf16[8,2,64,128]{3,2,1,0:T(8,128)(2,1)S(1)}, u32[]{:S(2)}, u32[]{:S(2)}) collective-permute-start(bf16[8,2,64,128]{3,2,1,0:T(8,128)(2,1)S(1)} %pad_maximum_fusion), channel_id=1, source_target_pairs={{0,64},{1,449},{64,128},{65,1},{128,192},{129,65},{192,256},{193,1... | collective-permute-start | bytes 786440 | tf_op jit(solution)/shard_map/ppermute | solution.py:176
  43.2 3.6 %collective-permute-done.2 = bf16[8,2,64,128]{3,2,1,0:T(8,128)(2,1)S(1)} collective-permute-done((bf16[8,2,64,128]{3,2,1,0:T(8,128)(2,1)S(1)}, bf16[8,2,64,128]{3,2,1,0:T(8,128)(2,1)S(1)}, u32[]{:S(2)}, u32[]{:S(2)}) %collective-permute-start.2) | collective-permute-done | bytes 262176 | tf_op jit(solution)/shard_map/ppermute | solution.py:176
  46.8 6.0 %collective-permute-start.7 = (bf16[16,2,64,128]{3,2,1,0:T(8,128)(2,1)S(1)}, bf16[16,2,64,128]{3,2,1,0:T(8,128)(2,1)S(1)}, u32[]{:S(2)}, u32[]{:S(2)}) collective-permute-start(bf16[16,2,64,128]{3,2,1,0:T(8,128)(2,1)S(1)} %constant_dynamic-update-slice_fusion.refs_0_), channel_id=1, source_target_pairs={{0,1},{1,0},{2,3},{3,2},{4,5},{5,4},{6,7},{7,6},{8,9},{9,8},{10,11... | collective-permute-start | bytes 1572872 | tf_op jit(solution)/shard_map/ppermute | solution.py:170
  52.9 2.5 %collective-permute-start.3 = (bf16[16,2,64,128]{3,2,1,0:T(8,128)(2,1)S(1)}, bf16[16,2,64,128]{3,2,1,0:T(8,128)(2,1)S(1)}, u32[]{:S(2)}, u32[]{:S(2)}) collective-permute-start(bf16[16,2,64,128]{3,2,1,0:T(8,128)(2,1)S(1)} %constant_dynamic-update-slice_fusion.refs_0_), channel_id=1, source_target_pairs={{0,16},{1,49},{16,32},{17,1},{32,48},{33,17},{48,0},{49,33},{2,18}... | collective-permute-start | bytes 1572872 | tf_op jit(solution)/shard_map/ppermute | solution.py:176
  55.4 4.3 %collective-permute-start.4 = (bf16[2,64,128]{2,1,0:T(8,128)(2,1)S(1)}, bf16[2,64,128]{2,1,0:T(8,128)(2,1)S(1)}, u32[]{:S(2)}, u32[]{:S(2)}) collective-permute-start(bf16[2,64,128]{2,1,0:T(8,128)(2,1)S(1)} %bitcast.58), channel_id=1, source_target_pairs={{0,16},{16,32},{32,48},{48,64},{64,80},{80,96},{96,112},{112,128},... | collective-permute-start | bytes 98312 | tf_op jit(solution)/shard_map/ppermute | solution.py:193
  60.8 5.8 %collective-permute-start.5 = (bf16[3,2,64,128]{3,2,1,0:T(8,128)(2,1)S(1)}, bf16[3,2,64,128]{3,2,1,0:T(8,128)(2,1)S(1)}, u32[]{:S(2)}, u32[]{:S(2)}) collective-permute-start(bf16[3,2,64,128]{3,2,1,0:T(8,128)(2,1)S(1)} %pad_maximum_fusion.2.refs_8_), channel_id=1, source_target_pairs={{0,1},{1,0},{2,3},{3,2},{4,5},{5,4},{6,7},{7,6},{8,9},{9,8},{10,11... | collective-permute-start | bytes 294920 | tf_op jit(solution)/shard_map/ppermute | solution.py:170
  66.7 3.2 %collective-permute-start.6 = (s32[2,17]{1,0:T(2,128)S(1)}, s32[2,17]{1,0:T(2,128)S(1)}, u32[]{:S(2)}, u32[]{:S(2)}) collective-permute-start(s32[2,17]{1,0:T(2,128)S(1)} %pad_add_fusion.lists), channel_id=1, source_target_pairs={{0,8},{8,0},{1,9},{9,1},{2,10},{10,2},{3,11},{11,3},{4,12},{12,4},... | collective-permute-start | bytes 416 | tf_op jit(solution)/shard_map/ppermute | solution.py:170
  71.0 1.9 %collective-permute-start.8 = (bf16[16,2,64,128]{3,2,1,0:T(8,128)(2,1)S(1)}, bf16[16,2,64,128]{3,2,1,0:T(8,128)(2,1)S(1)}, u32[]{:S(2)}, u32[]{:S(2)}) collective-permute-start(bf16[16,2,64,128]{3,2,1,0:T(8,128)(2,1)S(1)} %constant_dynamic-update-slice_fusion.refs_0_), channel_id=1, source_target_pairs={{0,48},{1,17},{16,0},{17,33},{32,16},{33,49},{48,32},{49,1},{2,50}... | collective-permute-start | bytes 1572872 | tf_op jit(solution)/shard_map/ppermute | solution.py:176
  72.9 3.4 %collective-permute-start.9 = (bf16[16,2,64,128]{3,2,1,0:T(8,128)(2,1)S(1)}, bf16[16,2,64,128]{3,2,1,0:T(8,128)(2,1)S(1)}, u32[]{:S(2)}, u32[]{:S(2)}) collective-permute-start(bf16[16,2,64,128]{3,2,1,0:T(8,128)(2,1)S(1)} %collective-permute-done.3.refs_1_), channel_id=1, source_target_pairs={{0,16},{1,49},{16,32},{17,1},{32,48},{33,17},{48,0},{49,33},{2,18}... | collective-permute-start | bytes 1572872 | tf_op jit(solution)/shard_map/ppermute | solution.py:176
  76.3 4.8 %collective-permute-start.10 = (bf16[16,2,64,128]{3,2,1,0:T(8,128)(2,1)S(1)}, bf16[16,2,64,128]{3,2,1,0:T(8,128)(2,1)}, u32[]{:S(2)}, u32[]{:S(2)}) collective-permute-start(bf16[16,2,64,128]{3,2,1,0:T(8,128)(2,1)S(1)} %collective-permute-done.3.refs_1_), channel_id=1, source_target_pairs={{0,1},{1,0},{2,3},{3,2},{4,5},{5,4},{6,7},{7,6},{8,9},{9,8},{10,11... | collective-permute-start | bytes 1572872 | tf_op jit(solution)/shard_map/ppermute | solution.py:170
  82.4 9.2 %collective-permute-start.11 = (bf16[16,2,64,128]{3,2,1,0:T(8,128)(2,1)S(1)}, bf16[16,2,64,128]{3,2,1,0:T(8,128)(2,1)}, u32[]{:S(2)}, u32[]{:S(2)}) collective-permute-start(bf16[16,2,64,128]{3,2,1,0:T(8,128)(2,1)S(1)} %collective-permute-done.8.refs_2_), channel_id=1, source_target_pairs={{0,1},{1,0},{2,3},{3,2},{4,5},{5,4},{6,7},{7,6},{8,9},{9,8},{10,11... | collective-permute-start | bytes 1572872 | tf_op jit(solution)/shard_map/ppermute | solution.py:170
  91.7 1.9 %collective-permute-start.12 = (bf16[16,2,64,128]{3,2,1,0:T(8,128)(2,1)S(1)}, bf16[16,2,64,128]{3,2,1,0:T(8,128)(2,1)}, u32[]{:S(2)}, u32[]{:S(2)}) collective-permute-start(bf16[16,2,64,128]{3,2,1,0:T(8,128)(2,1)S(1)} %collective-permute-done.9.refs_3_), channel_id=1, source_target_pairs={{0,1},{1,0},{2,3},{3,2},{4,5},{5,4},{6,7},{7,6},{8,9},{9,8},{10,11... | collective-permute-start | bytes 1572872 | tf_op jit(solution)/shard_map/ppermute | solution.py:170
  95.6 12.7 %shard_map.46 = bf16[8,32,1024]{2,1,0:T(8,128)(2,1)S(1)} custom-call(s32[5]{0:T(128)S(1)} %stack.32.meta, s32[2,17]{1,0:T(2,128)S(1)} %pad_add_fusion.lists, s32[2,17]{1,0:T(2,128)S(1)} %collective-permute-done.6.other_lists, bf16[8,32,1024]{2,1,0:T(8,128)(2,1)S(1)} %all-to-all-done.1.q_ref, ...), custom_call_target="tpu_custom_call" | custom-call | flops 2147483648 | bytes 8388608 | tf_op jit(solution)/shard_map/pallas_call | solution.py:134
  109.0 2.9 %collective-permute-start.19 = (bf16[32,1024]{1,0:T(8,128)(2,1)S(1)}, bf16[32,1024]{1,0:T(8,128)(2,1)S(1)}, u32[]{:S(2)}, u32[]{:S(2)}) collective-permute-start(bf16[32,1024]{1,0:T(8,128)(2,1)S(1)} %get-tuple-element.21), channel_id=1, source_target_pairs={{0,14},{2,12},{4,10},{6,8},{8,6},{10,4},{12,2},{14,0},{1,15},{3,13... | collective-permute-start | bytes 196616 | tf_op jit(solution)/shard_map/ppermute | solution.py:214
  111.8 4.9 %collective-permute-start.18 = (bf16[32,1024]{1,0:T(8,128)(2,1)S(1)}, bf16[32,1024]{1,0:T(8,128)(2,1)S(1)}, u32[]{:S(2)}, u32[]{:S(2)}) collective-permute-start(bf16[32,1024]{1,0:T(8,128)(2,1)S(1)} %get-tuple-element.22), channel_id=1, source_target_pairs={{0,12},{2,14},{4,8},{6,10},{8,4},{10,6},{12,0},{14,2},{1,13},{3,15... | collective-permute-start | bytes 196616 | tf_op jit(solution)/shard_map/ppermute | solution.py:214
  116.7 4.7 %collective-permute-start.17 = (bf16[32,1024]{1,0:T(8,128)(2,1)S(1)}, bf16[32,1024]{1,0:T(8,128)(2,1)S(1)}, u32[]{:S(2)}, u32[]{:S(2)}) collective-permute-start(bf16[32,1024]{1,0:T(8,128)(2,1)S(1)} %get-tuple-element.23), channel_id=1, source_target_pairs={{0,10},{2,8},{4,14},{6,12},{8,2},{10,0},{12,6},{14,4},{1,11},{3,9}... | collective-permute-start | bytes 196616 | tf_op jit(solution)/shard_map/ppermute | solution.py:214
  123.3 3.6 %collective-permute-start.15 = (bf16[32,1024]{1,0:T(8,128)(2,1)S(1)}, bf16[32,1024]{1,0:T(8,128)(2,1)S(1)}, u32[]{:S(2)}, u32[]{:S(2)}) collective-permute-start(bf16[32,1024]{1,0:T(8,128)(2,1)S(1)} %get-tuple-element.25), channel_id=1, source_target_pairs={{0,6},{2,4},{4,2},{6,0},{8,14},{10,12},{12,10},{14,8},{1,7},{3,5},... | collective-permute-start | bytes 196616 | tf_op jit(solution)/shard_map/ppermute | solution.py:214
  127.0 4.3 %collective-permute-start.14 = (bf16[32,1024]{1,0:T(8,128)(2,1)S(1)}, bf16[32,1024]{1,0:T(8,128)(2,1)S(1)}, u32[]{:S(2)}, u32[]{:S(2)}) collective-permute-start(bf16[32,1024]{1,0:T(8,128)(2,1)S(1)} %get-tuple-element.26), channel_id=1, source_target_pairs={{0,4},{2,6},{4,0},{6,2},{8,12},{10,14},{12,8},{14,10},{1,5},{3,7},... | collective-permute-start | bytes 196616 | tf_op jit(solution)/shard_map/ppermute | solution.py:214
  131.3 3.5 %collective-permute-start.13 = (bf16[32,1024]{1,0:T(8,128)(2,1)S(1)}, bf16[32,1024]{1,0:T(8,128)(2,1)S(1)}, u32[]{:S(2)}, u32[]{:S(2)}) collective-permute-start(bf16[32,1024]{1,0:T(8,128)(2,1)S(1)} %get-tuple-element.27), channel_id=1, source_target_pairs={{0,2},{2,0},{4,6},{6,4},{8,10},{10,8},{12,14},{14,12},{1,3},{3,1},... | collective-permute-start | bytes 196616 | tf_op jit(solution)/shard_map/ppermute | solution.py:214
  135.9 4.8 %collective-permute-done.13.refs_1_ = bf16[32,1024]{1,0:T(8,128)(2,1)S(1)} collective-permute-done((bf16[32,1024]{1,0:T(8,128)(2,1)S(1)}, bf16[32,1024]{1,0:T(8,128)(2,1)S(1)}, u32[]{:S(2)}, u32[]{:S(2)}) %collective-permute-start.13) | collective-permute-done | bytes 65568 | tf_op jit(solution)/shard_map/ppermute | solution.py:214
  (65 shorter events, 15.4 us)
Async XLA Ops:
  1.0 34.0 %copy-start.1 = (bf16[32,8192]{1,0:T(8,128)(2,1)S(1)}, bf16[32,8192]{1,0:T(8,128)(2,1)}, u32[]{:S(2)}) copy-start(bf16[32,8192]{1,0:T(8,128)(2,1)} %param.4) | copy-start | bytes 1572868
  14.8 12.4 %collective-permute-start = (bf16[2,2,64,128]{3,2,1,0:T(8,128)(2,1)S(1)}, bf16[2,2,64,128]{3,2,1,0:T(8,128)(2,1)S(1)}, u32[]{:S(2)}, u32[]{:S(2)}) collective-permute-start(bf16[2,2,64,128]{3,2,1,0:T(8,128)(2,1)S(1)} %pad_maximum_fusion.3), channel_id=1, source_target_pairs={{0,256},{1,257},{64,320},{65,321},{128,384},{129,385},{192,448},{1... | collective-permute-start | bytes 196616 | tf_op jit(solution)/shard_map/ppermute | solution.py:176
  27.2 12.1 %collective-permute-start.1 = (bf16[4,2,64,128]{3,2,1,0:T(8,128)(2,1)S(1)}, bf16[4,2,64,128]{3,2,1,0:T(8,128)(2,1)S(1)}, u32[]{:S(2)}, u32[]{:S(2)}) collective-permute-start(bf16[4,2,64,128]{3,2,1,0:T(8,128)(2,1)S(1)} %pad_maximum_fusion.1), channel_id=1, source_target_pairs={{0,128},{1,385},{64,192},{65,449},{128,256},{129,1},{192,320},{193... | collective-permute-start | bytes 393224 | tf_op jit(solution)/shard_map/ppermute | solution.py:176
  35.8 35.2 %all-to-all-start.1 = ((bf16[8,32,1024]{2,1,0:T(8,128)(2,1)}), bf16[8,32,1024]{2,1,0:T(8,128)(2,1)S(1)}, u32[]{:S(2)}, u32[]{:S(2)}) async-start(bf16[8,32,1024]{2,1,0:T(8,128)(2,1)} %bitcast.44), calls=%async_computation.1 | async-start | bytes 1048576 | tf_op jit(solution)/shard_map/all_to_all | solution.py:191
  39.4 7.4 %collective-permute-start.2 = (bf16[8,2,64,128]{3,2,1,0:T(8,128)(2,1)S(1)}, bf16[8,2,64,128]{3,2,1,0:T(8,128)(2,1)S(1)}, u32[]{:S(2)}, u32[]{:S(2)}) collective-permute-start(bf16[8,2,64,128]{3,2,1,0:T(8,128)(2,1)S(1)} %pad_maximum_fusion), channel_id=1, source_target_pairs={{0,64},{1,449},{64,128},{65,1},{128,192},{129,65},{192,256},{193,1... | collective-permute-start | bytes 786440 | tf_op jit(solution)/shard_map/ppermute | solution.py:176
  46.8 24.2 %collective-permute-start.7 = (bf16[16,2,64,128]{3,2,1,0:T(8,128)(2,1)S(1)}, bf16[16,2,64,128]{3,2,1,0:T(8,128)(2,1)S(1)}, u32[]{:S(2)}, u32[]{:S(2)}) collective-permute-start(bf16[16,2,64,128]{3,2,1,0:T(8,128)(2,1)S(1)} %constant_dynamic-update-slice_fusion.refs_0_), channel_id=1, source_target_pairs={{0,1},{1,0},{2,3},{3,2},{4,5},{5,4},{6,7},{7,6},{8,9},{9,8},{10,11... | collective-permute-start | bytes 1572872 | tf_op jit(solution)/shard_map/ppermute | solution.py:170
  52.9 18.1 %collective-permute-start.3 = (bf16[16,2,64,128]{3,2,1,0:T(8,128)(2,1)S(1)}, bf16[16,2,64,128]{3,2,1,0:T(8,128)(2,1)S(1)}, u32[]{:S(2)}, u32[]{:S(2)}) collective-permute-start(bf16[16,2,64,128]{3,2,1,0:T(8,128)(2,1)S(1)} %constant_dynamic-update-slice_fusion.refs_0_), channel_id=1, source_target_pairs={{0,16},{1,49},{16,32},{17,1},{32,48},{33,17},{48,0},{49,33},{2,18}... | collective-permute-start | bytes 1572872 | tf_op jit(solution)/shard_map/ppermute | solution.py:176
  55.4 5.4 %collective-permute-start.4 = (bf16[2,64,128]{2,1,0:T(8,128)(2,1)S(1)}, bf16[2,64,128]{2,1,0:T(8,128)(2,1)S(1)}, u32[]{:S(2)}, u32[]{:S(2)}) collective-permute-start(bf16[2,64,128]{2,1,0:T(8,128)(2,1)S(1)} %bitcast.58), channel_id=1, source_target_pairs={{0,16},{16,32},{32,48},{48,64},{64,80},{80,96},{96,112},{112,128},... | collective-permute-start | bytes 98312 | tf_op jit(solution)/shard_map/ppermute | solution.py:193
  60.8 10.2 %collective-permute-start.5 = (bf16[3,2,64,128]{3,2,1,0:T(8,128)(2,1)S(1)}, bf16[3,2,64,128]{3,2,1,0:T(8,128)(2,1)S(1)}, u32[]{:S(2)}, u32[]{:S(2)}) collective-permute-start(bf16[3,2,64,128]{3,2,1,0:T(8,128)(2,1)S(1)} %pad_maximum_fusion.2.refs_8_), channel_id=1, source_target_pairs={{0,1},{1,0},{2,3},{3,2},{4,5},{5,4},{6,7},{7,6},{8,9},{9,8},{10,11... | collective-permute-start | bytes 294920 | tf_op jit(solution)/shard_map/ppermute | solution.py:170
  66.7 4.3 %collective-permute-start.6 = (s32[2,17]{1,0:T(2,128)S(1)}, s32[2,17]{1,0:T(2,128)S(1)}, u32[]{:S(2)}, u32[]{:S(2)}) collective-permute-start(s32[2,17]{1,0:T(2,128)S(1)} %pad_add_fusion.lists), channel_id=1, source_target_pairs={{0,8},{8,0},{1,9},{9,1},{2,10},{10,2},{3,11},{11,3},{4,12},{12,4},... | collective-permute-start | bytes 416 | tf_op jit(solution)/shard_map/ppermute | solution.py:170
  71.0 11.4 %collective-permute-start.8 = (bf16[16,2,64,128]{3,2,1,0:T(8,128)(2,1)S(1)}, bf16[16,2,64,128]{3,2,1,0:T(8,128)(2,1)S(1)}, u32[]{:S(2)}, u32[]{:S(2)}) collective-permute-start(bf16[16,2,64,128]{3,2,1,0:T(8,128)(2,1)S(1)} %constant_dynamic-update-slice_fusion.refs_0_), channel_id=1, source_target_pairs={{0,48},{1,17},{16,0},{17,33},{32,16},{33,49},{48,32},{49,1},{2,50}... | collective-permute-start | bytes 1572872 | tf_op jit(solution)/shard_map/ppermute | solution.py:176
  72.9 18.7 %collective-permute-start.9 = (bf16[16,2,64,128]{3,2,1,0:T(8,128)(2,1)S(1)}, bf16[16,2,64,128]{3,2,1,0:T(8,128)(2,1)S(1)}, u32[]{:S(2)}, u32[]{:S(2)}) collective-permute-start(bf16[16,2,64,128]{3,2,1,0:T(8,128)(2,1)S(1)} %collective-permute-done.3.refs_1_), channel_id=1, source_target_pairs={{0,16},{1,49},{16,32},{17,1},{32,48},{33,17},{48,0},{49,33},{2,18}... | collective-permute-start | bytes 1572872 | tf_op jit(solution)/shard_map/ppermute | solution.py:176
  76.3 17.4 %collective-permute-start.10 = (bf16[16,2,64,128]{3,2,1,0:T(8,128)(2,1)S(1)}, bf16[16,2,64,128]{3,2,1,0:T(8,128)(2,1)}, u32[]{:S(2)}, u32[]{:S(2)}) collective-permute-start(bf16[16,2,64,128]{3,2,1,0:T(8,128)(2,1)S(1)} %collective-permute-done.3.refs_1_), channel_id=1, source_target_pairs={{0,1},{1,0},{2,3},{3,2},{4,5},{5,4},{6,7},{7,6},{8,9},{9,8},{10,11... | collective-permute-start | bytes 1572872 | tf_op jit(solution)/shard_map/ppermute | solution.py:170
  82.4 11.3 %collective-permute-start.11 = (bf16[16,2,64,128]{3,2,1,0:T(8,128)(2,1)S(1)}, bf16[16,2,64,128]{3,2,1,0:T(8,128)(2,1)}, u32[]{:S(2)}, u32[]{:S(2)}) collective-permute-start(bf16[16,2,64,128]{3,2,1,0:T(8,128)(2,1)S(1)} %collective-permute-done.8.refs_2_), channel_id=1, source_target_pairs={{0,1},{1,0},{2,3},{3,2},{4,5},{5,4},{6,7},{7,6},{8,9},{9,8},{10,11... | collective-permute-start | bytes 1572872 | tf_op jit(solution)/shard_map/ppermute | solution.py:170
  91.7 3.9 %collective-permute-start.12 = (bf16[16,2,64,128]{3,2,1,0:T(8,128)(2,1)S(1)}, bf16[16,2,64,128]{3,2,1,0:T(8,128)(2,1)}, u32[]{:S(2)}, u32[]{:S(2)}) collective-permute-start(bf16[16,2,64,128]{3,2,1,0:T(8,128)(2,1)S(1)} %collective-permute-done.9.refs_3_), channel_id=1, source_target_pairs={{0,1},{1,0},{2,3},{3,2},{4,5},{5,4},{6,7},{7,6},{8,9},{9,8},{10,11... | collective-permute-start | bytes 1572872 | tf_op jit(solution)/shard_map/ppermute | solution.py:170
  93.7 14.6 %copy-start = (s32[5]{0:T(128)}, s32[5]{0:T(128)S(1)}, u32[]{:S(2)}) copy-start(s32[5]{0:T(128)S(1)} %stack.32.meta) | copy-start | bytes 64
  109.0 18.0 %collective-permute-start.19 = (bf16[32,1024]{1,0:T(8,128)(2,1)S(1)}, bf16[32,1024]{1,0:T(8,128)(2,1)S(1)}, u32[]{:S(2)}, u32[]{:S(2)}) collective-permute-start(bf16[32,1024]{1,0:T(8,128)(2,1)S(1)} %get-tuple-element.21), channel_id=1, source_target_pairs={{0,14},{2,12},{4,10},{6,8},{8,6},{10,4},{12,2},{14,0},{1,15},{3,13... | collective-permute-start | bytes 196616 | tf_op jit(solution)/shard_map/ppermute | solution.py:214
  111.8 19.4 %collective-permute-start.18 = (bf16[32,1024]{1,0:T(8,128)(2,1)S(1)}, bf16[32,1024]{1,0:T(8,128)(2,1)S(1)}, u32[]{:S(2)}, u32[]{:S(2)}) collective-permute-start(bf16[32,1024]{1,0:T(8,128)(2,1)S(1)} %get-tuple-element.22), channel_id=1, source_target_pairs={{0,12},{2,14},{4,8},{6,10},{8,4},{10,6},{12,0},{14,2},{1,13},{3,15... | collective-permute-start | bytes 196616 | tf_op jit(solution)/shard_map/ppermute | solution.py:214
  116.7 18.0 %collective-permute-start.17 = (bf16[32,1024]{1,0:T(8,128)(2,1)S(1)}, bf16[32,1024]{1,0:T(8,128)(2,1)S(1)}, u32[]{:S(2)}, u32[]{:S(2)}) collective-permute-start(bf16[32,1024]{1,0:T(8,128)(2,1)S(1)} %get-tuple-element.23), channel_id=1, source_target_pairs={{0,10},{2,8},{4,14},{6,12},{8,2},{10,0},{12,6},{14,4},{1,11},{3,9}... | collective-permute-start | bytes 196616 | tf_op jit(solution)/shard_map/ppermute | solution.py:214
  121.4 13.4 %collective-permute-start.16 = (bf16[32,1024]{1,0:T(8,128)(2,1)S(1)}, bf16[32,1024]{1,0:T(8,128)(2,1)S(1)}, u32[]{:S(2)}, u32[]{:S(2)}) collective-permute-start(bf16[32,1024]{1,0:T(8,128)(2,1)S(1)} %get-tuple-element.24), channel_id=1, source_target_pairs={{0,8},{2,10},{4,12},{6,14},{8,0},{10,2},{12,4},{14,6},{1,9},{3,11}... | collective-permute-start | bytes 196616 | tf_op jit(solution)/shard_map/ppermute | solution.py:214
  123.3 11.5 %collective-permute-start.15 = (bf16[32,1024]{1,0:T(8,128)(2,1)S(1)}, bf16[32,1024]{1,0:T(8,128)(2,1)S(1)}, u32[]{:S(2)}, u32[]{:S(2)}) collective-permute-start(bf16[32,1024]{1,0:T(8,128)(2,1)S(1)} %get-tuple-element.25), channel_id=1, source_target_pairs={{0,6},{2,4},{4,2},{6,0},{8,14},{10,12},{12,10},{14,8},{1,7},{3,5},... | collective-permute-start | bytes 196616 | tf_op jit(solution)/shard_map/ppermute | solution.py:214
  127.0 13.8 %copy-start.2 = (bf16[32,1024]{1,0:T(8,128)(2,1)}, bf16[32,1024]{1,0:T(8,128)(2,1)S(1)}, u32[]{:S(2)}) copy-start(bf16[32,1024]{1,0:T(8,128)(2,1)S(1)} %collective-permute-done.19.refs_7_) | copy-start | bytes 196612
  127.0 8.9 %collective-permute-start.14 = (bf16[32,1024]{1,0:T(8,128)(2,1)S(1)}, bf16[32,1024]{1,0:T(8,128)(2,1)S(1)}, u32[]{:S(2)}, u32[]{:S(2)}) collective-permute-start(bf16[32,1024]{1,0:T(8,128)(2,1)S(1)} %get-tuple-element.26), channel_id=1, source_target_pairs={{0,4},{2,6},{4,0},{6,2},{8,12},{10,14},{12,8},{14,10},{1,5},{3,7},... | collective-permute-start | bytes 196616 | tf_op jit(solution)/shard_map/ppermute | solution.py:214
  131.3 9.5 %collective-permute-start.13 = (bf16[32,1024]{1,0:T(8,128)(2,1)S(1)}, bf16[32,1024]{1,0:T(8,128)(2,1)S(1)}, u32[]{:S(2)}, u32[]{:S(2)}) collective-permute-start(bf16[32,1024]{1,0:T(8,128)(2,1)S(1)} %get-tuple-element.27), channel_id=1, source_target_pairs={{0,2},{2,0},{4,6},{6,4},{8,10},{10,8},{12,14},{14,12},{1,3},{3,1},... | collective-permute-start | bytes 196616 | tf_op jit(solution)/shard_map/ppermute | solution.py:214
  (8 other events, 43.0 us)

commit v3 on v1

v3 whole, which is shorter than its diff:
```python
import math

import jax
import jax.numpy as jnp
from jax import lax
from jax.experimental import pallas as pl
from jax.experimental.pallas import tpu as pltpu
from jax.sharding import Mesh, PartitionSpec as P

HEAD_SIZE = 128
BLOCK_POSITIONS = 128
MAXB = 16
KEYS = MAXB * BLOCK_POSITIONS
HALF = BLOCK_POSITIONS // 2
STRIP = 32
GROUP = 8
ROWS = GROUP * STRIP
ODD = 3
NEGATIVE = -1e30
FACTOR = math.log2(math.e) / math.sqrt(HEAD_SIZE)
Z, X, YLO, YHI, CORE = "z", "x", "ylo", "yhi", "core"
RING = (YLO, YHI)


def attend(meta, lists, other_lists, q_ref, even, other_even, odd, other_odd, out_ref, qs, keys, values, scores, weights):
    z, x, ylo, core = (meta[i] for i in range(4))
    pair = z * 4 + x
    cell = lax.broadcasted_iota(jnp.int32, (ROWS, BLOCK_POSITIONS), 1)
    row = lax.broadcasted_iota(jnp.int32, (ROWS, BLOCK_POSITIONS), 0)
    cell_core = jnp.bitwise_xor(cell // HALF, core)
    key_position = (cell % HALF) // STRIP * HALF + cell_core * STRIP + cell % STRIP
    row_position = core * STRIP + row % STRIP

    def one_block(b, carry):
        mine = (b // 2) == ylo
        inside = b % 2
        count = jnp.where(mine, lists[inside, MAXB], other_lists[inside, MAXB])
        for e in range(MAXB):
            j = jnp.where(mine, lists[inside, e], other_lists[inside, e])
            is_even = j % 2 == 0
            even_row = (j // 4) % 4 * (even.shape[0] // 4) + j // 16 * 2 + (j // 2) % 2
            odd_row = jnp.clip((j - 4 * pair + 1) // 2, 0, ODD - 1)
            for rc, (evens, odds) in enumerate(((even, odd), (other_even, other_odd))):
                span = pl.ds(e * BLOCK_POSITIONS + rc * HALF, HALF)
                keys[span, :] = jnp.where(is_even, evens[even_row, 0], odds[odd_row, 0])
                values[span, :] = jnp.where(is_even, evens[even_row, 1], odds[odd_row, 1])
        for strip in range(2):
            for h in range(GROUP):
                qs[pl.ds((strip * GROUP + h) * STRIP, STRIP), :] = q_ref[
                    2 * b + strip, :, h * HEAD_SIZE : (h + 1) * HEAD_SIZE
                ]
        for g in range(MAXB // 2):
            s = lax.dot_general(
                qs[...],
                keys[g * 256 : (g + 1) * 256, :],
                (((1,), (1,)), ((), ())),
                preferred_element_type=jnp.float32,
            )
            for e in (2 * g, 2 * g + 1):
                for strip in range(2):
                    lines = slice(strip * ROWS, (strip + 1) * ROWS)
                    part = s[lines, (e % 2) * 128 : (e % 2 + 1) * 128]
                    keep = key_position <= row_position + strip * HALF if e == 0 else e < count
                    scores[lines, e * 128 : (e + 1) * 128] = jnp.where(keep, part, NEGATIVE)
        for strip in range(2):
            lines = slice(strip * ROWS, (strip + 1) * ROWS)
            peak = scores[lines, 0:128]
            for e in range(1, MAXB):
                peak = jnp.maximum(peak, scores[lines, e * 128 : (e + 1) * 128])
            top = jnp.max(peak, axis=1, keepdims=True) * FACTOR
            total = jnp.zeros((ROWS, BLOCK_POSITIONS), jnp.float32)
            for e in range(MAXB):
                span = slice(e * 128, (e + 1) * 128)
                w = jnp.exp2(scores[lines, span] * FACTOR - top)
                total = total + w
                weights[lines, span] = w.astype(jnp.bfloat16)
            numerator = jnp.dot(weights[lines, :], values[...], preferred_element_type=jnp.float32)
            result = (numerator / jnp.sum(total, axis=1, keepdims=True)).astype(jnp.bfloat16)
            for h in range(GROUP):
                out_ref[2 * b + strip, :, h * HEAD_SIZE : (h + 1) * HEAD_SIZE] = result[h * STRIP : (h + 1) * STRIP]
        return carry

    lax.fori_loop(0, 4, one_block, 0)


def attention(meta, lists, other_lists, q, even, other_even, odd, other_odd, interpret=False):
    smem = pl.BlockSpec(memory_space=pltpu.SMEM)
    vmem = pl.BlockSpec(memory_space=pltpu.VMEM)
    return pl.pallas_call(
        attend,
        out_shape=jax.ShapeDtypeStruct(q.shape, q.dtype),
        in_specs=[smem, smem, smem] + [vmem] * 5,
        out_specs=vmem,
        scratch_shapes=[
            pltpu.VMEM((2 * ROWS, HEAD_SIZE), jnp.bfloat16),
            pltpu.VMEM((KEYS, HEAD_SIZE), jnp.bfloat16),
            pltpu.VMEM((KEYS, HEAD_SIZE), jnp.bfloat16),
            pltpu.VMEM((2 * ROWS, KEYS), jnp.float32),
            pltpu.VMEM((2 * ROWS, KEYS), jnp.bfloat16),
        ],
        compiler_params=pltpu.CompilerParams(vmem_limit_bytes=40 * 2**20),
        cost_estimate=pl.CostEstimate(flops=2**31, bytes_accessed=8 * 2**20, transcendentals=2**22),
        interpret=interpret,
    )(meta, lists, other_lists, q, even, other_even, odd, other_odd)


def swap(array, axis):
    return lax.ppermute(array, axis, [(0, 1), (1, 0)])


def body(queries, keyvals, block_index, block_count):
    lists = jnp.concatenate([block_index, block_count[:, None]], axis=1)
    meta = jnp.stack([lax.axis_index(a) for a in (Z, X, YLO, CORE)]).astype(jnp.int32)
    heads = lax.axis_size(RING)

    sent = keyvals.reshape(2, STRIP, heads, HEAD_SIZE).transpose(2, 0, 1, 3)
    local = lax.all_to_all(sent, RING, split_axis=0, concat_axis=0, tiled=True)
    local = local.reshape(4, 2, 2, STRIP, HEAD_SIZE).transpose(0, 2, 1, 3, 4)
    local = local.reshape(4, 2, HALF, HEAD_SIZE)

    summary = jnp.stack([local[0], local[2]])
    copies = jnp.broadcast_to(summary[None], (lax.axis_size(Z),) + summary.shape)
    column = lax.all_to_all(copies, Z, split_axis=0, concat_axis=0, tiled=True)
    column = column.reshape((-1,) + summary.shape[1:])
    even = lax.all_gather(column, X, axis=0, tiled=True)

    queries, local, lists = lax.optimization_barrier((queries, local, lists, column))[:3]
    sent_q = queries.reshape(STRIP, heads, GROUP * HEAD_SIZE).transpose(1, 0, 2)
    q = lax.all_to_all(sent_q, RING, split_axis=0, concat_axis=0, tiled=True)
    other_lists = swap(lists, YLO)
    pairs = lax.axis_size((Z, X))
    before = lax.ppermute(local[3], (Z, X), [(i, i + 1) for i in range(pairs - 1)])
    odd = jnp.stack([before, local[1], local[3]])
    other_odd = swap(odd, CORE)
    even, q, other_lists, odd, other_odd = lax.optimization_barrier((even, q, other_lists, odd, other_odd))

    result = attention(meta, lists, other_lists, q, even, swap(even, CORE), odd, other_odd)
    result = lax.all_to_all(result, RING, split_axis=0, concat_axis=0, tiled=True)
    return result.transpose(1, 0, 2).reshape(STRIP, heads * GROUP * HEAD_SIZE)


def solution(mesh):
    pb, kv, ha = mesh.devices.shape
    fine = Mesh(mesh.devices.reshape(pb, kv // 2, 2, ha // 2, 2), (Z, X, YLO, YHI, CORE))
    rows = (Z, X, YLO, YHI, CORE)
    shard = (Z, X, YLO)
    return jax.shard_map(
        body,
        mesh=fine,
        in_specs=(P(rows, None), P(None, rows, None), P(shard, None), P(shard)),
        out_specs=P(rows, None),
        check_vma=False,
    )
```

time: 129 us -> 128 us (level)
  starting transfers between devices: 36 us -> 13.1 us
  waiting for transfers between devices: 5.61 us -> 20.4 us
  between operations: 0.27 us -> 13.5 us
  blocking collectives: 70.7 us -> 64.7 us
    all_gather x1 -> x0, blocking collectives: 31.1 us -> none  [body(): gathered = lax.all_gather(summary, Z, axis=0, tiled=True)]
    all_to_all x0 -> x1, blocking collectives: none -> 25.5 us  [body(): column = lax.all_to_all(copies, Z, split_axis=0, concat_axis=0, tiled=True)]
    ppermute x4 -> x0, starting transfers between devices: 15.2 us -> none  [shift(): lax.ppermute(array, axis, [(i, (i + by) % size) for i in range(size)])]
    all_gather x0 -> x1, waiting for transfers between devices: none -> 10.7 us  [body(): even = lax.all_gather(column, X, axis=0, tiled=True)]
    ppermute x7 -> x3, starting transfers between devices: 14.4 us -> 5.75 us  [swap(): return lax.ppermute(array, axis, [(0, 1), (1, 0)])]
    ppermute x7 -> x3, waiting for transfers between devices: 1.75 us -> 7.79 us  [swap(): return lax.ppermute(array, axis, [(0, 1), (1, 0)])]
    ppermute x4 -> x0, waiting for transfers between devices: 2.39 us -> none  [shift(): lax.ppermute(array, axis, [(i, (i + by) % size) for i in range(size)])]
    unnamed x11 -> x9, local copies, waits for them, and re-layouts: 2.46 us -> 2.58 us
  transfers between devices with their start and end apart: 13 -> 6, of which waited for: 3 -> 4; matrix products, arithmetic and copies ran while one was open for 1% -> 1% of each run, Pallas kernels for 0% -> 0%
where the time goes in v3:
time: 128 us; the launch traced here: 127 us
  blocking collectives  64.7 us (51%)
  waiting for transfers between devices  20.4 us (16%)
  between operations  13.5 us (11%)
  starting transfers between devices  13.1 us (10%)
  Pallas kernels  10.7 us (8%)
  local copies, waits for them, and re-layouts  4.52 us (4%)
    all_to_all x1, blocking collectives, body(): column = lax.all_to_all(copies, Z, split_axis=0, concat_axis=0, tiled=True)  25.5 us
    all_to_all x1, blocking collectives, body(): lax.all_to_all(result, RING, split_axis=0, concat_axis=0, tiled=True)  23.4 us
    all_to_all x1, blocking collectives, body(): local = lax.all_to_all(sent, RING, split_axis=0, concat_axis=0, tiled=True)  15.8 us
    pallas_call x1, Pallas kernels, attention(): pl.pallas_call(attend, out_shape=jax.ShapeDtypeStruct(q.shape, q.dtype),...  10.7 us
    all_gather x1, waiting for transfers between devices, body(): even = lax.all_gather(column, X, axis=0, tiled=True)  10.7 us
    ppermute x3, waiting for transfers between devices, swap(): return lax.ppermute(array, axis, [(0, 1), (1, 0)])  7.79 us
    ppermute x3, starting transfers between devices, swap(): return lax.ppermute(array, axis, [(0, 1), (1, 0)])  5.75 us
    all_to_all x1, starting transfers between devices, body(): q = lax.all_to_all(sent_q, RING, split_axis=0, concat_axis=0, tiled=True)  3.93 us
  transfers between devices with their start and end apart: 6, of which 4 were waited for; matrix products, arithmetic and copies ran while one was open for 1% of the time, Pallas kernels for 0%

profile of v3, /device:TPU:8, one launch (start us, length us, event | category | flops | bytes accessed | tf_op | source)
XLA Modules:
  0.0 127.1 jit_solution(15190224795609195625)
XLA Ops:
  6.5 1.0 copy.26
  7.6 15.8 %all_to_all.20 = bf16[8,2,32,128]{3,2,1,0:T(8,128)(2,1)S(1)} all-to-all(bf16[8,2,32,128]{3,2,1,0:T(8,128)(2,1)S(1)} %copy.17), channel_id=1, replica_groups=mesh['z'=8,'x'=4,'ylo'=2,'yhi'=4,'core'=2] {'ylo','yhi'}, dimensions={0} | all-to-all | bytes 262144 | tf_op jit(solution)/shard_map/all_to_all | solution.py:117
  23.4 0.1 broadcast_in_dim.10
  23.6 25.5 %all_to_all.21 = bf16[8,2,2,64,128]{4,3,2,1,0:T(8,128)(2,1)} all-to-all(bf16[8,2,2,64,128]{4,3,2,1,0:T(8,128)(2,1)S(1)} %broadcast_in_dim.10), channel_id=1, replica_groups=mesh['z'=8,'x'=4,'ylo'=2,'yhi'=4,'core'=2] {'z'}, dimensions={0} | all-to-all | bytes 1048576 | tf_op jit(solution)/shard_map/all_to_all | solution.py:123
  49.0 0.0 all-gather.2.cloned.1.call-update
  49.1 0.1 copy.19
  49.2 0.1 pad_add_fusion.lists
  49.3 0.8 copy.28
  50.1 3.9 %all-to-all-start.2 = ((bf16[8,32,1024]{2,1,0:T(8,128)(2,1)}), bf16[8,32,1024]{2,1,0:T(8,128)(2,1)S(1)}, u32[]{:S(2)}, u32[]{:S(2)}) async-start(bf16[8,32,1024]{2,1,0:T(8,128)(2,1)} %bitcast.31), calls=%async_computation.2 | async-start | bytes 1048576 | tf_op jit(solution)/shard_map/all_to_all | solution.py:129
  54.0 3.4 %collective-permute-start.1 = (bf16[2,64,128]{2,1,0:T(8,128)(2,1)S(1)}, bf16[2,64,128]{2,1,0:T(8,128)(2,1)S(1)}, u32[]{:S(2)}, u32[]{:S(2)}) collective-permute-start(bf16[2,64,128]{2,1,0:T(8,128)(2,1)S(1)} %get-tuple-element.21), channel_id=1, source_target_pairs={{0,16},{16,32},{32,48},{48,64},{64,80},{80,96},{96,112},{112,128},... | collective-permute-start | bytes 98312 | tf_op jit(solution)/shard_map/ppermute | solution.py:132
  57.5 1.9 %collective-permute-done.1 = bf16[2,64,128]{2,1,0:T(8,128)(2,1)S(1)} collective-permute-done((bf16[2,64,128]{2,1,0:T(8,128)(2,1)S(1)}, bf16[2,64,128]{2,1,0:T(8,128)(2,1)S(1)}, u32[]{:S(2)}, u32[]{:S(2)}) %collective-permute-start.1) | collective-permute-done | bytes 32800 | tf_op jit(solution)/shard_map/ppermute | solution.py:132
  59.4 1.9 %collective-permute-start.2 = (bf16[3,2,64,128]{3,2,1,0:T(8,128)(2,1)S(1)}, bf16[3,2,64,128]{3,2,1,0:T(8,128)(2,1)S(1)}, u32[]{:S(2)}, u32[]{:S(2)}) collective-permute-start(bf16[3,2,64,128]{3,2,1,0:T(8,128)(2,1)S(1)} %pad_maximum_fusion.odd), channel_id=1, source_target_pairs={{0,1},{1,0},{2,3},{3,2},{4,5},{5,4},{6,7},{7,6},{8,9},{9,8},{10,11... | collective-permute-start | bytes 294920 | tf_op jit(solution)/shard_map/ppermute | solution.py:108
  61.3 1.9 %collective-permute-start = (s32[2,17]{1,0:T(2,128)S(1)}, s32[2,17]{1,0:T(2,128)S(1)}, u32[]{:S(2)}, u32[]{:S(2)}) collective-permute-start(s32[2,17]{1,0:T(2,128)S(1)} %pad_add_fusion.lists), channel_id=1, source_target_pairs={{0,8},{8,0},{1,9},{9,1},{2,10},{10,2},{3,11},{11,3},{4,12},{12,4},... | collective-permute-start | bytes 416 | tf_op jit(solution)/shard_map/ppermute | solution.py:108
  63.2 3.5 %collective-permute-done.other_lists = s32[2,17]{1,0:T(2,128)S(1)} collective-permute-done((s32[2,17]{1,0:T(2,128)S(1)}, s32[2,17]{1,0:T(2,128)S(1)}, u32[]{:S(2)}, u32[]{:S(2)}) %collective-permute-start) | collective-permute-done | bytes 168 | tf_op jit(solution)/shard_map/ppermute | solution.py:108
  66.8 0.0 collective-permute-done.2.other_odd
  66.8 0.0 all-to-all-done.2.q_ref
  66.8 10.7 %all-gather.2.cloned.1.call-done.even = bf16[64,2,64,128]{3,2,1,0:T(8,128)(2,1)} async-done(((bf16[16,2,64,128]{3,2,1,0:T(8,128)(2,1)}), bf16[64,2,64,128]{3,2,1,0:T(8,128)(2,1)}) %all-gather.2.cloned.1.call-update) | async-done | bytes 2097168 | tf_op jit(solution)/shard_map/all_gather | solution.py:125
  77.5 1.9 %collective-permute-start.3 = (bf16[64,2,64,128]{3,2,1,0:T(8,128)(2,1)}, bf16[64,2,64,128]{3,2,1,0:T(8,128)(2,1)S(1)}, u32[]{:S(2)}, u32[]{:S(2)}) collective-permute-start(bf16[64,2,64,128]{3,2,1,0:T(8,128)(2,1)} %all-gather.2.cloned.1.call-done.even), channel_id=1, source_target_pairs={{0,1},{1,0},{2,3},{3,2},{4,5},{5,4},{6,7},{7,6},{8,9},{9,8},{10,11... | collective-permute-start | bytes 6291464 | tf_op jit(solution)/shard_map/ppermute | solution.py:108
  79.4 0.1 pad_add_fusion.1.meta
  79.5 4.3 %collective-permute-done.3.other_even = bf16[64,2,64,128]{3,2,1,0:T(8,128)(2,1)S(1)} collective-permute-done((bf16[64,2,64,128]{3,2,1,0:T(8,128)(2,1)}, bf16[64,2,64,128]{3,2,1,0:T(8,128)(2,1)S(1)}, u32[]{:S(2)}, u32[]{:S(2)}) %collective-permute-start.3) | collective-permute-done | bytes 2097184 | tf_op jit(solution)/shard_map/ppermute | solution.py:108
  83.7 1.6 %copy-done = bf16[64,2,64,128]{3,2,1,0:T(8,128)(2,1)S(1)} copy-done((bf16[64,2,64,128]{3,2,1,0:T(8,128)(2,1)S(1)}, bf16[64,2,64,128]{3,2,1,0:T(8,128)(2,1)}, u32[]{:S(2)}) %copy-start) | copy-done | bytes 2097176
  85.3 10.7 %shard_map.46 = bf16[8,32,1024]{2,1,0:T(8,128)(2,1)S(1)} custom-call(s32[4]{0:T(128)S(1)} %pad_add_fusion.1.meta, s32[2,17]{1,0:T(2,128)S(1)} %pad_add_fusion.lists, s32[2,17]{1,0:T(2,128)S(1)} %collective-permute-done.other_lists, bf16[8,32,1024]{2,1,0:T(8,128)(2,1)S(1)} %all-to-all-done.2.q_ref, bf16[64,2,64,128]{3,2,1,0:T(8,128)(2,1)S(1)} %copy-done, ...), custom_call_target="tpu_custom_call" | custom-call | flops 2147483648 | bytes 8388608 | tf_op jit(solution)/shard_map/pallas_call | solution.py:89
  96.0 23.4 %all_to_all.22 = bf16[8,32,1024]{2,1,0:T(8,128)(2,1)S(1)} all-to-all(bf16[8,32,1024]{2,1,0:T(8,128)(2,1)S(1)} %shard_map.46), channel_id=1, replica_groups=mesh['z'=8,'x'=4,'ylo'=2,'yhi'=4,'core'=2] {'ylo','yhi'}, dimensions={0} | all-to-all | bytes 1048576 | tf_op jit(solution)/shard_map/all_to_all | solution.py:138
  119.4 0.8 copy.25
  (17 shorter events, 0.1 us)
Async XLA Ops:
  6.5 42.5 %copy-start.3 = (s32[2]{0:T(128)S(1)}, s32[2]{0:T(128)}, u32[]{:S(2)}) copy-start(s32[2]{0:T(128)} %param.7) | copy-start | bytes 28
  6.5 42.6 %copy-start.2 = (s32[2,16]{1,0:T(2,128)S(1)}, s32[2,16]{1,0:T(2,128)}, u32[]{:S(2)}) copy-start(s32[2,16]{1,0:T(2,128)} %param.6) | copy-start | bytes 388
  6.5 42.7 %copy-start.1 = (bf16[32,8192]{1,0:T(8,128)(2,1)S(1)}, bf16[32,8192]{1,0:T(8,128)(2,1)}, u32[]{:S(2)}) copy-start(bf16[32,8192]{1,0:T(8,128)(2,1)} %param.4) | copy-start | bytes 1572868
  6.5 70.9 %all-gather.2.cloned.1.call-start = ((), (), s32[]{:S(2)}) async-start(), calls=%async_computation.4 | async-start | bytes 2621440 | tf_op jit(solution)/shard_map/all_gather | solution.py:125
  50.1 16.7 %all-to-all-start.2 = ((bf16[8,32,1024]{2,1,0:T(8,128)(2,1)}), bf16[8,32,1024]{2,1,0:T(8,128)(2,1)S(1)}, u32[]{:S(2)}, u32[]{:S(2)}) async-start(bf16[8,32,1024]{2,1,0:T(8,128)(2,1)} %bitcast.31), calls=%async_computation.2 | async-start | bytes 1048576 | tf_op jit(solution)/shard_map/all_to_all | solution.py:129
  54.0 5.3 %collective-permute-start.1 = (bf16[2,64,128]{2,1,0:T(8,128)(2,1)S(1)}, bf16[2,64,128]{2,1,0:T(8,128)(2,1)S(1)}, u32[]{:S(2)}, u32[]{:S(2)}) collective-permute-start(bf16[2,64,128]{2,1,0:T(8,128)(2,1)S(1)} %get-tuple-element.21), channel_id=1, source_target_pairs={{0,16},{16,32},{32,48},{48,64},{64,80},{80,96},{96,112},{112,128},... | collective-permute-start | bytes 98312 | tf_op jit(solution)/shard_map/ppermute | solution.py:132
  59.4 7.4 %collective-permute-start.2 = (bf16[3,2,64,128]{3,2,1,0:T(8,128)(2,1)S(1)}, bf16[3,2,64,128]{3,2,1,0:T(8,128)(2,1)S(1)}, u32[]{:S(2)}, u32[]{:S(2)}) collective-permute-start(bf16[3,2,64,128]{3,2,1,0:T(8,128)(2,1)S(1)} %pad_maximum_fusion.odd), channel_id=1, source_target_pairs={{0,1},{1,0},{2,3},{3,2},{4,5},{5,4},{6,7},{7,6},{8,9},{9,8},{10,11... | collective-permute-start | bytes 294920 | tf_op jit(solution)/shard_map/ppermute | solution.py:108
  61.3 5.5 %collective-permute-start = (s32[2,17]{1,0:T(2,128)S(1)}, s32[2,17]{1,0:T(2,128)S(1)}, u32[]{:S(2)}, u32[]{:S(2)}) collective-permute-start(s32[2,17]{1,0:T(2,128)S(1)} %pad_add_fusion.lists), channel_id=1, source_target_pairs={{0,8},{8,0},{1,9},{9,1},{2,10},{10,2},{3,11},{11,3},{4,12},{12,4},... | collective-permute-start | bytes 416 | tf_op jit(solution)/shard_map/ppermute | solution.py:108
  77.5 6.3 %collective-permute-start.3 = (bf16[64,2,64,128]{3,2,1,0:T(8,128)(2,1)}, bf16[64,2,64,128]{3,2,1,0:T(8,128)(2,1)S(1)}, u32[]{:S(2)}, u32[]{:S(2)}) collective-permute-start(bf16[64,2,64,128]{3,2,1,0:T(8,128)(2,1)} %all-gather.2.cloned.1.call-done.even), channel_id=1, source_target_pairs={{0,1},{1,0},{2,3},{3,2},{4,5},{5,4},{6,7},{7,6},{8,9},{9,8},{10,11... | collective-permute-start | bytes 6291464 | tf_op jit(solution)/shard_map/ppermute | solution.py:108
  83.7 1.6 %copy-start = (bf16[64,2,64,128]{3,2,1,0:T(8,128)(2,1)S(1)}, bf16[64,2,64,128]{3,2,1,0:T(8,128)(2,1)}, u32[]{:S(2)}) copy-start(bf16[64,2,64,128]{3,2,1,0:T(8,128)(2,1)} %all-gather.2.cloned.1.call-done.even) | copy-start | bytes 6291460
Sparse Core Ops, SparseCore 0:
  49.2 28.2 all-gather.1

commit v4 on v3

--- a/solution.py
+++ b/solution.py
@@ -38,7 +38,7 @@
         for e in range(MAXB):
             j = jnp.where(mine, lists[inside, e], other_lists[inside, e])
             is_even = j % 2 == 0
-            even_row = (j // 4) % 4 * (even.shape[0] // 4) + j // 16 * 2 + (j // 2) % 2
+            even_row = j // 2
             odd_row = jnp.clip((j - 4 * pair + 1) // 2, 0, ODD - 1)
             for rc, (evens, odds) in enumerate(((even, odd), (other_even, other_odd))):
                 span = pl.ds(e * BLOCK_POSITIONS + rc * HALF, HALF)
@@ -113,24 +113,25 @@
     meta = jnp.stack([lax.axis_index(a) for a in (Z, X, YLO, CORE)]).astype(jnp.int32)
     heads = lax.axis_size(RING)
 
+    chips = lax.axis_size(X)
     sent = keyvals.reshape(2, STRIP, heads, HEAD_SIZE).transpose(2, 0, 1, 3)
-    local = lax.all_to_all(sent, RING, split_axis=0, concat_axis=0, tiled=True)
-    local = local.reshape(4, 2, 2, STRIP, HEAD_SIZE).transpose(0, 2, 1, 3, 4)
-    local = local.reshape(4, 2, HALF, HEAD_SIZE)
+    sent = jnp.broadcast_to(sent[None], (chips,) + sent.shape).reshape((chips * heads,) + sent.shape[1:])
+    plane = lax.all_to_all(sent, (X,) + RING, split_axis=0, concat_axis=0, tiled=True)
+    plane = plane.reshape(chips, 4, 2, 2, STRIP, HEAD_SIZE).transpose(0, 1, 3, 2, 4, 5)
+    plane = plane.reshape(chips, 4, 2, HALF, HEAD_SIZE)
+    mine = plane[:, 0::2].reshape(2 * chips, 2, HALF, HEAD_SIZE)
+    even = lax.all_gather(mine, Z, axis=0, tiled=True)
 
-    summary = jnp.stack([local[0], local[2]])
-    copies = jnp.broadcast_to(summary[None], (lax.axis_size(Z),) + summary.shape)
-    column = lax.all_to_all(copies, Z, split_axis=0, concat_axis=0, tiled=True)
-    column = column.reshape((-1,) + summary.shape[1:])
-    even = lax.all_gather(column, X, axis=0, tiled=True)
-
-    queries, local, lists = lax.optimization_barrier((queries, local, lists, column))[:3]
+    queries, plane, lists = lax.optimization_barrier((queries, plane, lists, mine))[:3]
     sent_q = queries.reshape(STRIP, heads, GROUP * HEAD_SIZE).transpose(1, 0, 2)
     q = lax.all_to_all(sent_q, RING, split_axis=0, concat_axis=0, tiled=True)
     other_lists = swap(lists, YLO)
-    pairs = lax.axis_size((Z, X))
-    before = lax.ppermute(local[3], (Z, X), [(i, i + 1) for i in range(pairs - 1)])
-    odd = jnp.stack([before, local[1], local[3]])
+    x = lax.axis_index(X)
+    layers = lax.axis_size(Z)
+    below = lax.ppermute(plane[chips - 1, 3], Z, [(i, i + 1) for i in range(layers - 1)])
+    left = lax.dynamic_index_in_dim(plane, jnp.maximum(x - 1, 0), 0, keepdims=False)[3]
+    own = lax.dynamic_index_in_dim(plane, x, 0, keepdims=False)
+    odd = jnp.stack([jnp.where(x == 0, below, left), own[1], own[3]])
     other_odd = swap(odd, CORE)
     even, q, other_lists, odd, other_odd = lax.optimization_barrier((even, q, other_lists, odd, other_odd))
 

time: 128 us -> 130 us (1.016)
  waiting for transfers between devices: 20.4 us -> 35.3 us
  blocking collectives: 64.7 us -> 49.9 us
  starting transfers between devices: 13.1 us -> 15.1 us
    all_to_all x2 -> x1, blocking collectives: 41.3 us -> 26.5 us  [body(): lax.all_to_all(sent, (X,) + RING, split_axis=0, concat_axis=0, tiled=True)]
    all_gather x1, waiting for transfers between devices: 10.7 us -> 23.9 us  [body(): even = lax.all_gather(mine, Z, axis=0, tiled=True)]
    all_to_all x1, waiting for transfers between devices: 0.01 us -> 2.08 us  [body(): q = lax.all_to_all(sent_q, RING, split_axis=0, concat_axis=0, tiled=True)]
  transfers between devices with their start and end apart: 6 -> 6, of which waited for: 4 -> 5; matrix products, arithmetic and copies ran while one was open for 1% -> 1% of each run, Pallas kernels for 0% -> 0%
where the time goes in v4:
time: 130 us; the launch traced here: 129 us
  blocking collectives  49.9 us (38%)
  waiting for transfers between devices  35.3 us (27%)
  starting transfers between devices  15.1 us (12%)
  between operations  13.5 us (10%)
  Pallas kernels  10.3 us (8%)
  local copies, waits for them, and re-layouts  5.22 us (4%)
    all_to_all x1, blocking collectives, body(): lax.all_to_all(sent, (X,) + RING, split_axis=0, concat_axis=0, tiled=True)  26.5 us
    all_gather x1, waiting for transfers between devices, body(): even = lax.all_gather(mine, Z, axis=0, tiled=True)  23.9 us
    all_to_all x1, blocking collectives, body(): lax.all_to_all(result, RING, split_axis=0, concat_axis=0, tiled=True)  23.4 us
    pallas_call x1, Pallas kernels, attention(): pl.pallas_call(attend, out_shape=jax.ShapeDtypeStruct(q.shape, q.dtype),...  10.3 us
    ppermute x3, waiting for transfers between devices, swap(): return lax.ppermute(array, axis, [(0, 1), (1, 0)])  7.79 us
    ppermute x3, starting transfers between devices, swap(): return lax.ppermute(array, axis, [(0, 1), (1, 0)])  5.75 us
    all_to_all x1, starting transfers between devices, body(): q = lax.all_to_all(sent_q, RING, split_axis=0, concat_axis=0, tiled=True)  5.11 us
    ppermute x1, starting transfers between devices, body(): lax.ppermute(plane[chips - 1, 3], Z, [(i, i + 1) for i in range(layers -...  4.28 us
  transfers between devices with their start and end apart: 6, of which 5 were waited for; matrix products, arithmetic and copies ran while one was open for 1% of the time, Pallas kernels for 0%

profile of v4, /device:TPU:8, one launch (start us, length us, event | category | flops | bytes accessed | tf_op | source)
XLA Modules:
  0.0 129.5 jit_solution(8069239021803046824)
XLA Ops:
  6.5 0.9 copy.19
  7.5 0.1 broadcast_in_dim.4
  7.7 26.5 %all_to_all.15 = bf16[32,2,32,128]{3,2,1,0:T(8,128)(2,1)S(1)} all-to-all(bf16[32,2,32,128]{3,2,1,0:T(8,128)(2,1)S(1)} %bitcast.43), channel_id=1, replica_groups=mesh['z'=8,'x'=4,'ylo'=2,'yhi'=4,'core'=2] {'x','ylo','yhi'}, dimensions={0} | all-to-all | bytes 1048576 | tf_op jit(solution)/shard_map/all_to_all | solution.py:119
  34.2 0.1 copy.13
  34.2 0.7 slice.22
  34.9 0.0 all-gather.2.cloned.1.call-update
  35.0 0.1 copy.14
  35.1 0.1 pad_add_fusion.lists
  35.1 0.8 copy.21
  36.0 5.1 %all-to-all-start.1 = ((bf16[8,32,1024]{2,1,0:T(8,128)(2,1)}), bf16[8,32,1024]{2,1,0:T(8,128)(2,1)S(1)}, u32[]{:S(2)}, u32[]{:S(2)}) async-start(bf16[8,32,1024]{2,1,0:T(8,128)(2,1)} %bitcast.41), calls=%async_computation.1 | async-start | bytes 1048576 | tf_op jit(solution)/shard_map/all_to_all | solution.py:127
  41.1 4.3 %collective-permute-start.1 = (bf16[2,64,128]{2,1,0:T(8,128)(2,1)S(1)}, bf16[2,64,128]{2,1,0:T(8,128)(2,1)S(1)}, u32[]{:S(2)}, u32[]{:S(2)}) collective-permute-start(bf16[2,64,128]{2,1,0:T(8,128)(2,1)S(1)} %get-tuple-element.21), channel_id=1, source_target_pairs={{0,64},{64,128},{128,192},{192,256},{256,320},{320,384},{384,448},... | collective-permute-start | bytes 98312 | tf_op jit(solution)/shard_map/ppermute | solution.py:131
  45.4 1.6 %collective-permute-done.1 = bf16[2,64,128]{2,1,0:T(8,128)(2,1)S(1)} collective-permute-done((bf16[2,64,128]{2,1,0:T(8,128)(2,1)S(1)}, bf16[2,64,128]{2,1,0:T(8,128)(2,1)S(1)}, u32[]{:S(2)}, u32[]{:S(2)}) %collective-permute-start.1) | collective-permute-done | bytes 32800 | tf_op jit(solution)/shard_map/ppermute | solution.py:131
  47.0 1.9 %collective-permute-start.2 = (bf16[3,2,64,128]{3,2,1,0:T(8,128)(2,1)S(1)}, bf16[3,2,64,128]{3,2,1,0:T(8,128)(2,1)S(1)}, u32[]{:S(2)}, u32[]{:S(2)}) collective-permute-start(bf16[3,2,64,128]{3,2,1,0:T(8,128)(2,1)S(1)} %pad_maximum_fusion.odd), channel_id=1, source_target_pairs={{0,1},{1,0},{2,3},{3,2},{4,5},{5,4},{6,7},{7,6},{8,9},{9,8},{10,11... | collective-permute-start | bytes 294920 | tf_op jit(solution)/shard_map/ppermute | solution.py:108
  48.9 1.9 %collective-permute-start = (s32[2,17]{1,0:T(2,128)S(1)}, s32[2,17]{1,0:T(2,128)S(1)}, u32[]{:S(2)}, u32[]{:S(2)}) collective-permute-start(s32[2,17]{1,0:T(2,128)S(1)} %pad_add_fusion.lists), channel_id=1, source_target_pairs={{0,8},{8,0},{1,9},{9,1},{2,10},{10,2},{3,11},{11,3},{4,12},{12,4},... | collective-permute-start | bytes 416 | tf_op jit(solution)/shard_map/ppermute | solution.py:108
  50.9 3.5 %collective-permute-done.other_lists = s32[2,17]{1,0:T(2,128)S(1)} collective-permute-done((s32[2,17]{1,0:T(2,128)S(1)}, s32[2,17]{1,0:T(2,128)S(1)}, u32[]{:S(2)}, u32[]{:S(2)}) %collective-permute-start) | collective-permute-done | bytes 168 | tf_op jit(solution)/shard_map/ppermute | solution.py:108
  54.4 2.1 %all-to-all-done.1.q_ref = bf16[8,32,1024]{2,1,0:T(8,128)(2,1)S(1)} async-done(((bf16[8,32,1024]{2,1,0:T(8,128)(2,1)}), bf16[8,32,1024]{2,1,0:T(8,128)(2,1)S(1)}, u32[]{:S(2)}, u32[]{:S(2)}) %all-to-all-start.1) | async-done | bytes 524320 | tf_op jit(solution)/shard_map/all_to_all | solution.py:127
  56.5 23.9 %all-gather.2.cloned.1.call-done.even = bf16[64,2,64,128]{3,2,1,0:T(8,128)(2,1)} async-done(((bf16[8,2,64,128]{3,2,1,0:T(8,128)(2,1)}), bf16[64,2,64,128]{3,2,1,0:T(8,128)(2,1)}) %all-gather.2.cloned.1.call-update) | async-done | bytes 2097168 | tf_op jit(solution)/shard_map/all_gather | solution.py:123
  80.3 1.9 %collective-permute-start.3 = (bf16[64,2,64,128]{3,2,1,0:T(8,128)(2,1)}, bf16[64,2,64,128]{3,2,1,0:T(8,128)(2,1)S(1)}, u32[]{:S(2)}, u32[]{:S(2)}) collective-permute-start(bf16[64,2,64,128]{3,2,1,0:T(8,128)(2,1)} %all-gather.2.cloned.1.call-done.even), channel_id=1, source_target_pairs={{0,1},{1,0},{2,3},{3,2},{4,5},{5,4},{6,7},{7,6},{8,9},{9,8},{10,11... | collective-permute-start | bytes 6291464 | tf_op jit(solution)/shard_map/ppermute | solution.py:108
  82.2 0.1 pad_add_fusion.1.meta
  82.3 4.3 %collective-permute-done.3.other_even = bf16[64,2,64,128]{3,2,1,0:T(8,128)(2,1)S(1)} collective-permute-done((bf16[64,2,64,128]{3,2,1,0:T(8,128)(2,1)}, bf16[64,2,64,128]{3,2,1,0:T(8,128)(2,1)S(1)}, u32[]{:S(2)}, u32[]{:S(2)}) %collective-permute-start.3) | collective-permute-done | bytes 2097184 | tf_op jit(solution)/shard_map/ppermute | solution.py:108
  86.6 1.6 %copy-done = bf16[64,2,64,128]{3,2,1,0:T(8,128)(2,1)S(1)} copy-done((bf16[64,2,64,128]{3,2,1,0:T(8,128)(2,1)S(1)}, bf16[64,2,64,128]{3,2,1,0:T(8,128)(2,1)}, u32[]{:S(2)}) %copy-start) | copy-done | bytes 2097176
  88.2 10.3 %shard_map.46 = bf16[8,32,1024]{2,1,0:T(8,128)(2,1)S(1)} custom-call(s32[4]{0:T(128)S(1)} %pad_add_fusion.1.meta, s32[2,17]{1,0:T(2,128)S(1)} %pad_add_fusion.lists, s32[2,17]{1,0:T(2,128)S(1)} %collective-permute-done.other_lists, bf16[8,32,1024]{2,1,0:T(8,128)(2,1)S(1)} %all-to-all-done.1.q_ref, bf16[64,2,64,128]{3,2,1,0:T(8,128)(2,1)S(1)} %copy-done, ...), custom_call_target="tpu_custom_call" | custom-call | flops 2147483648 | bytes 8388608 | tf_op jit(solution)/shard_map/pallas_call | solution.py:89
  98.4 23.4 %all_to_all.16 = bf16[8,32,1024]{2,1,0:T(8,128)(2,1)S(1)} all-to-all(bf16[8,32,1024]{2,1,0:T(8,128)(2,1)S(1)} %shard_map.46), channel_id=1, replica_groups=mesh['z'=8,'x'=4,'ylo'=2,'yhi'=4,'core'=2] {'ylo','yhi'}, dimensions={0} | all-to-all | bytes 1048576 | tf_op jit(solution)/shard_map/all_to_all | solution.py:139
  121.8 0.8 copy.18
  (14 shorter events, 0.1 us)
Async XLA Ops:
  6.5 73.8 %all-gather.2.cloned.1.call-start = ((), (), s32[]{:S(2)}) async-start(), calls=%async_computation.3 | async-start | bytes 2359296 | tf_op jit(solution)/shard_map/all_gather | solution.py:123
  7.5 27.5 %copy-start.3 = (s32[2]{0:T(128)S(1)}, s32[2]{0:T(128)}, u32[]{:S(2)}) copy-start(s32[2]{0:T(128)} %param.7) | copy-start | bytes 28
  7.5 27.6 %copy-start.2 = (s32[2,16]{1,0:T(2,128)S(1)}, s32[2,16]{1,0:T(2,128)}, u32[]{:S(2)}) copy-start(s32[2,16]{1,0:T(2,128)} %param.6) | copy-start | bytes 388
  7.5 27.7 %copy-start.1 = (bf16[32,8192]{1,0:T(8,128)(2,1)S(1)}, bf16[32,8192]{1,0:T(8,128)(2,1)}, u32[]{:S(2)}) copy-start(bf16[32,8192]{1,0:T(8,128)(2,1)} %param.4) | copy-start | bytes 1572868
  36.0 20.5 %all-to-all-start.1 = ((bf16[8,32,1024]{2,1,0:T(8,128)(2,1)}), bf16[8,32,1024]{2,1,0:T(8,128)(2,1)S(1)}, u32[]{:S(2)}, u32[]{:S(2)}) async-start(bf16[8,32,1024]{2,1,0:T(8,128)(2,1)} %bitcast.41), calls=%async_computation.1 | async-start | bytes 1048576 | tf_op jit(solution)/shard_map/all_to_all | solution.py:127
  41.1 5.9 %collective-permute-start.1 = (bf16[2,64,128]{2,1,0:T(8,128)(2,1)S(1)}, bf16[2,64,128]{2,1,0:T(8,128)(2,1)S(1)}, u32[]{:S(2)}, u32[]{:S(2)}) collective-permute-start(bf16[2,64,128]{2,1,0:T(8,128)(2,1)S(1)} %get-tuple-element.21), channel_id=1, source_target_pairs={{0,64},{64,128},{128,192},{192,256},{256,320},{320,384},{384,448},... | collective-permute-start | bytes 98312 | tf_op jit(solution)/shard_map/ppermute | solution.py:131
  47.0 7.4 %collective-permute-start.2 = (bf16[3,2,64,128]{3,2,1,0:T(8,128)(2,1)S(1)}, bf16[3,2,64,128]{3,2,1,0:T(8,128)(2,1)S(1)}, u32[]{:S(2)}, u32[]{:S(2)}) collective-permute-start(bf16[3,2,64,128]{3,2,1,0:T(8,128)(2,1)S(1)} %pad_maximum_fusion.odd), channel_id=1, source_target_pairs={{0,1},{1,0},{2,3},{3,2},{4,5},{5,4},{6,7},{7,6},{8,9},{9,8},{10,11... | collective-permute-start | bytes 294920 | tf_op jit(solution)/shard_map/ppermute | solution.py:108
  48.9 5.5 %collective-permute-start = (s32[2,17]{1,0:T(2,128)S(1)}, s32[2,17]{1,0:T(2,128)S(1)}, u32[]{:S(2)}, u32[]{:S(2)}) collective-permute-start(s32[2,17]{1,0:T(2,128)S(1)} %pad_add_fusion.lists), channel_id=1, source_target_pairs={{0,8},{8,0},{1,9},{9,1},{2,10},{10,2},{3,11},{11,3},{4,12},{12,4},... | collective-permute-start | bytes 416 | tf_op jit(solution)/shard_map/ppermute | solution.py:108
  80.3 6.3 %collective-permute-start.3 = (bf16[64,2,64,128]{3,2,1,0:T(8,128)(2,1)}, bf16[64,2,64,128]{3,2,1,0:T(8,128)(2,1)S(1)}, u32[]{:S(2)}, u32[]{:S(2)}) collective-permute-start(bf16[64,2,64,128]{3,2,1,0:T(8,128)(2,1)} %all-gather.2.cloned.1.call-done.even), channel_id=1, source_target_pairs={{0,1},{1,0},{2,3},{3,2},{4,5},{5,4},{6,7},{7,6},{8,9},{9,8},{10,11... | collective-permute-start | bytes 6291464 | tf_op jit(solution)/shard_map/ppermute | solution.py:108
  86.6 1.6 %copy-start = (bf16[64,2,64,128]{3,2,1,0:T(8,128)(2,1)S(1)}, bf16[64,2,64,128]{3,2,1,0:T(8,128)(2,1)}, u32[]{:S(2)}) copy-start(bf16[64,2,64,128]{3,2,1,0:T(8,128)(2,1)} %all-gather.2.cloned.1.call-done.even) | copy-start | bytes 6291460
Sparse Core Ops, SparseCore 0:
  35.1 45.1 all-gather.1

commit v5 on v1

v5 whole, which is shorter than its diff:
```python
import math

import jax
import jax.numpy as jnp
from jax import lax
from jax.experimental import pallas as pl
from jax.experimental.pallas import tpu as pltpu
from jax.sharding import Mesh, PartitionSpec as P

HEAD_SIZE = 128
BLOCK_POSITIONS = 128
MAXB = 16
KEYS = MAXB * BLOCK_POSITIONS
HALF = BLOCK_POSITIONS // 2
STRIP = 32
GROUP = 8
ROWS = GROUP * STRIP
ODD = 3
NEGATIVE = -1e30
FACTOR = math.log2(math.e) / math.sqrt(HEAD_SIZE)
Z, X, YLO, YHI, CORE = "z", "x", "ylo", "yhi", "core"
RING = (YLO, YHI)


def attend(core_ref, entries, q_ref, *refs):
    columns, odds = refs[:8], refs[8:10]
    out_ref, table, keys, values, scores, weights, sems = refs[10:]
    core = core_ref[0]
    evens = table.shape[1] - ODD
    per_column = evens // 4
    copies = []

    def bring(source, target):
        copy = pltpu.make_async_copy(source, target, sems.at[len(copies)])
        copy.start()
        copies.append(copy)

    for rc in range(2):
        side = jnp.bitwise_xor(core, rc)
        for source, relative in zip(columns[rc * 4 : rc * 4 + 4], (0, 3 - 2 * side, 1 + 2 * side, 2)):
            bring(source, table.at[rc, pl.ds(relative * per_column, per_column)])
        bring(odds[rc], table.at[rc, pl.ds(evens, ODD)])
    for copy in copies:
        copy.wait()

    cell = lax.broadcasted_iota(jnp.int32, (ROWS, BLOCK_POSITIONS), 1)
    row = lax.broadcasted_iota(jnp.int32, (ROWS, BLOCK_POSITIONS), 0)
    cell_core = jnp.bitwise_xor(cell // HALF, core)
    key_position = (cell % HALF) // STRIP * HALF + cell_core * STRIP + cell % STRIP
    ahead = key_position - core * STRIP - row % STRIP

    def one_block(b, carry):
        count = entries[b, MAXB]
        for e in range(MAXB):
            t = entries[b, e]
            for rc in range(2):
                span = pl.ds(e * BLOCK_POSITIONS + rc * HALF, HALF)
                keys[span, :] = table[rc, t, 0]
                values[span, :] = table[rc, t, 1]
        peaks = []
        for strip in range(2):
            q = jnp.concatenate(
                [q_ref[2 * b + strip, :, h * HEAD_SIZE : (h + 1) * HEAD_SIZE] for h in range(GROUP)], axis=0
            )
            peak = None
            for g in range(MAXB // 2):
                s = lax.dot_general(
                    q,
                    keys[g * 256 : (g + 1) * 256, :],
                    (((1,), (1,)), ((), ())),
                    preferred_element_type=jnp.float32,
                )
                for e in (2 * g, 2 * g + 1):
                    part = s[:, (e % 2) * 128 : (e % 2 + 1) * 128]
                    part = jnp.where(ahead <= strip * HALF if e == 0 else e < count, part, NEGATIVE)
                    scores[strip, e] = part
                    peak = part if peak is None else jnp.maximum(peak, part)
            peaks.append(jnp.max(peak, axis=1, keepdims=True) * FACTOR)
        for strip in range(2):
            total = jnp.zeros((ROWS, BLOCK_POSITIONS), jnp.float32)
            for e in range(MAXB):
                w = jnp.exp2(scores[strip, e] * FACTOR - peaks[strip])
                total = total + w
                weights[strip, :, e * 128 : (e + 1) * 128] = w.astype(jnp.bfloat16)
            numerator = jnp.dot(weights[strip], values[...], preferred_element_type=jnp.float32)
            result = (numerator / jnp.sum(total, axis=1, keepdims=True)).astype(jnp.bfloat16)
            for h in range(GROUP):
                out_ref[2 * b + strip, :, h * HEAD_SIZE : (h + 1) * HEAD_SIZE] = result[h * STRIP : (h + 1) * STRIP]
        return carry

    lax.fori_loop(0, 4, one_block, 0)


def attention(core, entries, q, columns, odds, interpret=False):
    evens = 4 * columns[0].shape[0]
    smem = pl.BlockSpec(memory_space=pltpu.SMEM)
    vmem = pl.BlockSpec(memory_space=pltpu.VMEM)
    hbm = pl.BlockSpec(memory_space=pl.ANY)
    return pl.pallas_call(
        attend,
        out_shape=jax.ShapeDtypeStruct(q.shape, q.dtype),
        in_specs=[smem, smem, vmem] + [hbm] * 10,
        out_specs=vmem,
        scratch_shapes=[
            pltpu.VMEM((2, evens + ODD, 2, HALF, HEAD_SIZE), jnp.bfloat16),
            pltpu.VMEM((KEYS, HEAD_SIZE), jnp.bfloat16),
            pltpu.VMEM((KEYS, HEAD_SIZE), jnp.bfloat16),
            pltpu.VMEM((2, MAXB, ROWS, BLOCK_POSITIONS), jnp.float32),
            pltpu.VMEM((2, ROWS, KEYS), jnp.bfloat16),
            pltpu.SemaphoreType.DMA((10,)),
        ],
        compiler_params=pltpu.CompilerParams(vmem_limit_bytes=40 * 2**20),
        cost_estimate=pl.CostEstimate(flops=2**31, bytes_accessed=8 * 2**20, transcendentals=2**22),
        interpret=interpret,
    )(core, entries, q, *columns, *odds)


def table_entries(z, x, ylo, lists, other_lists, evens):
    listed = jnp.where(ylo == 0, jnp.concatenate([lists, other_lists]), jnp.concatenate([other_lists, lists]))
    j = listed[:, :MAXB]
    relative = jnp.bitwise_and(j // 4 - x, 3)
    even_row = relative * (evens // 4) + j // 16 * 2 + (j // 2) % 2
    odd_row = evens + jnp.clip((j - 4 * (z * 4 + x) + 1) // 2, 0, ODD - 1)
    return jnp.concatenate([jnp.where(j % 2 == 0, even_row, odd_row), listed[:, MAXB:]], axis=1)


def swap(array, axis):
    return lax.ppermute(array, axis, [(0, 1), (1, 0)])


def around(array, axis, by):
    size = lax.axis_size(axis)
    pairs = [(2 * i + c, 2 * ((i + (by, -by)[c]) % size) + c) for i in range(size) for c in range(2)]
    return lax.ppermute(array, (axis, CORE), pairs)


def body(queries, keyvals, block_index, block_count):
    lists = jnp.concatenate([block_index, block_count[:, None]], axis=1)
    z, x, ylo, core = (lax.axis_index(a).astype(jnp.int32) for a in (Z, X, YLO, CORE))
    heads = lax.axis_size(RING)

    sent = keyvals.reshape(2, STRIP, heads, HEAD_SIZE).transpose(2, 0, 1, 3)
    local = lax.all_to_all(sent, RING, split_axis=0, concat_axis=0, tiled=True)
    local, queries = lax.optimization_barrier((local, queries))
    local = local.reshape(4, 2, 2, STRIP, HEAD_SIZE).transpose(0, 2, 1, 3, 4)
    local = local.reshape(4, 2, HALF, HEAD_SIZE)

    summary = jnp.stack([local[0], local[2]])
    copies = jnp.broadcast_to(summary[None], (lax.axis_size(Z),) + summary.shape)
    column = lax.all_to_all(copies, Z, split_axis=0, concat_axis=0, tiled=True)
    column = column.reshape((-1,) + summary.shape[1:])

    sent_q = queries.reshape(STRIP, heads, GROUP * HEAD_SIZE).transpose(1, 0, 2)
    q = lax.all_to_all(sent_q, RING, split_axis=0, concat_axis=0, tiled=True)
    entries = table_entries(z, x, ylo, lists, swap(lists, YLO), 4 * column.shape[0])
    pairs = lax.axis_size((Z, X))
    before = lax.ppermute(local[3], (Z, X), [(i, i + 1) for i in range(pairs - 1)])
    odd = jnp.stack([before, local[1], local[3]])
    other_odd = swap(odd, CORE)
    column, q, entries, odd, other_odd = lax.optimization_barrier((column, q, entries, odd, other_odd))

    first = around(column, X, 1)
    first, column = lax.optimization_barrier((first, column))
    far = around(first, X, 1)
    second = around(column, X, -1)
    columns = [column, first, second, far]
    columns += [swap(piece, CORE) for piece in columns]
    result = attention(core[None], entries, q, columns, [odd, other_odd])
    result = lax.all_to_all(result, RING, split_axis=0, concat_axis=0, tiled=True)
    return result.transpose(1, 0, 2).reshape(STRIP, heads * GROUP * HEAD_SIZE)


def solution(mesh):
    pb, kv, ha = mesh.devices.shape
    fine = Mesh(mesh.devices.reshape(pb, kv // 2, 2, ha // 2, 2), (Z, X, YLO, YHI, CORE))
    rows = (Z, X, YLO, YHI, CORE)
    shard = (Z, X, YLO)
    return jax.shard_map(
        body,
        mesh=fine,
        in_specs=(P(rows, None), P(None, rows, None), P(shard, None), P(shard)),
        out_specs=P(rows, None),
        check_vma=False,
    )
```

time: 129 us -> 136 us (1.054)
  the two profiles are of different devices: /device:TPU:8 before, /device:TPU:72 now
where the time goes in v5:
time: 136 us
  waiting for transfers between devices  42.6 us (31%)
  blocking collectives  39.4 us (29%)
  starting transfers between devices  37.7 us (28%)
  Pallas kernels  10.6 us (8%)
  local copies, waits for them, and re-layouts  4.96 us (4%)
    all_to_all x1, blocking collectives, body(): lax.all_to_all(result, RING, split_axis=0, concat_axis=0, tiled=True)  24.5 us
    ppermute x3, waiting for transfers between devices, around(): return lax.ppermute(array, (axis, CORE), pairs)  15.9 us
    all_to_all x1, blocking collectives, body(): local = lax.all_to_all(sent, RING, split_axis=0, concat_axis=0, tiled=True)  14.9 us
    all_to_all x1, waiting for transfers between devices, body(): column = lax.all_to_all(copies, Z, split_axis=0, concat_axis=0, tiled=True)  13.9 us
    ppermute x6, starting transfers between devices, swap(): return lax.ppermute(array, axis, [(0, 1), (1, 0)])  12.6 us
    pallas_call x1, Pallas kernels, attention(): pl.pallas_call(attend, out_shape=jax.ShapeDtypeStruct(q.shape, q.dtype),...  10.6 us
    all_to_all x1, starting transfers between devices, body(): column = lax.all_to_all(copies, Z, split_axis=0, concat_axis=0, tiled=True)  10.1 us
    ppermute x3, starting transfers between devices, around(): return lax.ppermute(array, (axis, CORE), pairs)  7.74 us
  transfers between devices with their start and end apart: 12, of which 7 were waited for; matrix products, arithmetic and copies ran while one was open for 1% of the time, Pallas kernels for 0%

profile of v5, /device:TPU:72, one launch (start us, length us, event | category | flops | bytes accessed | tf_op | source)
XLA Modules:
  0.0 135.8 jit_solution(9984602789499606534)
XLA Ops:
  0.0 0.9 copy.32
  1.0 14.9 %all_to_all.20 = bf16[8,2,32,128]{3,2,1,0:T(8,128)(2,1)S(1)} all-to-all(bf16[8,2,32,128]{3,2,1,0:T(8,128)(2,1)S(1)} %copy.21), channel_id=1, replica_groups=mesh['z'=8,'x'=4,'ylo'=2,'yhi'=4,'core'=2] {'ylo','yhi'}, dimensions={0} | all-to-all | bytes 262144 | tf_op jit(solution)/shard_map/all_to_all | solution.py:143
  15.9 0.9 broadcast_in_dim.13
  16.8 10.1 %all-to-all-start.1 = ((bf16[8,2,2,64,128]{4,3,2,1,0:T(8,128)(2,1)}), bf16[8,2,2,64,128]{4,3,2,1,0:T(8,128)(2,1)S(1)}, u32[]{:S(2)}, u32[]{:S(2)}) async-start(bf16[8,2,2,64,128]{4,3,2,1,0:T(8,128)(2,1)} %broadcast_in_dim.13), calls=%async_computation.1 | async-start | bytes 1048576 | tf_op jit(solution)/shard_map/all_to_all | solution.py:150
  27.8 13.9 %all-to-all-done.1 = bf16[8,2,2,64,128]{4,3,2,1,0:T(8,128)(2,1)S(1)} async-done(((bf16[8,2,2,64,128]{4,3,2,1,0:T(8,128)(2,1)}), bf16[8,2,2,64,128]{4,3,2,1,0:T(8,128)(2,1)S(1)}, u32[]{:S(2)}, u32[]{:S(2)}) %all-to-all-start.1) | async-done | bytes 524320 | tf_op jit(solution)/shard_map/all_to_all | solution.py:150
  41.7 3.9 %all-to-all-start.2 = ((bf16[8,32,1024]{2,1,0:T(8,128)(2,1)}), bf16[8,32,1024]{2,1,0:T(8,128)(2,1)S(1)}, u32[]{:S(2)}, u32[]{:S(2)}) async-start(bf16[8,32,1024]{2,1,0:T(8,128)(2,1)} %bitcast.28), calls=%async_computation.2 | async-start | bytes 1048576 | tf_op jit(solution)/shard_map/all_to_all | solution.py:154
  47.0 2.0 %collective-permute-start = (s32[2,17]{1,0:T(2,128)S(1)}, s32[2,17]{1,0:T(2,128)S(1)}, u32[]{:S(2)}, u32[]{:S(2)}) collective-permute-start(s32[2,17]{1,0:T(2,128)S(1)} %pad_add_fusion.1), channel_id=1, source_target_pairs={{0,8},{8,0},{1,9},{9,1},{2,10},{10,2},{3,11},{11,3},{4,12},{12,4},... | collective-permute-start | bytes 416 | tf_op jit(solution)/shard_map/ppermute | solution.py:128
  49.0 4.4 %collective-permute-done = s32[2,17]{1,0:T(2,128)S(1)} collective-permute-done((s32[2,17]{1,0:T(2,128)S(1)}, s32[2,17]{1,0:T(2,128)S(1)}, u32[]{:S(2)}, u32[]{:S(2)}) %collective-permute-start) | collective-permute-done | bytes 168 | tf_op jit(solution)/shard_map/ppermute | solution.py:128
  53.5 3.4 %collective-permute-start.1 = (bf16[2,64,128]{2,1,0:T(8,128)(2,1)S(1)}, bf16[2,64,128]{2,1,0:T(8,128)(2,1)S(1)}, u32[]{:S(2)}, u32[]{:S(2)}) collective-permute-start(bf16[2,64,128]{2,1,0:T(8,128)(2,1)S(1)} %bitcast.39), channel_id=1, source_target_pairs={{0,16},{16,32},{32,48},{48,64},{64,80},{80,96},{96,112},{112,128},... | collective-permute-start | bytes 98312 | tf_op jit(solution)/shard_map/ppermute | solution.py:157
  57.0 5.6 %collective-permute-done.1 = bf16[2,64,128]{2,1,0:T(8,128)(2,1)S(1)} collective-permute-done((bf16[2,64,128]{2,1,0:T(8,128)(2,1)S(1)}, bf16[2,64,128]{2,1,0:T(8,128)(2,1)S(1)}, u32[]{:S(2)}, u32[]{:S(2)}) %collective-permute-start.1) | collective-permute-done | bytes 32800 | tf_op jit(solution)/shard_map/ppermute | solution.py:157
  62.6 1.9 %collective-permute-start.2 = (bf16[3,2,64,128]{3,2,1,0:T(8,128)(2,1)S(1)}, bf16[3,2,64,128]{3,2,1,0:T(8,128)(2,1)S(1)}, u32[]{:S(2)}, u32[]{:S(2)}) collective-permute-start(bf16[3,2,64,128]{3,2,1,0:T(8,128)(2,1)S(1)} %pad_maximum_fusion.refs_8_), channel_id=1, source_target_pairs={{0,1},{1,0},{2,3},{3,2},{4,5},{5,4},{6,7},{7,6},{8,9},{9,8},{10,11... | collective-permute-start | bytes 294920 | tf_op jit(solution)/shard_map/ppermute | solution.py:128
  64.6 1.2 collective-permute-done.2.refs_9_
  65.8 1.9 %collective-permute-start.3 = (bf16[16,2,64,128]{3,2,1,0:T(8,128)(2,1)S(1)}, bf16[16,2,64,128]{3,2,1,0:T(8,128)(2,1)S(1)}, u32[]{:S(2)}, u32[]{:S(2)}) collective-permute-start(bf16[16,2,64,128]{3,2,1,0:T(8,128)(2,1)S(1)} %bitcast.30), channel_id=1, source_target_pairs={{0,16},{1,49},{16,32},{17,1},{32,48},{33,17},{48,0},{49,33},{2,18}... | collective-permute-start | bytes 1572872 | tf_op jit(solution)/shard_map/ppermute | solution.py:134
  67.7 10.4 %collective-permute-done.3.refs_1_ = bf16[16,2,64,128]{3,2,1,0:T(8,128)(2,1)S(1)} collective-permute-done((bf16[16,2,64,128]{3,2,1,0:T(8,128)(2,1)S(1)}, bf16[16,2,64,128]{3,2,1,0:T(8,128)(2,1)S(1)}, u32[]{:S(2)}, u32[]{:S(2)}) %collective-permute-start.3) | collective-permute-done | bytes 524320 | tf_op jit(solution)/shard_map/ppermute | solution.py:134
  78.1 1.9 %collective-permute-start.4 = (bf16[16,2,64,128]{3,2,1,0:T(8,128)(2,1)S(1)}, bf16[16,2,64,128]{3,2,1,0:T(8,128)(2,1)S(1)}, u32[]{:S(2)}, u32[]{:S(2)}) collective-permute-start(bf16[16,2,64,128]{3,2,1,0:T(8,128)(2,1)S(1)} %bitcast.31), channel_id=1, source_target_pairs={{0,48},{1,17},{16,0},{17,33},{32,16},{33,49},{48,32},{49,1},{2,50}... | collective-permute-start | bytes 1572872 | tf_op jit(solution)/shard_map/ppermute | solution.py:134
  80.0 3.9 %collective-permute-start.5 = (bf16[16,2,64,128]{3,2,1,0:T(8,128)(2,1)S(1)}, bf16[16,2,64,128]{3,2,1,0:T(8,128)(2,1)S(1)}, u32[]{:S(2)}, u32[]{:S(2)}) collective-permute-start(bf16[16,2,64,128]{3,2,1,0:T(8,128)(2,1)S(1)} %collective-permute-done.3.refs_1_), channel_id=1, source_target_pairs={{0,16},{1,49},{16,32},{17,1},{32,48},{33,17},{48,0},{49,33},{2,18}... | collective-permute-start | bytes 1572872 | tf_op jit(solution)/shard_map/ppermute | solution.py:134
  83.9 1.9 %collective-permute-start.6 = (bf16[16,2,64,128]{3,2,1,0:T(8,128)(2,1)S(1)}, bf16[16,2,64,128]{3,2,1,0:T(8,128)(2,1)S(1)}, u32[]{:S(2)}, u32[]{:S(2)}) collective-permute-start(bf16[16,2,64,128]{3,2,1,0:T(8,128)(2,1)S(1)} %bitcast.32), channel_id=1, source_target_pairs={{0,1},{1,0},{2,3},{3,2},{4,5},{5,4},{6,7},{7,6},{8,9},{9,8},{10,11... | collective-permute-start | bytes 1572872 | tf_op jit(solution)/shard_map/ppermute | solution.py:128
  85.8 2.4 %collective-permute-start.7 = (bf16[16,2,64,128]{3,2,1,0:T(8,128)(2,1)S(1)}, bf16[16,2,64,128]{3,2,1,0:T(8,128)(2,1)}, u32[]{:S(2)}, u32[]{:S(2)}) collective-permute-start(bf16[16,2,64,128]{3,2,1,0:T(8,128)(2,1)S(1)} %collective-permute-done.3.refs_1_), channel_id=1, source_target_pairs={{0,1},{1,0},{2,3},{3,2},{4,5},{5,4},{6,7},{7,6},{8,9},{9,8},{10,11... | collective-permute-start | bytes 1572872 | tf_op jit(solution)/shard_map/ppermute | solution.py:128
  88.2 5.5 %collective-permute-done.4.refs_2_ = bf16[16,2,64,128]{3,2,1,0:T(8,128)(2,1)S(1)} collective-permute-done((bf16[16,2,64,128]{3,2,1,0:T(8,128)(2,1)S(1)}, bf16[16,2,64,128]{3,2,1,0:T(8,128)(2,1)S(1)}, u32[]{:S(2)}, u32[]{:S(2)}) %collective-permute-start.4) | collective-permute-done | bytes 524320 | tf_op jit(solution)/shard_map/ppermute | solution.py:134
  93.8 1.9 %collective-permute-start.8 = (bf16[16,2,64,128]{3,2,1,0:T(8,128)(2,1)S(1)}, bf16[16,2,64,128]{3,2,1,0:T(8,128)(2,1)}, u32[]{:S(2)}, u32[]{:S(2)}) collective-permute-start(bf16[16,2,64,128]{3,2,1,0:T(8,128)(2,1)S(1)} %collective-permute-done.4.refs_2_), channel_id=1, source_target_pairs={{0,1},{1,0},{2,3},{3,2},{4,5},{5,4},{6,7},{7,6},{8,9},{9,8},{10,11... | collective-permute-start | bytes 1572872 | tf_op jit(solution)/shard_map/ppermute | solution.py:128
  95.7 2.4 %collective-permute-start.9 = (bf16[16,2,64,128]{3,2,1,0:T(8,128)(2,1)S(1)}, bf16[16,2,64,128]{3,2,1,0:T(8,128)(2,1)}, u32[]{:S(2)}, u32[]{:S(2)}) collective-permute-start(bf16[16,2,64,128]{3,2,1,0:T(8,128)(2,1)S(1)} %collective-permute-done.5.refs_3_), channel_id=1, source_target_pairs={{0,1},{1,0},{2,3},{3,2},{4,5},{5,4},{6,7},{7,6},{8,9},{9,8},{10,11... | collective-permute-start | bytes 1572872 | tf_op jit(solution)/shard_map/ppermute | solution.py:128
  98.2 1.6 %collective-permute-done.9.refs_7_ = bf16[16,2,64,128]{3,2,1,0:T(8,128)(2,1)} collective-permute-done((bf16[16,2,64,128]{3,2,1,0:T(8,128)(2,1)S(1)}, bf16[16,2,64,128]{3,2,1,0:T(8,128)(2,1)}, u32[]{:S(2)}, u32[]{:S(2)}) %collective-permute-start.9) | collective-permute-done | bytes 524320 | tf_op jit(solution)/shard_map/ppermute | solution.py:128
  99.8 10.6 %shard_map.46 = bf16[8,32,1024]{2,1,0:T(8,128)(2,1)S(1)} custom-call(s32[1]{0:T(128)} %bitcast.core_ref, s32[4,17]{1,0:T(4,128)S(1)} %pad_add_fusion.entries, bf16[8,32,1024]{2,1,0:T(8,128)(2,1)S(1)} %all-to-all-done.2.q_ref, bf16[16,2,64,128]{3,2,1,0:T(8,128)(2,1)S(1)} %bitcast.33, bf16[16,2,64,128]{3,2,1,0:T(8,128)(2,1)S(1)} %collective-permute-done.3.refs_1_, ...), custom_call_target="tpu_custom_call" | custom-call | flops 2147483648 | bytes 8388608 | tf_op jit(solution)/shard_map/pallas_call | solution.py:99
  110.4 24.5 %all_to_all.21 = bf16[8,32,1024]{2,1,0:T(8,128)(2,1)S(1)} all-to-all(bf16[8,32,1024]{2,1,0:T(8,128)(2,1)S(1)} %shard_map.46), channel_id=1, replica_groups=mesh['z'=8,'x'=4,'ylo'=2,'yhi'=4,'core'=2] {'ylo','yhi'}, dimensions={0} | all-to-all | bytes 1048576 | tf_op jit(solution)/shard_map/all_to_all | solution.py:169
  (28 shorter events, 3.4 us)
Async XLA Ops:
  16.8 10.1 %copy-start = (bf16[32,8192]{1,0:T(8,128)(2,1)S(1)}, bf16[32,8192]{1,0:T(8,128)(2,1)}, u32[]{:S(2)}) copy-start(bf16[32,8192]{1,0:T(8,128)(2,1)} %param.4) | copy-start | bytes 1572868
  16.8 24.8 %all-to-all-start.1 = ((bf16[8,2,2,64,128]{4,3,2,1,0:T(8,128)(2,1)}), bf16[8,2,2,64,128]{4,3,2,1,0:T(8,128)(2,1)S(1)}, u32[]{:S(2)}, u32[]{:S(2)}) async-start(bf16[8,2,2,64,128]{4,3,2,1,0:T(8,128)(2,1)} %broadcast_in_dim.13), calls=%async_computation.1 | async-start | bytes 1048576 | tf_op jit(solution)/shard_map/all_to_all | solution.py:150
  41.7 24.1 %all-to-all-start.2 = ((bf16[8,32,1024]{2,1,0:T(8,128)(2,1)}), bf16[8,32,1024]{2,1,0:T(8,128)(2,1)S(1)}, u32[]{:S(2)}, u32[]{:S(2)}) async-start(bf16[8,32,1024]{2,1,0:T(8,128)(2,1)} %bitcast.28), calls=%async_computation.2 | async-start | bytes 1048576 | tf_op jit(solution)/shard_map/all_to_all | solution.py:154
  45.6 0.7 copy-start.2
  46.3 0.7 copy-start.1
  47.0 6.4 %collective-permute-start = (s32[2,17]{1,0:T(2,128)S(1)}, s32[2,17]{1,0:T(2,128)S(1)}, u32[]{:S(2)}, u32[]{:S(2)}) collective-permute-start(s32[2,17]{1,0:T(2,128)S(1)} %pad_add_fusion.1), channel_id=1, source_target_pairs={{0,8},{8,0},{1,9},{9,1},{2,10},{10,2},{3,11},{11,3},{4,12},{12,4},... | collective-permute-start | bytes 416 | tf_op jit(solution)/shard_map/ppermute | solution.py:128
  53.5 9.1 %collective-permute-start.1 = (bf16[2,64,128]{2,1,0:T(8,128)(2,1)S(1)}, bf16[2,64,128]{2,1,0:T(8,128)(2,1)S(1)}, u32[]{:S(2)}, u32[]{:S(2)}) collective-permute-start(bf16[2,64,128]{2,1,0:T(8,128)(2,1)S(1)} %bitcast.39), channel_id=1, source_target_pairs={{0,16},{16,32},{32,48},{48,64},{64,80},{80,96},{96,112},{112,128},... | collective-permute-start | bytes 98312 | tf_op jit(solution)/shard_map/ppermute | solution.py:157
  62.6 3.2 %collective-permute-start.2 = (bf16[3,2,64,128]{3,2,1,0:T(8,128)(2,1)S(1)}, bf16[3,2,64,128]{3,2,1,0:T(8,128)(2,1)S(1)}, u32[]{:S(2)}, u32[]{:S(2)}) collective-permute-start(bf16[3,2,64,128]{3,2,1,0:T(8,128)(2,1)S(1)} %pad_maximum_fusion.refs_8_), channel_id=1, source_target_pairs={{0,1},{1,0},{2,3},{3,2},{4,5},{5,4},{6,7},{7,6},{8,9},{9,8},{10,11... | collective-permute-start | bytes 294920 | tf_op jit(solution)/shard_map/ppermute | solution.py:128
  65.8 12.3 %collective-permute-start.3 = (bf16[16,2,64,128]{3,2,1,0:T(8,128)(2,1)S(1)}, bf16[16,2,64,128]{3,2,1,0:T(8,128)(2,1)S(1)}, u32[]{:S(2)}, u32[]{:S(2)}) collective-permute-start(bf16[16,2,64,128]{3,2,1,0:T(8,128)(2,1)S(1)} %bitcast.30), channel_id=1, source_target_pairs={{0,16},{1,49},{16,32},{17,1},{32,48},{33,17},{48,0},{49,33},{2,18}... | collective-permute-start | bytes 1572872 | tf_op jit(solution)/shard_map/ppermute | solution.py:134
  78.1 15.7 %collective-permute-start.4 = (bf16[16,2,64,128]{3,2,1,0:T(8,128)(2,1)S(1)}, bf16[16,2,64,128]{3,2,1,0:T(8,128)(2,1)S(1)}, u32[]{:S(2)}, u32[]{:S(2)}) collective-permute-start(bf16[16,2,64,128]{3,2,1,0:T(8,128)(2,1)S(1)} %bitcast.31), channel_id=1, source_target_pairs={{0,48},{1,17},{16,0},{17,33},{32,16},{33,49},{48,32},{49,1},{2,50}... | collective-permute-start | bytes 1572872 | tf_op jit(solution)/shard_map/ppermute | solution.py:134
  80.0 15.7 %collective-permute-start.5 = (bf16[16,2,64,128]{3,2,1,0:T(8,128)(2,1)S(1)}, bf16[16,2,64,128]{3,2,1,0:T(8,128)(2,1)S(1)}, u32[]{:S(2)}, u32[]{:S(2)}) collective-permute-start(bf16[16,2,64,128]{3,2,1,0:T(8,128)(2,1)S(1)} %collective-permute-done.3.refs_1_), channel_id=1, source_target_pairs={{0,16},{1,49},{16,32},{17,1},{32,48},{33,17},{48,0},{49,33},{2,18}... | collective-permute-start | bytes 1572872 | tf_op jit(solution)/shard_map/ppermute | solution.py:134
  83.9 14.2 %collective-permute-start.6 = (bf16[16,2,64,128]{3,2,1,0:T(8,128)(2,1)S(1)}, bf16[16,2,64,128]{3,2,1,0:T(8,128)(2,1)S(1)}, u32[]{:S(2)}, u32[]{:S(2)}) collective-permute-start(bf16[16,2,64,128]{3,2,1,0:T(8,128)(2,1)S(1)} %bitcast.32), channel_id=1, source_target_pairs={{0,1},{1,0},{2,3},{3,2},{4,5},{5,4},{6,7},{7,6},{8,9},{9,8},{10,11... | collective-permute-start | bytes 1572872 | tf_op jit(solution)/shard_map/ppermute | solution.py:128
  85.8 12.3 %collective-permute-start.7 = (bf16[16,2,64,128]{3,2,1,0:T(8,128)(2,1)S(1)}, bf16[16,2,64,128]{3,2,1,0:T(8,128)(2,1)}, u32[]{:S(2)}, u32[]{:S(2)}) collective-permute-start(bf16[16,2,64,128]{3,2,1,0:T(8,128)(2,1)S(1)} %collective-permute-done.3.refs_1_), channel_id=1, source_target_pairs={{0,1},{1,0},{2,3},{3,2},{4,5},{5,4},{6,7},{7,6},{8,9},{9,8},{10,11... | collective-permute-start | bytes 1572872 | tf_op jit(solution)/shard_map/ppermute | solution.py:128
  93.8 4.4 %collective-permute-start.8 = (bf16[16,2,64,128]{3,2,1,0:T(8,128)(2,1)S(1)}, bf16[16,2,64,128]{3,2,1,0:T(8,128)(2,1)}, u32[]{:S(2)}, u32[]{:S(2)}) collective-permute-start(bf16[16,2,64,128]{3,2,1,0:T(8,128)(2,1)S(1)} %collective-permute-done.4.refs_2_), channel_id=1, source_target_pairs={{0,1},{1,0},{2,3},{3,2},{4,5},{5,4},{6,7},{7,6},{8,9},{9,8},{10,11... | collective-permute-start | bytes 1572872 | tf_op jit(solution)/shard_map/ppermute | solution.py:128
  95.7 4.1 %collective-permute-start.9 = (bf16[16,2,64,128]{3,2,1,0:T(8,128)(2,1)S(1)}, bf16[16,2,64,128]{3,2,1,0:T(8,128)(2,1)}, u32[]{:S(2)}, u32[]{:S(2)}) collective-permute-start(bf16[16,2,64,128]{3,2,1,0:T(8,128)(2,1)S(1)} %collective-permute-done.5.refs_3_), channel_id=1, source_target_pairs={{0,1},{1,0},{2,3},{3,2},{4,5},{5,4},{6,7},{7,6},{8,9},{9,8},{10,11... | collective-permute-start | bytes 1572872 | tf_op jit(solution)/shard_map/ppermute | solution.py:128

commit v6 on v5

v6 whole, which is shorter than its diff:
```python
import math

import jax
import jax.numpy as jnp
from jax import lax
from jax.experimental import pallas as pl
from jax.experimental.pallas import tpu as pltpu
from jax.sharding import Mesh, PartitionSpec as P

HEAD_SIZE = 128
BLOCK_POSITIONS = 128
MAXB = 16
KEYS = MAXB * BLOCK_POSITIONS
HALF = BLOCK_POSITIONS // 2
STRIP = 32
GROUP = 8
ROWS = GROUP * STRIP
ODD = 3
PLANE = 8
NEGATIVE = -1e30
FACTOR = math.log2(math.e) / math.sqrt(HEAD_SIZE)
Z, X, YLO, YHI, CORE = "z", "x", "ylo", "yhi", "core"
RING = (YLO, YHI)


def attend(place, entries, q_ref, *refs):
    own, odd, rings, swapped = refs[0], refs[1], refs[2:6], refs[6:10]
    out_ref, table, keys, values, scores, weights, sems = refs[10:]
    z, core = place[0], place[1]
    layers = 2 * len(rings)
    evens = layers * PLANE
    copies = []

    def bring(source, target):
        copy = pltpu.make_async_copy(source, target, sems.at[len(copies)])
        copy.start()
        copies.append(copy)

    for half in range(2):
        bring(own.at[half, pl.ds(0, PLANE)], table.at[half, pl.ds(z * PLANE, PLANE)])
        bring(odd.at[half], table.at[half, pl.ds(evens, ODD)])
        for side, pieces in enumerate((rings, swapped)):
            above = jnp.bitwise_xor(core, side)
            for k, piece in enumerate(pieces, 1):
                row = jnp.bitwise_and(z + (2 * above - 1) * k, layers - 1) * PLANE
                size = PLANE
                if k == len(rings):
                    row, size = row + above * (PLANE // 2), PLANE // 2
                bring(piece.at[half, pl.ds(0, size)], table.at[half, pl.ds(row, size)])
                if k == 1:
                    bring(piece.at[half, pl.ds(PLANE, 1)], table.at[half, pl.ds(evens + ODD + above, 1)])
    for copy in copies:
        copy.wait()

    cell = lax.broadcasted_iota(jnp.int32, (ROWS, BLOCK_POSITIONS), 1)
    row = lax.broadcasted_iota(jnp.int32, (ROWS, BLOCK_POSITIONS), 0)
    key_position = (cell % HALF) // STRIP * HALF + cell // HALF * STRIP + cell % STRIP
    ahead = key_position - core * STRIP - row % STRIP

    def one_block(b, carry):
        count = entries[b, MAXB]
        for e in range(MAXB):
            t = entries[b, e]
            for half in range(2):
                span = pl.ds(e * BLOCK_POSITIONS + half * HALF, HALF)
                keys[span, :] = table[half, t, 0]
                values[span, :] = table[half, t, 1]
        peaks = []
        for strip in range(2):
            q = jnp.concatenate(
                [q_ref[2 * b + strip, :, h * HEAD_SIZE : (h + 1) * HEAD_SIZE] for h in range(GROUP)], axis=0
            )
            peak = None
            for g in range(MAXB // 2):
                s = lax.dot_general(
                    q,
                    keys[g * 256 : (g + 1) * 256, :],
                    (((1,), (1,)), ((), ())),
                    preferred_element_type=jnp.float32,
                )
                for e in (2 * g, 2 * g + 1):
                    part = s[:, (e % 2) * 128 : (e % 2 + 1) * 128]
                    part = jnp.where(ahead <= strip * HALF if e == 0 else e < count, part, NEGATIVE)
                    scores[strip, e] = part
                    peak = part if peak is None else jnp.maximum(peak, part)
            peaks.append(jnp.max(peak, axis=1, keepdims=True) * FACTOR)
        for strip in range(2):
            total = jnp.zeros((ROWS, BLOCK_POSITIONS), jnp.float32)
            for e in range(MAXB):
                w = jnp.exp2(scores[strip, e] * FACTOR - peaks[strip])
                total = total + w
                weights[strip, :, e * 128 : (e + 1) * 128] = w.astype(jnp.bfloat16)
            numerator = jnp.dot(weights[strip], values[...], preferred_element_type=jnp.float32)
            result = (numerator / jnp.sum(total, axis=1, keepdims=True)).astype(jnp.bfloat16)
            for h in range(GROUP):
                out_ref[2 * b + strip, :, h * HEAD_SIZE : (h + 1) * HEAD_SIZE] = result[h * STRIP : (h + 1) * STRIP]
        return carry

    lax.fori_loop(0, 4, one_block, 0)


def attention(place, entries, q, own, odd, rings, swapped, interpret=False):
    evens = 2 * len(rings) * PLANE
    smem = pl.BlockSpec(memory_space=pltpu.SMEM)
    vmem = pl.BlockSpec(memory_space=pltpu.VMEM)
    hbm = pl.BlockSpec(memory_space=pl.ANY)
    return pl.pallas_call(
        attend,
        out_shape=jax.ShapeDtypeStruct(q.shape, q.dtype),
        in_specs=[smem, smem, vmem] + [hbm] * 10,
        out_specs=vmem,
        scratch_shapes=[
            pltpu.VMEM((2, evens + ODD + 2, 2, HALF, HEAD_SIZE), jnp.bfloat16),
            pltpu.VMEM((KEYS, HEAD_SIZE), jnp.bfloat16),
            pltpu.VMEM((KEYS, HEAD_SIZE), jnp.bfloat16),
            pltpu.VMEM((2, MAXB, ROWS, BLOCK_POSITIONS), jnp.float32),
            pltpu.VMEM((2, ROWS, KEYS), jnp.bfloat16),
            pltpu.SemaphoreType.DMA((24,)),
        ],
        compiler_params=pltpu.CompilerParams(vmem_limit_bytes=40 * 2**20),
        cost_estimate=pl.CostEstimate(flops=2**31, bytes_accessed=8 * 2**20, transcendentals=2**22),
        interpret=interpret,
    )(place, entries, q, own, odd, *rings, *swapped)


def table_entries(z, x, ylo, lists, other_lists, evens):
    listed = jnp.where(ylo == 0, jnp.concatenate([lists, other_lists]), jnp.concatenate([other_lists, lists]))
    j = listed[:, :MAXB]
    near = jnp.clip((j - 4 * (z * 4 + x) + 1) // 2, 0, ODD - 1)
    odd_row = evens + jnp.where((near == 0) & (x == 0), ODD, near)
    return jnp.concatenate([jnp.where(j % 2 == 0, j // 2, odd_row), listed[:, MAXB:]], axis=1)


def swap(array, axis):
    return lax.ppermute(array, axis, [(0, 1), (1, 0)])


def around(array, axis, by):
    size = lax.axis_size(axis)
    pairs = [(2 * i + c, 2 * ((i + (by, -by)[c]) % size) + c) for i in range(size) for c in range(2)]
    return lax.ppermute(array, (axis, CORE), pairs)


def body(queries, keyvals, block_index, block_count):
    lists = jnp.concatenate([block_index, block_count[:, None]], axis=1)
    z, x, ylo, core = (lax.axis_index(a).astype(jnp.int32) for a in (Z, X, YLO, CORE))
    heads, chips, layers = lax.axis_size(RING), lax.axis_size(X), lax.axis_size(Z)

    sent = keyvals.reshape(2, STRIP, heads, HEAD_SIZE).transpose(2, 0, 1, 3)
    sent = jnp.broadcast_to(sent[None], (chips,) + sent.shape).reshape((chips * heads,) + sent.shape[1:])
    plane = lax.all_to_all(sent, (X,) + RING, split_axis=0, concat_axis=0, tiled=True)
    plane, queries, lists = lax.optimization_barrier((plane, queries, lists))
    plane = plane.reshape(chips, 4, 2, 2, STRIP, HEAD_SIZE).transpose(0, 1, 3, 2, 4, 5)
    plane = plane.reshape(chips, 4, 2, HALF, HEAD_SIZE)

    mine = lax.dynamic_index_in_dim(plane, x, 0, keepdims=False)
    left = lax.dynamic_index_in_dim(plane, jnp.maximum(x - 1, 0), 0, keepdims=False)
    half = jnp.concatenate(
        [
            plane[:, 0::2].reshape(PLANE, 2, HALF, HEAD_SIZE),
            jnp.stack([plane[chips - 1, 3], left[3], mine[1], mine[3]]),
        ]
    )
    other = swap(half, CORE)
    low, high = jnp.where(core == 0, half, other), jnp.where(core == 0, other, half)
    own = jnp.stack([low[: PLANE + 1], high[: PLANE + 1]])
    odd = jnp.stack([low[PLANE + 1 :], high[PLANE + 1 :]])

    sent_q = queries.reshape(STRIP, heads, GROUP * HEAD_SIZE).transpose(1, 0, 2)
    q = lax.all_to_all(sent_q, RING, split_axis=0, concat_axis=0, tiled=True)
    entries = table_entries(z, x, ylo, lists, swap(lists, YLO), layers * PLANE)

    first = around(own, Z, 1)
    second = around(first[:, :PLANE], Z, 1)
    swapped = [swap(first, CORE)]
    second, swapped[0] = lax.optimization_barrier((second, swapped[0]))
    third = around(second, Z, 1)
    swapped.append(swap(second, CORE))
    third, swapped[1], q, entries = lax.optimization_barrier((third, swapped[1], q, entries))
    fourth = around(lax.dynamic_slice_in_dim(third, core * (PLANE // 2), PLANE // 2, 1), Z, 1)
    rings = [first, second, third, fourth]
    swapped += [swap(third, CORE), swap(fourth, CORE)]
    result = attention(jnp.stack([z, core]), entries, q, own, odd, rings, swapped)
    result = lax.all_to_all(result, RING, split_axis=0, concat_axis=0, tiled=True)
    return result.transpose(1, 0, 2).reshape(STRIP, heads * GROUP * HEAD_SIZE)


def solution(mesh):
    pb, kv, ha = mesh.devices.shape
    fine = Mesh(mesh.devices.reshape(pb, kv // 2, 2, ha // 2, 2), (Z, X, YLO, YHI, CORE))
    rows = (Z, X, YLO, YHI, CORE)
    shard = (Z, X, YLO)
    return jax.shard_map(
        body,
        mesh=fine,
        in_specs=(P(rows, None), P(None, rows, None), P(shard, None), P(shard)),
        out_specs=P(rows, None),
        check_vma=False,
    )
```

time: 136 us -> 128 us (0.941)
  the two profiles are of different devices: /device:TPU:72 before, /device:TPU:8 now
where the time goes in v6:
time: 128 us; the launch traced here: 127 us
  waiting for transfers between devices  49.1 us (38%)
  starting transfers between devices  37.7 us (29%)
  blocking collectives  21.2 us (17%)
  Pallas kernels  11.2 us (9%)
  local copies, waits for them, and re-layouts  7.07 us (6%)
    ppermute x4, waiting for transfers between devices, around(): return lax.ppermute(array, (axis, CORE), pairs)  27 us
    all_to_all x1, blocking collectives, body(): lax.all_to_all(result, RING, split_axis=0, concat_axis=0, tiled=True)  21.2 us
    all_to_all x1, waiting for transfers between devices, body(): lax.all_to_all(sent, (X,) + RING, split_axis=0, concat_axis=0, tiled=True)  15 us
    ppermute x6, starting transfers between devices, swap(): return lax.ppermute(array, axis, [(0, 1), (1, 0)])  12.3 us
    pallas_call x1, Pallas kernels, attention(): pl.pallas_call(attend, out_shape=jax.ShapeDtypeStruct(q.shape, q.dtype),...  11.2 us
    ppermute x4, starting transfers between devices, around(): return lax.ppermute(array, (axis, CORE), pairs)  10.2 us
    all_to_all x1, starting transfers between devices, body(): lax.all_to_all(sent, (X,) + RING, split_axis=0, concat_axis=0, tiled=True)  10.2 us
    ppermute x6, waiting for transfers between devices, swap(): return lax.ppermute(array, axis, [(0, 1), (1, 0)])  5.11 us
  transfers between devices with their start and end apart: 12, of which 9 were waited for; matrix products, arithmetic and copies ran while one was open for 2% of the time, Pallas kernels for 0%

profile of v6, /device:TPU:8, one launch (start us, length us, event | category | flops | bytes accessed | tf_op | source)
XLA Modules:
  0.0 127.0 jit_solution(144837986706820995)
XLA Ops:
  0.0 0.9 copy.14
  1.9 10.2 %all-to-all-start = ((bf16[32,2,32,128]{3,2,1,0:T(8,128)(2,1)}), bf16[32,2,32,128]{3,2,1,0:T(8,128)(2,1)S(1)}, u32[]{:S(2)}, u32[]{:S(2)}) async-start(bf16[32,2,32,128]{3,2,1,0:T(8,128)(2,1)} %bitcast.3), calls=%async_computation | async-start | bytes 1048576 | tf_op jit(solution)/shard_map/all_to_all | solution.py:151
  13.6 15.0 %all-to-all-done = bf16[32,2,32,128]{3,2,1,0:T(8,128)(2,1)S(1)} async-done(((bf16[32,2,32,128]{3,2,1,0:T(8,128)(2,1)}), bf16[32,2,32,128]{3,2,1,0:T(8,128)(2,1)S(1)}, u32[]{:S(2)}, u32[]{:S(2)}) %all-to-all-start) | async-done | bytes 524320 | tf_op jit(solution)/shard_map/all_to_all | solution.py:151
  28.8 1.9 %collective-permute-start = (bf16[12,2,64,128]{3,2,1,0:T(8,128)(2,1)S(1)}, bf16[12,2,64,128]{3,2,1,0:T(8,128)(2,1)S(1)}, u32[]{:S(2)}, u32[]{:S(2)}) collective-permute-start(bf16[12,2,64,128]{3,2,1,0:T(8,128)(2,1)S(1)} %fusion), channel_id=1, source_target_pairs={{0,1},{1,0},{2,3},{3,2},{4,5},{5,4},{6,7},{7,6},{8,9},{9,8},{10,11... | collective-permute-start | bytes 1179656 | tf_op jit(solution)/shard_map/ppermute | solution.py:135
  30.7 1.7 %collective-permute-done = bf16[12,2,64,128]{3,2,1,0:T(8,128)(2,1)S(1)} collective-permute-done((bf16[12,2,64,128]{3,2,1,0:T(8,128)(2,1)S(1)}, bf16[12,2,64,128]{3,2,1,0:T(8,128)(2,1)S(1)}, u32[]{:S(2)}, u32[]{:S(2)}) %collective-permute-start) | collective-permute-done | bytes 393248 | tf_op jit(solution)/shard_map/ppermute | solution.py:135
  33.4 4.4 %collective-permute-start.1 = (bf16[2,9,2,64,128]{4,3,2,1,0:T(8,128)(2,1)S(1)}, bf16[2,9,2,64,128]{4,3,2,1,0:T(8,128)(2,1)S(1)}, u32[]{:S(2)}, u32[]{:S(2)}) collective-permute-start(bf16[2,9,2,64,128]{4,3,2,1,0:T(8,128)(2,1)S(1)} %pad_maximum_fusion.refs_0_), channel_id=1, source_target_pairs={{0,64},{1,449},{64,128},{65,1},{128,192},{129,65},{192,256},{193,1... | collective-permute-start | bytes 1769480 | tf_op jit(solution)/shard_map/ppermute | solution.py:141
  37.8 14.5 %collective-permute-done.1.refs_2_ = bf16[2,9,2,64,128]{4,3,2,1,0:T(8,128)(2,1)S(1)} collective-permute-done((bf16[2,9,2,64,128]{4,3,2,1,0:T(8,128)(2,1)S(1)}, bf16[2,9,2,64,128]{4,3,2,1,0:T(8,128)(2,1)S(1)}, u32[]{:S(2)}, u32[]{:S(2)}) %collective-permute-start.1) | collective-permute-done | bytes 589856 | tf_op jit(solution)/shard_map/ppermute | solution.py:141
  52.4 1.9 %collective-permute-start.3 = (bf16[2,9,2,64,128]{4,3,2,1,0:T(8,128)(2,1)S(1)}, bf16[2,9,2,64,128]{4,3,2,1,0:T(8,128)(2,1)S(1)}, u32[]{:S(2)}, u32[]{:S(2)}) collective-permute-start(bf16[2,9,2,64,128]{4,3,2,1,0:T(8,128)(2,1)S(1)} %collective-permute-done.1.refs_2_), channel_id=1, source_target_pairs={{0,1},{1,0},{2,3},{3,2},{4,5},{5,4},{6,7},{7,6},{8,9},{9,8},{10,11... | collective-permute-start | bytes 1769480 | tf_op jit(solution)/shard_map/ppermute | solution.py:135
  54.3 1.9 %collective-permute-start.2 = (bf16[2,8,2,64,128]{4,3,2,1,0:T(8,128)(2,1)S(1)}, bf16[2,8,2,64,128]{4,3,2,1,0:T(8,128)(2,1)S(1)}, u32[]{:S(2)}, u32[]{:S(2)}) collective-permute-start(bf16[2,8,2,64,128]{4,3,2,1,0:T(8,128)(2,1)S(1)} %slice.63), channel_id=1, source_target_pairs={{0,64},{1,449},{64,128},{65,1},{128,192},{129,65},{192,256},{193,1... | collective-permute-start | bytes 1572872 | tf_op jit(solution)/shard_map/ppermute | solution.py:141
  57.1 5.1 %all-to-all-start.1 = ((bf16[8,32,1024]{2,1,0:T(8,128)(2,1)}), bf16[8,32,1024]{2,1,0:T(8,128)(2,1)S(1)}, u32[]{:S(2)}, u32[]{:S(2)}) async-start(bf16[8,32,1024]{2,1,0:T(8,128)(2,1)} %bitcast.49), calls=%async_computation.1 | async-start | bytes 1048576 | tf_op jit(solution)/shard_map/all_to_all | solution.py:170
  62.2 4.4 %collective-permute-done.2.refs_3_ = bf16[2,8,2,64,128]{4,3,2,1,0:T(8,128)(2,1)S(1)} collective-permute-done((bf16[2,8,2,64,128]{4,3,2,1,0:T(8,128)(2,1)S(1)}, bf16[2,8,2,64,128]{4,3,2,1,0:T(8,128)(2,1)S(1)}, u32[]{:S(2)}, u32[]{:S(2)}) %collective-permute-start.2) | collective-permute-done | bytes 524320 | tf_op jit(solution)/shard_map/ppermute | solution.py:141
  66.6 1.9 %collective-permute-start.5 = (bf16[2,8,2,64,128]{4,3,2,1,0:T(8,128)(2,1)S(1)}, bf16[2,8,2,64,128]{4,3,2,1,0:T(8,128)(2,1)}, u32[]{:S(2)}, u32[]{:S(2)}) collective-permute-start(bf16[2,8,2,64,128]{4,3,2,1,0:T(8,128)(2,1)S(1)} %collective-permute-done.2.refs_3_), channel_id=1, source_target_pairs={{0,1},{1,0},{2,3},{3,2},{4,5},{5,4},{6,7},{7,6},{8,9},{9,8},{10,11... | collective-permute-start | bytes 1572872 | tf_op jit(solution)/shard_map/ppermute | solution.py:135
  68.5 1.9 %collective-permute-start.4 = (bf16[2,8,2,64,128]{4,3,2,1,0:T(8,128)(2,1)S(1)}, bf16[2,8,2,64,128]{4,3,2,1,0:T(8,128)(2,1)S(1)}, u32[]{:S(2)}, u32[]{:S(2)}) collective-permute-start(bf16[2,8,2,64,128]{4,3,2,1,0:T(8,128)(2,1)S(1)} %collective-permute-done.2.refs_3_), channel_id=1, source_target_pairs={{0,64},{1,449},{64,128},{65,1},{128,192},{129,65},{192,256},{193,1... | collective-permute-start | bytes 1572872 | tf_op jit(solution)/shard_map/ppermute | solution.py:141
  70.5 2.6 %collective-permute-start.6 = (s32[2,17]{1,0:T(2,128)S(1)}, s32[2,17]{1,0:T(2,128)S(1)}, u32[]{:S(2)}, u32[]{:S(2)}) collective-permute-start(s32[2,17]{1,0:T(2,128)S(1)} %pad_add_fusion.1), channel_id=1, source_target_pairs={{0,8},{8,0},{1,9},{9,1},{2,10},{10,2},{3,11},{11,3},{4,12},{12,4},... | collective-permute-start | bytes 416 | tf_op jit(solution)/shard_map/ppermute | solution.py:135
  73.0 2.9 %collective-permute-done.6 = s32[2,17]{1,0:T(2,128)S(1)} collective-permute-done((s32[2,17]{1,0:T(2,128)S(1)}, s32[2,17]{1,0:T(2,128)S(1)}, u32[]{:S(2)}, u32[]{:S(2)}) %collective-permute-start.6) | collective-permute-done | bytes 168 | tf_op jit(solution)/shard_map/ppermute | solution.py:135
  76.1 2.0 %all-to-all-done.1.q_ref = bf16[8,32,1024]{2,1,0:T(8,128)(2,1)S(1)} async-done(((bf16[8,32,1024]{2,1,0:T(8,128)(2,1)}), bf16[8,32,1024]{2,1,0:T(8,128)(2,1)S(1)}, u32[]{:S(2)}, u32[]{:S(2)}) %all-to-all-start.1) | async-done | bytes 524320 | tf_op jit(solution)/shard_map/all_to_all | solution.py:170
  78.1 2.7 %collective-permute-done.4.refs_4_ = bf16[2,8,2,64,128]{4,3,2,1,0:T(8,128)(2,1)S(1)} collective-permute-done((bf16[2,8,2,64,128]{4,3,2,1,0:T(8,128)(2,1)S(1)}, bf16[2,8,2,64,128]{4,3,2,1,0:T(8,128)(2,1)S(1)}, u32[]{:S(2)}, u32[]{:S(2)}) %collective-permute-start.4) | collective-permute-done | bytes 524320 | tf_op jit(solution)/shard_map/ppermute | solution.py:141
  80.8 1.9 %collective-permute-start.7 = (bf16[2,4,2,64,128]{4,3,2,1,0:T(8,128)(2,1)S(1)}, bf16[2,4,2,64,128]{4,3,2,1,0:T(8,128)(2,1)S(1)}, u32[]{:S(2)}, u32[]{:S(2)}) collective-permute-start(bf16[2,4,2,64,128]{4,3,2,1,0:T(8,128)(2,1)S(1)} %constant_dynamic-slice_fusion), channel_id=1, source_target_pairs={{0,64},{1,449},{64,128},{65,1},{128,192},{129,65},{192,256},{193,1... | collective-permute-start | bytes 786440 | tf_op jit(solution)/shard_map/ppermute | solution.py:141
  82.8 2.1 %collective-permute-start.8 = (bf16[2,8,2,64,128]{4,3,2,1,0:T(8,128)(2,1)S(1)}, bf16[2,8,2,64,128]{4,3,2,1,0:T(8,128)(2,1)S(1)}, u32[]{:S(2)}, u32[]{:S(2)}) collective-permute-start(bf16[2,8,2,64,128]{4,3,2,1,0:T(8,128)(2,1)S(1)} %collective-permute-done.4.refs_4_), channel_id=1, source_target_pairs={{0,1},{1,0},{2,3},{3,2},{4,5},{5,4},{6,7},{7,6},{8,9},{9,8},{10,11... | collective-permute-start | bytes 1572872 | tf_op jit(solution)/shard_map/ppermute | solution.py:135
  84.9 5.4 %collective-permute-done.7.refs_5_ = bf16[2,4,2,64,128]{4,3,2,1,0:T(8,128)(2,1)S(1)} collective-permute-done((bf16[2,4,2,64,128]{4,3,2,1,0:T(8,128)(2,1)S(1)}, bf16[2,4,2,64,128]{4,3,2,1,0:T(8,128)(2,1)S(1)}, u32[]{:S(2)}, u32[]{:S(2)}) %collective-permute-start.7) | collective-permute-done | bytes 262176 | tf_op jit(solution)/shard_map/ppermute | solution.py:141
  90.3 1.9 %collective-permute-start.9 = (bf16[2,4,2,64,128]{4,3,2,1,0:T(8,128)(2,1)S(1)}, bf16[2,4,2,64,128]{4,3,2,1,0:T(8,128)(2,1)S(1)}, u32[]{:S(2)}, u32[]{:S(2)}) collective-permute-start(bf16[2,4,2,64,128]{4,3,2,1,0:T(8,128)(2,1)S(1)} %collective-permute-done.7.refs_5_), channel_id=1, source_target_pairs={{0,1},{1,0},{2,3},{3,2},{4,5},{5,4},{6,7},{7,6},{8,9},{9,8},{10,11... | collective-permute-start | bytes 786440 | tf_op jit(solution)/shard_map/ppermute | solution.py:135
  92.2 1.0 slice_bitcast_fusion.2
  93.7 11.2 %shard_map.46 = bf16[8,32,1024]{2,1,0:T(8,128)(2,1)S(1)} custom-call(s32[2]{0:T(128)S(1)} %pad_add_fusion.2.place, s32[4,17]{1,0:T(4,128)S(1)} %pad_add_fusion.entries, bf16[8,32,1024]{2,1,0:T(8,128)(2,1)S(1)} %all-to-all-done.1.q_ref, bf16[2,9,2,64,128]{4,3,2,1,0:T(8,128)(2,1)S(1)} %pad_maximum_fusion.refs_0_, ...), custom_call_target="tpu_custom_call" | custom-call | flops 2147483648 | bytes 8388608 | tf_op jit(solution)/shard_map/pallas_call | solution.py:107
  104.9 21.2 %all_to_all.15 = bf16[8,32,1024]{2,1,0:T(8,128)(2,1)S(1)} all-to-all(bf16[8,32,1024]{2,1,0:T(8,128)(2,1)S(1)} %shard_map.46), channel_id=1, replica_groups=mesh['z'=8,'x'=4,'ylo'=2,'yhi'=4,'core'=2] {'ylo','yhi'}, dimensions={0} | all-to-all | bytes 1048576 | tf_op jit(solution)/shard_map/all_to_all | solution.py:184
  (39 shorter events, 6.1 us)
Async XLA Ops:
  1.9 26.7 %all-to-all-start = ((bf16[32,2,32,128]{3,2,1,0:T(8,128)(2,1)}), bf16[32,2,32,128]{3,2,1,0:T(8,128)(2,1)S(1)}, u32[]{:S(2)}, u32[]{:S(2)}) async-start(bf16[32,2,32,128]{3,2,1,0:T(8,128)(2,1)} %bitcast.3), calls=%async_computation | async-start | bytes 1048576 | tf_op jit(solution)/shard_map/all_to_all | solution.py:151
  12.1 0.7 copy-start.4
  12.8 0.7 copy-start.3
  28.8 3.6 %collective-permute-start = (bf16[12,2,64,128]{3,2,1,0:T(8,128)(2,1)S(1)}, bf16[12,2,64,128]{3,2,1,0:T(8,128)(2,1)S(1)}, u32[]{:S(2)}, u32[]{:S(2)}) collective-permute-start(bf16[12,2,64,128]{3,2,1,0:T(8,128)(2,1)S(1)} %fusion), channel_id=1, source_target_pairs={{0,1},{1,0},{2,3},{3,2},{4,5},{5,4},{6,7},{7,6},{8,9},{9,8},{10,11... | collective-permute-start | bytes 1179656 | tf_op jit(solution)/shard_map/ppermute | solution.py:135
  32.5 0.8 copy-start
  32.5 0.9 copy-start.1
  33.4 22.8 %copy-start.2 = (bf16[32,8192]{1,0:T(8,128)(2,1)S(1)}, bf16[32,8192]{1,0:T(8,128)(2,1)}, u32[]{:S(2)}) copy-start(bf16[32,8192]{1,0:T(8,128)(2,1)} %param.4) | copy-start | bytes 1572868
  33.4 18.9 %collective-permute-start.1 = (bf16[2,9,2,64,128]{4,3,2,1,0:T(8,128)(2,1)S(1)}, bf16[2,9,2,64,128]{4,3,2,1,0:T(8,128)(2,1)S(1)}, u32[]{:S(2)}, u32[]{:S(2)}) collective-permute-start(bf16[2,9,2,64,128]{4,3,2,1,0:T(8,128)(2,1)S(1)} %pad_maximum_fusion.refs_0_), channel_id=1, source_target_pairs={{0,64},{1,449},{64,128},{65,1},{128,192},{129,65},{192,256},{193,1... | collective-permute-start | bytes 1769480 | tf_op jit(solution)/shard_map/ppermute | solution.py:141
  52.4 14.3 %collective-permute-start.3 = (bf16[2,9,2,64,128]{4,3,2,1,0:T(8,128)(2,1)S(1)}, bf16[2,9,2,64,128]{4,3,2,1,0:T(8,128)(2,1)S(1)}, u32[]{:S(2)}, u32[]{:S(2)}) collective-permute-start(bf16[2,9,2,64,128]{4,3,2,1,0:T(8,128)(2,1)S(1)} %collective-permute-done.1.refs_2_), channel_id=1, source_target_pairs={{0,1},{1,0},{2,3},{3,2},{4,5},{5,4},{6,7},{7,6},{8,9},{9,8},{10,11... | collective-permute-start | bytes 1769480 | tf_op jit(solution)/shard_map/ppermute | solution.py:135
  54.3 12.3 %collective-permute-start.2 = (bf16[2,8,2,64,128]{4,3,2,1,0:T(8,128)(2,1)S(1)}, bf16[2,8,2,64,128]{4,3,2,1,0:T(8,128)(2,1)S(1)}, u32[]{:S(2)}, u32[]{:S(2)}) collective-permute-start(bf16[2,8,2,64,128]{4,3,2,1,0:T(8,128)(2,1)S(1)} %slice.63), channel_id=1, source_target_pairs={{0,64},{1,449},{64,128},{65,1},{128,192},{129,65},{192,256},{193,1... | collective-permute-start | bytes 1572872 | tf_op jit(solution)/shard_map/ppermute | solution.py:141
  57.1 21.0 %all-to-all-start.1 = ((bf16[8,32,1024]{2,1,0:T(8,128)(2,1)}), bf16[8,32,1024]{2,1,0:T(8,128)(2,1)S(1)}, u32[]{:S(2)}, u32[]{:S(2)}) async-start(bf16[8,32,1024]{2,1,0:T(8,128)(2,1)} %bitcast.49), calls=%async_computation.1 | async-start | bytes 1048576 | tf_op jit(solution)/shard_map/all_to_all | solution.py:170
  66.6 11.5 %collective-permute-start.5 = (bf16[2,8,2,64,128]{4,3,2,1,0:T(8,128)(2,1)S(1)}, bf16[2,8,2,64,128]{4,3,2,1,0:T(8,128)(2,1)}, u32[]{:S(2)}, u32[]{:S(2)}) collective-permute-start(bf16[2,8,2,64,128]{4,3,2,1,0:T(8,128)(2,1)S(1)} %collective-permute-done.2.refs_3_), channel_id=1, source_target_pairs={{0,1},{1,0},{2,3},{3,2},{4,5},{5,4},{6,7},{7,6},{8,9},{9,8},{10,11... | collective-permute-start | bytes 1572872 | tf_op jit(solution)/shard_map/ppermute | solution.py:135
  68.5 12.3 %collective-permute-start.4 = (bf16[2,8,2,64,128]{4,3,2,1,0:T(8,128)(2,1)S(1)}, bf16[2,8,2,64,128]{4,3,2,1,0:T(8,128)(2,1)S(1)}, u32[]{:S(2)}, u32[]{:S(2)}) collective-permute-start(bf16[2,8,2,64,128]{4,3,2,1,0:T(8,128)(2,1)S(1)} %collective-permute-done.2.refs_3_), channel_id=1, source_target_pairs={{0,64},{1,449},{64,128},{65,1},{128,192},{129,65},{192,256},{193,1... | collective-permute-start | bytes 1572872 | tf_op jit(solution)/shard_map/ppermute | solution.py:141
  70.5 5.5 %collective-permute-start.6 = (s32[2,17]{1,0:T(2,128)S(1)}, s32[2,17]{1,0:T(2,128)S(1)}, u32[]{:S(2)}, u32[]{:S(2)}) collective-permute-start(s32[2,17]{1,0:T(2,128)S(1)} %pad_add_fusion.1), channel_id=1, source_target_pairs={{0,8},{8,0},{1,9},{9,1},{2,10},{10,2},{3,11},{11,3},{4,12},{12,4},... | collective-permute-start | bytes 416 | tf_op jit(solution)/shard_map/ppermute | solution.py:135
  80.8 9.5 %collective-permute-start.7 = (bf16[2,4,2,64,128]{4,3,2,1,0:T(8,128)(2,1)S(1)}, bf16[2,4,2,64,128]{4,3,2,1,0:T(8,128)(2,1)S(1)}, u32[]{:S(2)}, u32[]{:S(2)}) collective-permute-start(bf16[2,4,2,64,128]{4,3,2,1,0:T(8,128)(2,1)S(1)} %constant_dynamic-slice_fusion), channel_id=1, source_target_pairs={{0,64},{1,449},{64,128},{65,1},{128,192},{129,65},{192,256},{193,1... | collective-permute-start | bytes 786440 | tf_op jit(solution)/shard_map/ppermute | solution.py:141
  82.8 10.5 %collective-permute-start.8 = (bf16[2,8,2,64,128]{4,3,2,1,0:T(8,128)(2,1)S(1)}, bf16[2,8,2,64,128]{4,3,2,1,0:T(8,128)(2,1)S(1)}, u32[]{:S(2)}, u32[]{:S(2)}) collective-permute-start(bf16[2,8,2,64,128]{4,3,2,1,0:T(8,128)(2,1)S(1)} %collective-permute-done.4.refs_4_), channel_id=1, source_target_pairs={{0,1},{1,0},{2,3},{3,2},{4,5},{5,4},{6,7},{7,6},{8,9},{9,8},{10,11... | collective-permute-start | bytes 1572872 | tf_op jit(solution)/shard_map/ppermute | solution.py:135
  90.3 3.4 %collective-permute-start.9 = (bf16[2,4,2,64,128]{4,3,2,1,0:T(8,128)(2,1)S(1)}, bf16[2,4,2,64,128]{4,3,2,1,0:T(8,128)(2,1)S(1)}, u32[]{:S(2)}, u32[]{:S(2)}) collective-permute-start(bf16[2,4,2,64,128]{4,3,2,1,0:T(8,128)(2,1)S(1)} %collective-permute-done.7.refs_5_), channel_id=1, source_target_pairs={{0,1},{1,0},{2,3},{3,2},{4,5},{5,4},{6,7},{7,6},{8,9},{9,8},{10,11... | collective-permute-start | bytes 786440 | tf_op jit(solution)/shard_map/ppermute | solution.py:135

commit v7 on v5

--- a/solution.py
+++ b/solution.py
@@ -23,8 +23,8 @@
 
 
 def attend(core_ref, entries, q_ref, *refs):
-    columns, odds = refs[:8], refs[8:10]
-    out_ref, table, keys, values, scores, weights, sems = refs[10:]
+    columns = refs[:8]
+    out_ref, table, keys, values, scores, weights, sems = refs[8:]
     core = core_ref[0]
     evens = table.shape[1] - ODD
     per_column = evens // 4
@@ -38,8 +38,8 @@
     for rc in range(2):
         side = jnp.bitwise_xor(core, rc)
         for source, relative in zip(columns[rc * 4 : rc * 4 + 4], (0, 3 - 2 * side, 1 + 2 * side, 2)):
-            bring(source, table.at[rc, pl.ds(relative * per_column, per_column)])
-        bring(odds[rc], table.at[rc, pl.ds(evens, ODD)])
+            bring(source.at[pl.ds(0, per_column)], table.at[rc, pl.ds(relative * per_column, per_column)])
+        bring(columns[rc * 4].at[pl.ds(per_column, ODD)], table.at[rc, pl.ds(evens, ODD)])
     for copy in copies:
         copy.wait()
 
@@ -91,15 +91,15 @@
     lax.fori_loop(0, 4, one_block, 0)
 
 
-def attention(core, entries, q, columns, odds, interpret=False):
-    evens = 4 * columns[0].shape[0]
+def attention(core, entries, q, columns, interpret=False):
+    evens = 4 * columns[1].shape[0]
     smem = pl.BlockSpec(memory_space=pltpu.SMEM)
     vmem = pl.BlockSpec(memory_space=pltpu.VMEM)
     hbm = pl.BlockSpec(memory_space=pl.ANY)
     return pl.pallas_call(
         attend,
         out_shape=jax.ShapeDtypeStruct(q.shape, q.dtype),
-        in_specs=[smem, smem, vmem] + [hbm] * 10,
+        in_specs=[smem, smem, vmem] + [hbm] * 8,
         out_specs=vmem,
         scratch_shapes=[
             pltpu.VMEM((2, evens + ODD, 2, HALF, HEAD_SIZE), jnp.bfloat16),
@@ -112,11 +112,10 @@
         compiler_params=pltpu.CompilerParams(vmem_limit_bytes=40 * 2**20),
         cost_estimate=pl.CostEstimate(flops=2**31, bytes_accessed=8 * 2**20, transcendentals=2**22),
         interpret=interpret,
-    )(core, entries, q, *columns, *odds)
+    )(core, entries, q, *columns)
 
 
-def table_entries(z, x, ylo, lists, other_lists, evens):
-    listed = jnp.where(ylo == 0, jnp.concatenate([lists, other_lists]), jnp.concatenate([other_lists, lists]))
+def table_entries(z, x, listed, evens):
     j = listed[:, :MAXB]
     relative = jnp.bitwise_and(j // 4 - x, 3)
     even_row = relative * (evens // 4) + j // 16 * 2 + (j // 2) % 2
@@ -135,37 +134,42 @@
 
 
 def body(queries, keyvals, block_index, block_count):
-    lists = jnp.concatenate([block_index, block_count[:, None]], axis=1)
-    z, x, ylo, core = (lax.axis_index(a).astype(jnp.int32) for a in (Z, X, YLO, CORE))
+    z, x, core = (lax.axis_index(a).astype(jnp.int32) for a in (Z, X, CORE))
     heads = lax.axis_size(RING)
 
-    sent = keyvals.reshape(2, STRIP, heads, HEAD_SIZE).transpose(2, 0, 1, 3)
-    local = lax.all_to_all(sent, RING, split_axis=0, concat_axis=0, tiled=True)
-    local, queries = lax.optimization_barrier((local, queries))
-    local = local.reshape(4, 2, 2, STRIP, HEAD_SIZE).transpose(0, 2, 1, 3, 4)
+    lists = jnp.concatenate([block_index, block_count[:, None]], axis=1).reshape(1, -1).astype(jnp.bfloat16)
+    lists = jnp.pad(lists, ((0, 15), (0, HEAD_SIZE - lists.shape[1])))
+    sent = keyvals.reshape(2 * STRIP, heads, HEAD_SIZE).transpose(1, 0, 2)
+    sent = jnp.concatenate([sent, jnp.broadcast_to(lists[None], (heads,) + lists.shape)], axis=1)
+    received = lax.all_to_all(sent, RING, split_axis=0, concat_axis=0, tiled=True)
+    local = received[:, : 2 * STRIP].reshape(4, 2, 2, STRIP, HEAD_SIZE).transpose(0, 2, 1, 3, 4)
     local = local.reshape(4, 2, HALF, HEAD_SIZE)
 
     summary = jnp.stack([local[0], local[2]])
     copies = jnp.broadcast_to(summary[None], (lax.axis_size(Z),) + summary.shape)
     column = lax.all_to_all(copies, Z, split_axis=0, concat_axis=0, tiled=True)
     column = column.reshape((-1,) + summary.shape[1:])
+    column, queries, odd = lax.optimization_barrier((column, queries, local[1::2]))
 
+    first = around(column, X, 1)
     sent_q = queries.reshape(STRIP, heads, GROUP * HEAD_SIZE).transpose(1, 0, 2)
     q = lax.all_to_all(sent_q, RING, split_axis=0, concat_axis=0, tiled=True)
-    entries = table_entries(z, x, ylo, lists, swap(lists, YLO), 4 * column.shape[0])
     pairs = lax.axis_size((Z, X))
-    before = lax.ppermute(local[3], (Z, X), [(i, i + 1) for i in range(pairs - 1)])
-    odd = jnp.stack([before, local[1], local[3]])
-    other_odd = swap(odd, CORE)
-    column, q, entries, odd, other_odd = lax.optimization_barrier((column, q, entries, odd, other_odd))
+    before = lax.ppermute(odd[1], (Z, X), [(i, i + 1) for i in range(pairs - 1)])
+    first, column, before = lax.optimization_barrier((first, column, before))
 
-    first = around(column, X, 1)
-    first, column = lax.optimization_barrier((first, column))
     far = around(first, X, 1)
     second = around(column, X, -1)
-    columns = [column, first, second, far]
-    columns += [swap(piece, CORE) for piece in columns]
-    result = attention(core[None], entries, q, columns, [odd, other_odd])
+    own = jnp.concatenate([column, before[None], odd])
+    own_swapped = swap(own, CORE)
+    first_swapped = swap(first, CORE)
+    listed = received[:: heads // 2, 2 * STRIP, : 2 * MAXB + 2].astype(jnp.int32).reshape(4, MAXB + 1)
+    entries = table_entries(z, x, listed, 4 * column.shape[0])
+    second, q, entries, own_swapped, first_swapped = lax.optimization_barrier(
+        (second, q, entries, own_swapped, first_swapped)
+    )
+    columns = [own, first, second, far, own_swapped, first_swapped, swap(second, CORE), swap(far, CORE)]
+    result = attention(core[None], entries, q, columns)
     result = lax.all_to_all(result, RING, split_axis=0, concat_axis=0, tiled=True)
     return result.transpose(1, 0, 2).reshape(STRIP, heads * GROUP * HEAD_SIZE)
 

time: 136 us -> 119 us (0.88)
  waiting for transfers between devices: 42.6 us -> 27.6 us
  starting transfers between devices: 37.7 us -> 36 us
    ppermute x3, waiting for transfers between devices: 15.9 us -> 6.89 us  [around(): return lax.ppermute(array, (axis, CORE), pairs)]
    ppermute x6 -> x4, waiting for transfers between devices: 7.2 us -> 1.64 us  [swap(): return lax.ppermute(array, axis, [(0, 1), (1, 0)])]
    ppermute x6 -> x4, starting transfers between devices: 12.6 us -> 8.16 us  [swap(): return lax.ppermute(array, axis, [(0, 1), (1, 0)])]
    ppermute x3, starting transfers between devices: 7.74 us -> 10.4 us  [around(): return lax.ppermute(array, (axis, CORE), pairs)]
  transfers between devices with their start and end apart: 12 -> 10, of which waited for: 7 -> 4; matrix products, arithmetic and copies ran while one was open for 1% -> 1% of each run, Pallas kernels for 0% -> 0%
where the time goes in v7:
time: 119 us
  blocking collectives  39.2 us (33%)
  starting transfers between devices  36 us (30%)
  waiting for transfers between devices  27.6 us (23%)
  Pallas kernels  10.6 us (9%)
  local copies, waits for them, and re-layouts  3.94 us (3%)
    all_to_all x1, blocking collectives, body(): lax.all_to_all(result, RING, split_axis=0, concat_axis=0, tiled=True)  23.6 us
    all_to_all x1, blocking collectives, body(): lax.all_to_all(sent, RING, split_axis=0, concat_axis=0, tiled=True)  15.7 us
    all_to_all x1, waiting for transfers between devices, body(): column = lax.all_to_all(copies, Z, split_axis=0, concat_axis=0, tiled=True)  14.6 us
    pallas_call x1, Pallas kernels, attention(): pl.pallas_call(attend, out_shape=jax.ShapeDtypeStruct(q.shape, q.dtype),...  10.6 us
    ppermute x3, starting transfers between devices, around(): return lax.ppermute(array, (axis, CORE), pairs)  10.4 us
    all_to_all x1, starting transfers between devices, body(): column = lax.all_to_all(copies, Z, split_axis=0, concat_axis=0, tiled=True)  10.1 us
    ppermute x4, starting transfers between devices, swap(): return lax.ppermute(array, axis, [(0, 1), (1, 0)])  8.16 us
    ppermute x3, waiting for transfers between devices, around(): return lax.ppermute(array, (axis, CORE), pairs)  6.89 us
  transfers between devices with their start and end apart: 10, of which 4 were waited for; matrix products, arithmetic and copies ran while one was open for 1% of the time, Pallas kernels for 0%

profile of v7, /device:TPU:72, one launch (start us, length us, event | category | flops | bytes accessed | tf_op | source)
XLA Modules:
  0.0 118.6 jit_solution(4101704388065576624)
XLA Ops:
  0.0 0.7 convert.8
  0.7 0.1 copy.15
  0.9 0.1 convert_element_type.21
  1.0 0.9 copy.22
  2.0 15.7 %all_to_all.20 = bf16[8,80,128]{2,1,0:T(8,128)(2,1)S(1)} all-to-all(bf16[8,80,128]{2,1,0:T(8,128)(2,1)S(1)} %copy.16), channel_id=1, replica_groups=mesh['z'=8,'x'=4,'ylo'=2,'yhi'=4,'core'=2] {'ylo','yhi'}, dimensions={0} | all-to-all | bytes 327680 | tf_op jit(solution)/shard_map/all_to_all | solution.py:144
  17.7 0.9 broadcast_in_dim.25
  18.6 10.1 %all-to-all-start.1 = ((bf16[8,2,2,64,128]{4,3,2,1,0:T(8,128)(2,1)}), bf16[8,2,2,64,128]{4,3,2,1,0:T(8,128)(2,1)S(1)}, u32[]{:S(2)}, u32[]{:S(2)}) async-start(bf16[8,2,2,64,128]{4,3,2,1,0:T(8,128)(2,1)} %broadcast_in_dim.25), calls=%async_computation.1 | async-start | bytes 1048576 | tf_op jit(solution)/shard_map/all_to_all | solution.py:150
  28.7 14.6 %all-to-all-done.1 = bf16[8,2,2,64,128]{4,3,2,1,0:T(8,128)(2,1)S(1)} async-done(((bf16[8,2,2,64,128]{4,3,2,1,0:T(8,128)(2,1)}), bf16[8,2,2,64,128]{4,3,2,1,0:T(8,128)(2,1)S(1)}, u32[]{:S(2)}, u32[]{:S(2)}) %all-to-all-start.1) | async-done | bytes 524320 | tf_op jit(solution)/shard_map/all_to_all | solution.py:150
  43.3 3.4 %collective-permute-start = (bf16[16,2,64,128]{3,2,1,0:T(8,128)(2,1)S(1)}, bf16[16,2,64,128]{3,2,1,0:T(8,128)(2,1)S(1)}, u32[]{:S(2)}, u32[]{:S(2)}) collective-permute-start(bf16[16,2,64,128]{3,2,1,0:T(8,128)(2,1)S(1)} %bitcast.29), channel_id=1, source_target_pairs={{0,16},{1,49},{16,32},{17,1},{32,48},{33,17},{48,0},{49,33},{2,18}... | collective-permute-start | bytes 1572872 | tf_op jit(solution)/shard_map/ppermute | solution.py:133
  46.7 0.8 copy.26
  47.5 3.9 %all-to-all-start.2 = ((bf16[8,32,1024]{2,1,0:T(8,128)(2,1)}), bf16[8,32,1024]{2,1,0:T(8,128)(2,1)S(1)}, u32[]{:S(2)}, u32[]{:S(2)}) async-start(bf16[8,32,1024]{2,1,0:T(8,128)(2,1)} %bitcast.28), calls=%async_computation.2 | async-start | bytes 1048576 | tf_op jit(solution)/shard_map/all_to_all | solution.py:156
  51.4 3.4 %collective-permute-start.1 = (bf16[2,64,128]{2,1,0:T(8,128)(2,1)S(1)}, bf16[2,64,128]{2,1,0:T(8,128)(2,1)S(1)}, u32[]{:S(2)}, u32[]{:S(2)}) collective-permute-start(bf16[2,64,128]{2,1,0:T(8,128)(2,1)S(1)} %slice_bitcast_fusion), channel_id=1, source_target_pairs={{0,16},{16,32},{32,48},{48,64},{64,80},{80,96},{96,112},{112,128},... | collective-permute-start | bytes 98312 | tf_op jit(solution)/shard_map/ppermute | solution.py:158
  54.8 4.5 %collective-permute-done.1 = bf16[2,64,128]{2,1,0:T(8,128)(2,1)S(1)} collective-permute-done((bf16[2,64,128]{2,1,0:T(8,128)(2,1)S(1)}, bf16[2,64,128]{2,1,0:T(8,128)(2,1)S(1)}, u32[]{:S(2)}, u32[]{:S(2)}) %collective-permute-start.1) | collective-permute-done | bytes 32800 | tf_op jit(solution)/shard_map/ppermute | solution.py:158
  59.4 1.9 %collective-permute-start.3 = (bf16[19,2,64,128]{3,2,1,0:T(8,128)(2,1)S(1)}, bf16[19,2,64,128]{3,2,1,0:T(8,128)(2,1)S(1)}, u32[]{:S(2)}, u32[]{:S(2)}) collective-permute-start(bf16[19,2,64,128]{3,2,1,0:T(8,128)(2,1)S(1)} %pad_maximum_fusion.refs_0_), channel_id=1, source_target_pairs={{0,1},{1,0},{2,3},{3,2},{4,5},{5,4},{6,7},{7,6},{8,9},{9,8},{10,11... | collective-permute-start | bytes 1867784 | tf_op jit(solution)/shard_map/ppermute | solution.py:127
  61.4 1.9 %collective-permute-start.5 = (bf16[16,2,64,128]{3,2,1,0:T(8,128)(2,1)S(1)}, bf16[16,2,64,128]{3,2,1,0:T(8,128)(2,1)S(1)}, u32[]{:S(2)}, u32[]{:S(2)}) collective-permute-start(bf16[16,2,64,128]{3,2,1,0:T(8,128)(2,1)S(1)} %collective-permute-done.refs_1_), channel_id=1, source_target_pairs={{0,16},{1,49},{16,32},{17,1},{32,48},{33,17},{48,0},{49,33},{2,18}... | collective-permute-start | bytes 1572872 | tf_op jit(solution)/shard_map/ppermute | solution.py:133
  63.3 5.1 %collective-permute-start.2 = (bf16[16,2,64,128]{3,2,1,0:T(8,128)(2,1)}, bf16[16,2,64,128]{3,2,1,0:T(8,128)(2,1)S(1)}, u32[]{:S(2)}, u32[]{:S(2)}) collective-permute-start(bf16[16,2,64,128]{3,2,1,0:T(8,128)(2,1)} %bitcast.31), channel_id=1, source_target_pairs={{0,48},{1,17},{16,0},{17,33},{32,16},{33,49},{48,32},{49,1},{2,50}... | collective-permute-start | bytes 1572872 | tf_op jit(solution)/shard_map/ppermute | solution.py:133
  68.4 1.9 %collective-permute-start.4 = (bf16[16,2,64,128]{3,2,1,0:T(8,128)(2,1)S(1)}, bf16[16,2,64,128]{3,2,1,0:T(8,128)(2,1)}, u32[]{:S(2)}, u32[]{:S(2)}) collective-permute-start(bf16[16,2,64,128]{3,2,1,0:T(8,128)(2,1)S(1)} %collective-permute-done.refs_1_), channel_id=1, source_target_pairs={{0,1},{1,0},{2,3},{3,2},{4,5},{5,4},{6,7},{7,6},{8,9},{9,8},{10,11... | collective-permute-start | bytes 1572872 | tf_op jit(solution)/shard_map/ppermute | solution.py:127
  70.6 6.9 %collective-permute-done.5.refs_3_ = bf16[16,2,64,128]{3,2,1,0:T(8,128)(2,1)S(1)} collective-permute-done((bf16[16,2,64,128]{3,2,1,0:T(8,128)(2,1)S(1)}, bf16[16,2,64,128]{3,2,1,0:T(8,128)(2,1)S(1)}, u32[]{:S(2)}, u32[]{:S(2)}) %collective-permute-start.5) | collective-permute-done | bytes 524320 | tf_op jit(solution)/shard_map/ppermute | solution.py:133
  77.5 1.9 %collective-permute-start.7 = (bf16[16,2,64,128]{3,2,1,0:T(8,128)(2,1)S(1)}, bf16[16,2,64,128]{3,2,1,0:T(8,128)(2,1)}, u32[]{:S(2)}, u32[]{:S(2)}) collective-permute-start(bf16[16,2,64,128]{3,2,1,0:T(8,128)(2,1)S(1)} %collective-permute-done.5.refs_3_), channel_id=1, source_target_pairs={{0,1},{1,0},{2,3},{3,2},{4,5},{5,4},{6,7},{7,6},{8,9},{9,8},{10,11... | collective-permute-start | bytes 1572872 | tf_op jit(solution)/shard_map/ppermute | solution.py:127
  79.5 2.4 %collective-permute-start.6 = (bf16[16,2,64,128]{3,2,1,0:T(8,128)(2,1)S(1)}, bf16[16,2,64,128]{3,2,1,0:T(8,128)(2,1)}, u32[]{:S(2)}, u32[]{:S(2)}) collective-permute-start(bf16[16,2,64,128]{3,2,1,0:T(8,128)(2,1)S(1)} %collective-permute-done.2.refs_2_), channel_id=1, source_target_pairs={{0,1},{1,0},{2,3},{3,2},{4,5},{5,4},{6,7},{7,6},{8,9},{9,8},{10,11... | collective-permute-start | bytes 1572872 | tf_op jit(solution)/shard_map/ppermute | solution.py:127
  81.9 1.6 %collective-permute-done.6.refs_6_ = bf16[16,2,64,128]{3,2,1,0:T(8,128)(2,1)} collective-permute-done((bf16[16,2,64,128]{3,2,1,0:T(8,128)(2,1)S(1)}, bf16[16,2,64,128]{3,2,1,0:T(8,128)(2,1)}, u32[]{:S(2)}, u32[]{:S(2)}) %collective-permute-start.6) | collective-permute-done | bytes 524320 | tf_op jit(solution)/shard_map/ppermute | solution.py:127
  83.6 10.6 %shard_map.46 = bf16[8,32,1024]{2,1,0:T(8,128)(2,1)S(1)} custom-call(s32[1]{0:T(128)} %bitcast.core_ref, s32[4,17]{1,0:T(4,128)S(1)} %pad_add_fusion.entries, bf16[8,32,1024]{2,1,0:T(8,128)(2,1)S(1)} %all-to-all-done.2.q_ref, bf16[19,2,64,128]{3,2,1,0:T(8,128)(2,1)S(1)} %pad_maximum_fusion.refs_0_, ...), custom_call_target="tpu_custom_call" | custom-call | flops 2147483648 | bytes 8388608 | tf_op jit(solution)/shard_map/pallas_call | solution.py:99
  94.2 23.6 %all_to_all.21 = bf16[8,32,1024]{2,1,0:T(8,128)(2,1)S(1)} all-to-all(bf16[8,32,1024]{2,1,0:T(8,128)(2,1)S(1)} %shard_map.46), channel_id=1, replica_groups=mesh['z'=8,'x'=4,'ylo'=2,'yhi'=4,'core'=2] {'ylo','yhi'}, dimensions={0} | all-to-all | bytes 1048576 | tf_op jit(solution)/shard_map/all_to_all | solution.py:173
  117.7 0.8 copy.21
  (30 shorter events, 0.6 us)
Async XLA Ops:
  0.0 0.7 copy-start.2
  18.6 28.1 %copy-start.1 = (bf16[32,8192]{1,0:T(8,128)(2,1)S(1)}, bf16[32,8192]{1,0:T(8,128)(2,1)}, u32[]{:S(2)}) copy-start(bf16[32,8192]{1,0:T(8,128)(2,1)} %param.4) | copy-start | bytes 1572868
  18.6 24.7 %all-to-all-start.1 = ((bf16[8,2,2,64,128]{4,3,2,1,0:T(8,128)(2,1)}), bf16[8,2,2,64,128]{4,3,2,1,0:T(8,128)(2,1)S(1)}, u32[]{:S(2)}, u32[]{:S(2)}) async-start(bf16[8,2,2,64,128]{4,3,2,1,0:T(8,128)(2,1)} %broadcast_in_dim.25), calls=%async_computation.1 | async-start | bytes 1048576 | tf_op jit(solution)/shard_map/all_to_all | solution.py:150
  43.3 16.0 %copy-start = (bf16[8,2,2,64,128]{4,3,2,1,0:T(8,128)(2,1)}, bf16[8,2,2,64,128]{4,3,2,1,0:T(8,128)(2,1)S(1)}, u32[]{:S(2)}) copy-start(bf16[8,2,2,64,128]{4,3,2,1,0:T(8,128)(2,1)S(1)} %all-to-all-done.1) | copy-start | bytes 1572868
  43.3 16.0 %collective-permute-start = (bf16[16,2,64,128]{3,2,1,0:T(8,128)(2,1)S(1)}, bf16[16,2,64,128]{3,2,1,0:T(8,128)(2,1)S(1)}, u32[]{:S(2)}, u32[]{:S(2)}) collective-permute-start(bf16[16,2,64,128]{3,2,1,0:T(8,128)(2,1)S(1)} %bitcast.29), channel_id=1, source_target_pairs={{0,16},{1,49},{16,32},{17,1},{32,48},{33,17},{48,0},{49,33},{2,18}... | collective-permute-start | bytes 1572872 | tf_op jit(solution)/shard_map/ppermute | solution.py:133
  47.5 31.9 %all-to-all-start.2 = ((bf16[8,32,1024]{2,1,0:T(8,128)(2,1)}), bf16[8,32,1024]{2,1,0:T(8,128)(2,1)S(1)}, u32[]{:S(2)}, u32[]{:S(2)}) async-start(bf16[8,32,1024]{2,1,0:T(8,128)(2,1)} %bitcast.28), calls=%async_computation.2 | async-start | bytes 1048576 | tf_op jit(solution)/shard_map/all_to_all | solution.py:156
  51.4 7.9 %collective-permute-start.1 = (bf16[2,64,128]{2,1,0:T(8,128)(2,1)S(1)}, bf16[2,64,128]{2,1,0:T(8,128)(2,1)S(1)}, u32[]{:S(2)}, u32[]{:S(2)}) collective-permute-start(bf16[2,64,128]{2,1,0:T(8,128)(2,1)S(1)} %slice_bitcast_fusion), channel_id=1, source_target_pairs={{0,16},{16,32},{32,48},{48,64},{64,80},{80,96},{96,112},{112,128},... | collective-permute-start | bytes 98312 | tf_op jit(solution)/shard_map/ppermute | solution.py:158
  59.4 20.1 %collective-permute-start.3 = (bf16[19,2,64,128]{3,2,1,0:T(8,128)(2,1)S(1)}, bf16[19,2,64,128]{3,2,1,0:T(8,128)(2,1)S(1)}, u32[]{:S(2)}, u32[]{:S(2)}) collective-permute-start(bf16[19,2,64,128]{3,2,1,0:T(8,128)(2,1)S(1)} %pad_maximum_fusion.refs_0_), channel_id=1, source_target_pairs={{0,1},{1,0},{2,3},{3,2},{4,5},{5,4},{6,7},{7,6},{8,9},{9,8},{10,11... | collective-permute-start | bytes 1867784 | tf_op jit(solution)/shard_map/ppermute | solution.py:127
  61.4 16.2 %collective-permute-start.5 = (bf16[16,2,64,128]{3,2,1,0:T(8,128)(2,1)S(1)}, bf16[16,2,64,128]{3,2,1,0:T(8,128)(2,1)S(1)}, u32[]{:S(2)}, u32[]{:S(2)}) collective-permute-start(bf16[16,2,64,128]{3,2,1,0:T(8,128)(2,1)S(1)} %collective-permute-done.refs_1_), channel_id=1, source_target_pairs={{0,16},{1,49},{16,32},{17,1},{32,48},{33,17},{48,0},{49,33},{2,18}... | collective-permute-start | bytes 1572872 | tf_op jit(solution)/shard_map/ppermute | solution.py:133
  63.3 16.2 %collective-permute-start.2 = (bf16[16,2,64,128]{3,2,1,0:T(8,128)(2,1)}, bf16[16,2,64,128]{3,2,1,0:T(8,128)(2,1)S(1)}, u32[]{:S(2)}, u32[]{:S(2)}) collective-permute-start(bf16[16,2,64,128]{3,2,1,0:T(8,128)(2,1)} %bitcast.31), channel_id=1, source_target_pairs={{0,48},{1,17},{16,0},{17,33},{32,16},{33,49},{48,32},{49,1},{2,50}... | collective-permute-start | bytes 1572872 | tf_op jit(solution)/shard_map/ppermute | solution.py:133
  68.4 11.0 %collective-permute-start.4 = (bf16[16,2,64,128]{3,2,1,0:T(8,128)(2,1)S(1)}, bf16[16,2,64,128]{3,2,1,0:T(8,128)(2,1)}, u32[]{:S(2)}, u32[]{:S(2)}) collective-permute-start(bf16[16,2,64,128]{3,2,1,0:T(8,128)(2,1)S(1)} %collective-permute-done.refs_1_), channel_id=1, source_target_pairs={{0,1},{1,0},{2,3},{3,2},{4,5},{5,4},{6,7},{7,6},{8,9},{9,8},{10,11... | collective-permute-start | bytes 1572872 | tf_op jit(solution)/shard_map/ppermute | solution.py:127
  77.5 4.4 %collective-permute-start.7 = (bf16[16,2,64,128]{3,2,1,0:T(8,128)(2,1)S(1)}, bf16[16,2,64,128]{3,2,1,0:T(8,128)(2,1)}, u32[]{:S(2)}, u32[]{:S(2)}) collective-permute-start(bf16[16,2,64,128]{3,2,1,0:T(8,128)(2,1)S(1)} %collective-permute-done.5.refs_3_), channel_id=1, source_target_pairs={{0,1},{1,0},{2,3},{3,2},{4,5},{5,4},{6,7},{7,6},{8,9},{9,8},{10,11... | collective-permute-start | bytes 1572872 | tf_op jit(solution)/shard_map/ppermute | solution.py:127
  79.5 4.1 %collective-permute-start.6 = (bf16[16,2,64,128]{3,2,1,0:T(8,128)(2,1)S(1)}, bf16[16,2,64,128]{3,2,1,0:T(8,128)(2,1)}, u32[]{:S(2)}, u32[]{:S(2)}) collective-permute-start(bf16[16,2,64,128]{3,2,1,0:T(8,128)(2,1)S(1)} %collective-permute-done.2.refs_2_), channel_id=1, source_target_pairs={{0,1},{1,0},{2,3},{3,2},{4,5},{5,4},{6,7},{7,6},{8,9},{9,8},{10,11... | collective-permute-start | bytes 1572872 | tf_op jit(solution)/shard_map/ppermute | solution.py:127

commit v8 on v7

--- a/solution.py
+++ b/solution.py
@@ -24,24 +24,8 @@
 
 def attend(core_ref, entries, q_ref, *refs):
     columns = refs[:8]
-    out_ref, table, keys, values, scores, weights, sems = refs[8:]
+    out_ref, keys, values, scores, weights = refs[8:]
     core = core_ref[0]
-    evens = table.shape[1] - ODD
-    per_column = evens // 4
-    copies = []
-
-    def bring(source, target):
-        copy = pltpu.make_async_copy(source, target, sems.at[len(copies)])
-        copy.start()
-        copies.append(copy)
-
-    for rc in range(2):
-        side = jnp.bitwise_xor(core, rc)
-        for source, relative in zip(columns[rc * 4 : rc * 4 + 4], (0, 3 - 2 * side, 1 + 2 * side, 2)):
-            bring(source.at[pl.ds(0, per_column)], table.at[rc, pl.ds(relative * per_column, per_column)])
-        bring(columns[rc * 4].at[pl.ds(per_column, ODD)], table.at[rc, pl.ds(evens, ODD)])
-    for copy in copies:
-        copy.wait()
 
     cell = lax.broadcasted_iota(jnp.int32, (ROWS, BLOCK_POSITIONS), 1)
     row = lax.broadcasted_iota(jnp.int32, (ROWS, BLOCK_POSITIONS), 0)
@@ -52,11 +36,16 @@
     def one_block(b, carry):
         count = entries[b, MAXB]
         for e in range(MAXB):
-            t = entries[b, e]
+            relative, row = entries[b, e] // 32, entries[b, e] % 32
+            inside = jnp.minimum(row, columns[1].shape[0] - 1)
             for rc in range(2):
+                own, first, second, far = columns[rc * 4 : rc * 4 + 4]
+                side = jnp.bitwise_xor(core, rc)
                 span = pl.ds(e * BLOCK_POSITIONS + rc * HALF, HALF)
-                keys[span, :] = table[rc, t, 0]
-                values[span, :] = table[rc, t, 1]
+                for which, target in enumerate((keys, values)):
+                    picked = jnp.where(relative == 0, own[row, which], far[inside, which])
+                    picked = jnp.where(relative == 3 - 2 * side, first[inside, which], picked)
+                    target[span, :] = jnp.where(relative == 1 + 2 * side, second[inside, which], picked)
         peaks = []
         for strip in range(2):
             q = jnp.concatenate(
@@ -92,22 +81,18 @@
 
 
 def attention(core, entries, q, columns, interpret=False):
-    evens = 4 * columns[1].shape[0]
     smem = pl.BlockSpec(memory_space=pltpu.SMEM)
     vmem = pl.BlockSpec(memory_space=pltpu.VMEM)
-    hbm = pl.BlockSpec(memory_space=pl.ANY)
     return pl.pallas_call(
         attend,
         out_shape=jax.ShapeDtypeStruct(q.shape, q.dtype),
-        in_specs=[smem, smem, vmem] + [hbm] * 8,
+        in_specs=[smem, smem] + [vmem] * 9,
         out_specs=vmem,
         scratch_shapes=[
-            pltpu.VMEM((2, evens + ODD, 2, HALF, HEAD_SIZE), jnp.bfloat16),
             pltpu.VMEM((KEYS, HEAD_SIZE), jnp.bfloat16),
             pltpu.VMEM((KEYS, HEAD_SIZE), jnp.bfloat16),
             pltpu.VMEM((2, MAXB, ROWS, BLOCK_POSITIONS), jnp.float32),
             pltpu.VMEM((2, ROWS, KEYS), jnp.bfloat16),
-            pltpu.SemaphoreType.DMA((10,)),
         ],
         compiler_params=pltpu.CompilerParams(vmem_limit_bytes=40 * 2**20),
         cost_estimate=pl.CostEstimate(flops=2**31, bytes_accessed=8 * 2**20, transcendentals=2**22),
@@ -115,12 +100,11 @@
     )(core, entries, q, *columns)
 
 
-def table_entries(z, x, listed, evens):
+def table_entries(z, x, listed, per_column):
     j = listed[:, :MAXB]
-    relative = jnp.bitwise_and(j // 4 - x, 3)
-    even_row = relative * (evens // 4) + j // 16 * 2 + (j // 2) % 2
-    odd_row = evens + jnp.clip((j - 4 * (z * 4 + x) + 1) // 2, 0, ODD - 1)
-    return jnp.concatenate([jnp.where(j % 2 == 0, even_row, odd_row), listed[:, MAXB:]], axis=1)
+    even = jnp.bitwise_and(j // 4 - x, 3) * 32 + j // 16 * 2 + (j // 2) % 2
+    odd = per_column + jnp.clip((j - 4 * (z * 4 + x) + 1) // 2, 0, ODD - 1)
+    return jnp.concatenate([jnp.where(j % 2 == 0, even, odd), listed[:, MAXB:]], axis=1)
 
 
 def swap(array, axis):
@@ -164,7 +148,7 @@
     own_swapped = swap(own, CORE)
     first_swapped = swap(first, CORE)
     listed = received[:: heads // 2, 2 * STRIP, : 2 * MAXB + 2].astype(jnp.int32).reshape(4, MAXB + 1)
-    entries = table_entries(z, x, listed, 4 * column.shape[0])
+    entries = table_entries(z, x, listed, column.shape[0])
     second, q, entries, own_swapped, first_swapped = lax.optimization_barrier(
         (second, q, entries, own_swapped, first_swapped)
     )

time: 119 us -> 121 us (1.017)
  Pallas kernels: 10.6 us -> 11.9 us
    pallas_call x1, Pallas kernels: 10.6 us -> 11.9 us  [attention(): pl.pallas_call(attend, out_shape=jax.ShapeDtypeStruct(q.shape, q.dtype),...]
where the time goes in v8:
time: 121 us; the launch traced here: 120 us
  blocking collectives  39.2 us (32%)
  starting transfers between devices  36 us (30%)
  waiting for transfers between devices  27.6 us (23%)
  Pallas kernels  11.9 us (10%)
  local copies, waits for them, and re-layouts  3.94 us (3%)
    all_to_all x1, blocking collectives, body(): lax.all_to_all(result, RING, split_axis=0, concat_axis=0, tiled=True)  23.6 us
    all_to_all x1, blocking collectives, body(): lax.all_to_all(sent, RING, split_axis=0, concat_axis=0, tiled=True)  15.7 us
    all_to_all x1, waiting for transfers between devices, body(): column = lax.all_to_all(copies, Z, split_axis=0, concat_axis=0, tiled=True)  14.6 us
    pallas_call x1, Pallas kernels, attention(): pl.pallas_call(attend, out_shape=jax.ShapeDtypeStruct(q.shape, q.dtype),...  11.9 us
    ppermute x3, starting transfers between devices, around(): return lax.ppermute(array, (axis, CORE), pairs)  10.4 us
    all_to_all x1, starting transfers between devices, body(): column = lax.all_to_all(copies, Z, split_axis=0, concat_axis=0, tiled=True)  10.1 us
    ppermute x4, starting transfers between devices, swap(): return lax.ppermute(array, axis, [(0, 1), (1, 0)])  8.16 us
    ppermute x3, waiting for transfers between devices, around(): return lax.ppermute(array, (axis, CORE), pairs)  6.89 us
  transfers between devices with their start and end apart: 10, of which 4 were waited for; matrix products, arithmetic and copies ran while one was open for 1% of the time, Pallas kernels for 0%

profile of v8, /device:TPU:72, one launch (start us, length us, event | category | flops | bytes accessed | tf_op | source)
XLA Modules:
  0.0 119.9 jit_solution(10935140070080157072)
XLA Ops:
  0.0 0.7 convert.8
  0.7 0.1 copy.15
  0.9 0.1 convert_element_type.21
  1.0 0.9 copy.22
  2.0 15.7 %all_to_all.20 = bf16[8,80,128]{2,1,0:T(8,128)(2,1)S(1)} all-to-all(bf16[8,80,128]{2,1,0:T(8,128)(2,1)S(1)} %copy.16), channel_id=1, replica_groups=mesh['z'=8,'x'=4,'ylo'=2,'yhi'=4,'core'=2] {'ylo','yhi'}, dimensions={0} | all-to-all | bytes 327680 | tf_op jit(solution)/shard_map/all_to_all | solution.py:128
  17.7 0.9 broadcast_in_dim.25
  18.6 10.1 %all-to-all-start.1 = ((bf16[8,2,2,64,128]{4,3,2,1,0:T(8,128)(2,1)}), bf16[8,2,2,64,128]{4,3,2,1,0:T(8,128)(2,1)S(1)}, u32[]{:S(2)}, u32[]{:S(2)}) async-start(bf16[8,2,2,64,128]{4,3,2,1,0:T(8,128)(2,1)} %broadcast_in_dim.25), calls=%async_computation.1 | async-start | bytes 1048576 | tf_op jit(solution)/shard_map/all_to_all | solution.py:134
  28.7 14.6 %all-to-all-done.1 = bf16[8,2,2,64,128]{4,3,2,1,0:T(8,128)(2,1)S(1)} async-done(((bf16[8,2,2,64,128]{4,3,2,1,0:T(8,128)(2,1)}), bf16[8,2,2,64,128]{4,3,2,1,0:T(8,128)(2,1)S(1)}, u32[]{:S(2)}, u32[]{:S(2)}) %all-to-all-start.1) | async-done | bytes 524320 | tf_op jit(solution)/shard_map/all_to_all | solution.py:134
  43.3 3.4 %collective-permute-start = (bf16[16,2,64,128]{3,2,1,0:T(8,128)(2,1)S(1)}, bf16[16,2,64,128]{3,2,1,0:T(8,128)(2,1)S(1)}, u32[]{:S(2)}, u32[]{:S(2)}) collective-permute-start(bf16[16,2,64,128]{3,2,1,0:T(8,128)(2,1)S(1)} %bitcast.29), channel_id=1, source_target_pairs={{0,16},{1,49},{16,32},{17,1},{32,48},{33,17},{48,0},{49,33},{2,18}... | collective-permute-start | bytes 1572872 | tf_op jit(solution)/shard_map/ppermute | solution.py:117
  46.7 0.8 copy.26
  47.5 3.9 %all-to-all-start.2 = ((bf16[8,32,1024]{2,1,0:T(8,128)(2,1)}), bf16[8,32,1024]{2,1,0:T(8,128)(2,1)S(1)}, u32[]{:S(2)}, u32[]{:S(2)}) async-start(bf16[8,32,1024]{2,1,0:T(8,128)(2,1)} %bitcast.28), calls=%async_computation.2 | async-start | bytes 1048576 | tf_op jit(solution)/shard_map/all_to_all | solution.py:140
  51.4 3.4 %collective-permute-start.1 = (bf16[2,64,128]{2,1,0:T(8,128)(2,1)S(1)}, bf16[2,64,128]{2,1,0:T(8,128)(2,1)S(1)}, u32[]{:S(2)}, u32[]{:S(2)}) collective-permute-start(bf16[2,64,128]{2,1,0:T(8,128)(2,1)S(1)} %slice_bitcast_fusion), channel_id=1, source_target_pairs={{0,16},{16,32},{32,48},{48,64},{64,80},{80,96},{96,112},{112,128},... | collective-permute-start | bytes 98312 | tf_op jit(solution)/shard_map/ppermute | solution.py:142
  54.8 4.5 %collective-permute-done.1 = bf16[2,64,128]{2,1,0:T(8,128)(2,1)S(1)} collective-permute-done((bf16[2,64,128]{2,1,0:T(8,128)(2,1)S(1)}, bf16[2,64,128]{2,1,0:T(8,128)(2,1)S(1)}, u32[]{:S(2)}, u32[]{:S(2)}) %collective-permute-start.1) | collective-permute-done | bytes 32800 | tf_op jit(solution)/shard_map/ppermute | solution.py:142
  59.4 1.9 %collective-permute-start.3 = (bf16[19,2,64,128]{3,2,1,0:T(8,128)(2,1)S(1)}, bf16[19,2,64,128]{3,2,1,0:T(8,128)(2,1)S(1)}, u32[]{:S(2)}, u32[]{:S(2)}) collective-permute-start(bf16[19,2,64,128]{3,2,1,0:T(8,128)(2,1)S(1)} %pad_maximum_fusion.refs_0_), channel_id=1, source_target_pairs={{0,1},{1,0},{2,3},{3,2},{4,5},{5,4},{6,7},{7,6},{8,9},{9,8},{10,11... | collective-permute-start | bytes 1867784 | tf_op jit(solution)/shard_map/ppermute | solution.py:111
  61.4 1.9 %collective-permute-start.5 = (bf16[16,2,64,128]{3,2,1,0:T(8,128)(2,1)S(1)}, bf16[16,2,64,128]{3,2,1,0:T(8,128)(2,1)S(1)}, u32[]{:S(2)}, u32[]{:S(2)}) collective-permute-start(bf16[16,2,64,128]{3,2,1,0:T(8,128)(2,1)S(1)} %collective-permute-done.refs_1_), channel_id=1, source_target_pairs={{0,16},{1,49},{16,32},{17,1},{32,48},{33,17},{48,0},{49,33},{2,18}... | collective-permute-start | bytes 1572872 | tf_op jit(solution)/shard_map/ppermute | solution.py:117
  63.3 5.1 %collective-permute-start.2 = (bf16[16,2,64,128]{3,2,1,0:T(8,128)(2,1)}, bf16[16,2,64,128]{3,2,1,0:T(8,128)(2,1)S(1)}, u32[]{:S(2)}, u32[]{:S(2)}) collective-permute-start(bf16[16,2,64,128]{3,2,1,0:T(8,128)(2,1)} %bitcast.31), channel_id=1, source_target_pairs={{0,48},{1,17},{16,0},{17,33},{32,16},{33,49},{48,32},{49,1},{2,50}... | collective-permute-start | bytes 1572872 | tf_op jit(solution)/shard_map/ppermute | solution.py:117
  68.4 1.9 %collective-permute-start.4 = (bf16[16,2,64,128]{3,2,1,0:T(8,128)(2,1)S(1)}, bf16[16,2,64,128]{3,2,1,0:T(8,128)(2,1)}, u32[]{:S(2)}, u32[]{:S(2)}) collective-permute-start(bf16[16,2,64,128]{3,2,1,0:T(8,128)(2,1)S(1)} %collective-permute-done.refs_1_), channel_id=1, source_target_pairs={{0,1},{1,0},{2,3},{3,2},{4,5},{5,4},{6,7},{7,6},{8,9},{9,8},{10,11... | collective-permute-start | bytes 1572872 | tf_op jit(solution)/shard_map/ppermute | solution.py:111
  70.6 6.9 %collective-permute-done.5.refs_3_ = bf16[16,2,64,128]{3,2,1,0:T(8,128)(2,1)S(1)} collective-permute-done((bf16[16,2,64,128]{3,2,1,0:T(8,128)(2,1)S(1)}, bf16[16,2,64,128]{3,2,1,0:T(8,128)(2,1)S(1)}, u32[]{:S(2)}, u32[]{:S(2)}) %collective-permute-start.5) | collective-permute-done | bytes 524320 | tf_op jit(solution)/shard_map/ppermute | solution.py:117
  77.5 1.9 %collective-permute-start.7 = (bf16[16,2,64,128]{3,2,1,0:T(8,128)(2,1)S(1)}, bf16[16,2,64,128]{3,2,1,0:T(8,128)(2,1)}, u32[]{:S(2)}, u32[]{:S(2)}) collective-permute-start(bf16[16,2,64,128]{3,2,1,0:T(8,128)(2,1)S(1)} %collective-permute-done.5.refs_3_), channel_id=1, source_target_pairs={{0,1},{1,0},{2,3},{3,2},{4,5},{5,4},{6,7},{7,6},{8,9},{9,8},{10,11... | collective-permute-start | bytes 1572872 | tf_op jit(solution)/shard_map/ppermute | solution.py:111
  79.5 2.4 %collective-permute-start.6 = (bf16[16,2,64,128]{3,2,1,0:T(8,128)(2,1)S(1)}, bf16[16,2,64,128]{3,2,1,0:T(8,128)(2,1)}, u32[]{:S(2)}, u32[]{:S(2)}) collective-permute-start(bf16[16,2,64,128]{3,2,1,0:T(8,128)(2,1)S(1)} %collective-permute-done.2.refs_2_), channel_id=1, source_target_pairs={{0,1},{1,0},{2,3},{3,2},{4,5},{5,4},{6,7},{7,6},{8,9},{9,8},{10,11... | collective-permute-start | bytes 1572872 | tf_op jit(solution)/shard_map/ppermute | solution.py:111
  81.9 1.6 %collective-permute-done.6.refs_6_ = bf16[16,2,64,128]{3,2,1,0:T(8,128)(2,1)} collective-permute-done((bf16[16,2,64,128]{3,2,1,0:T(8,128)(2,1)S(1)}, bf16[16,2,64,128]{3,2,1,0:T(8,128)(2,1)}, u32[]{:S(2)}, u32[]{:S(2)}) %collective-permute-start.6) | collective-permute-done | bytes 524320 | tf_op jit(solution)/shard_map/ppermute | solution.py:111
  83.6 11.9 %shard_map.46 = bf16[8,32,1024]{2,1,0:T(8,128)(2,1)S(1)} custom-call(s32[1]{0:T(128)} %bitcast.core_ref, s32[4,17]{1,0:T(4,128)S(1)} %pad_add_fusion.entries, bf16[8,32,1024]{2,1,0:T(8,128)(2,1)S(1)} %all-to-all-done.2.q_ref, bf16[19,2,64,128]{3,2,1,0:T(8,128)(2,1)S(1)} %pad_maximum_fusion.refs_0_, ...), custom_call_target="tpu_custom_call" | custom-call | flops 2147483648 | bytes 8388608 | tf_op jit(solution)/shard_map/pallas_call | solution.py:86
  95.5 23.6 %all_to_all.21 = bf16[8,32,1024]{2,1,0:T(8,128)(2,1)S(1)} all-to-all(bf16[8,32,1024]{2,1,0:T(8,128)(2,1)S(1)} %shard_map.46), channel_id=1, replica_groups=mesh['z'=8,'x'=4,'ylo'=2,'yhi'=4,'core'=2] {'ylo','yhi'}, dimensions={0} | all-to-all | bytes 1048576 | tf_op jit(solution)/shard_map/all_to_all | solution.py:157
  119.1 0.8 copy.21
  (30 shorter events, 0.6 us)
Async XLA Ops:
  0.0 0.7 copy-start.2
  18.6 28.1 %copy-start.1 = (bf16[32,8192]{1,0:T(8,128)(2,1)S(1)}, bf16[32,8192]{1,0:T(8,128)(2,1)}, u32[]{:S(2)}) copy-start(bf16[32,8192]{1,0:T(8,128)(2,1)} %param.4) | copy-start | bytes 1572868
  18.6 24.7 %all-to-all-start.1 = ((bf16[8,2,2,64,128]{4,3,2,1,0:T(8,128)(2,1)}), bf16[8,2,2,64,128]{4,3,2,1,0:T(8,128)(2,1)S(1)}, u32[]{:S(2)}, u32[]{:S(2)}) async-start(bf16[8,2,2,64,128]{4,3,2,1,0:T(8,128)(2,1)} %broadcast_in_dim.25), calls=%async_computation.1 | async-start | bytes 1048576 | tf_op jit(solution)/shard_map/all_to_all | solution.py:134
  43.3 16.0 %copy-start = (bf16[8,2,2,64,128]{4,3,2,1,0:T(8,128)(2,1)}, bf16[8,2,2,64,128]{4,3,2,1,0:T(8,128)(2,1)S(1)}, u32[]{:S(2)}) copy-start(bf16[8,2,2,64,128]{4,3,2,1,0:T(8,128)(2,1)S(1)} %all-to-all-done.1) | copy-start | bytes 1572868
  43.3 16.0 %collective-permute-start = (bf16[16,2,64,128]{3,2,1,0:T(8,128)(2,1)S(1)}, bf16[16,2,64,128]{3,2,1,0:T(8,128)(2,1)S(1)}, u32[]{:S(2)}, u32[]{:S(2)}) collective-permute-start(bf16[16,2,64,128]{3,2,1,0:T(8,128)(2,1)S(1)} %bitcast.29), channel_id=1, source_target_pairs={{0,16},{1,49},{16,32},{17,1},{32,48},{33,17},{48,0},{49,33},{2,18}... | collective-permute-start | bytes 1572872 | tf_op jit(solution)/shard_map/ppermute | solution.py:117
  47.5 31.9 %all-to-all-start.2 = ((bf16[8,32,1024]{2,1,0:T(8,128)(2,1)}), bf16[8,32,1024]{2,1,0:T(8,128)(2,1)S(1)}, u32[]{:S(2)}, u32[]{:S(2)}) async-start(bf16[8,32,1024]{2,1,0:T(8,128)(2,1)} %bitcast.28), calls=%async_computation.2 | async-start | bytes 1048576 | tf_op jit(solution)/shard_map/all_to_all | solution.py:140
  51.4 7.9 %collective-permute-start.1 = (bf16[2,64,128]{2,1,0:T(8,128)(2,1)S(1)}, bf16[2,64,128]{2,1,0:T(8,128)(2,1)S(1)}, u32[]{:S(2)}, u32[]{:S(2)}) collective-permute-start(bf16[2,64,128]{2,1,0:T(8,128)(2,1)S(1)} %slice_bitcast_fusion), channel_id=1, source_target_pairs={{0,16},{16,32},{32,48},{48,64},{64,80},{80,96},{96,112},{112,128},... | collective-permute-start | bytes 98312 | tf_op jit(solution)/shard_map/ppermute | solution.py:142
  59.4 20.1 %collective-permute-start.3 = (bf16[19,2,64,128]{3,2,1,0:T(8,128)(2,1)S(1)}, bf16[19,2,64,128]{3,2,1,0:T(8,128)(2,1)S(1)}, u32[]{:S(2)}, u32[]{:S(2)}) collective-permute-start(bf16[19,2,64,128]{3,2,1,0:T(8,128)(2,1)S(1)} %pad_maximum_fusion.refs_0_), channel_id=1, source_target_pairs={{0,1},{1,0},{2,3},{3,2},{4,5},{5,4},{6,7},{7,6},{8,9},{9,8},{10,11... | collective-permute-start | bytes 1867784 | tf_op jit(solution)/shard_map/ppermute | solution.py:111
  61.4 16.2 %collective-permute-start.5 = (bf16[16,2,64,128]{3,2,1,0:T(8,128)(2,1)S(1)}, bf16[16,2,64,128]{3,2,1,0:T(8,128)(2,1)S(1)}, u32[]{:S(2)}, u32[]{:S(2)}) collective-permute-start(bf16[16,2,64,128]{3,2,1,0:T(8,128)(2,1)S(1)} %collective-permute-done.refs_1_), channel_id=1, source_target_pairs={{0,16},{1,49},{16,32},{17,1},{32,48},{33,17},{48,0},{49,33},{2,18}... | collective-permute-start | bytes 1572872 | tf_op jit(solution)/shard_map/ppermute | solution.py:117
  63.3 16.2 %collective-permute-start.2 = (bf16[16,2,64,128]{3,2,1,0:T(8,128)(2,1)}, bf16[16,2,64,128]{3,2,1,0:T(8,128)(2,1)S(1)}, u32[]{:S(2)}, u32[]{:S(2)}) collective-permute-start(bf16[16,2,64,128]{3,2,1,0:T(8,128)(2,1)} %bitcast.31), channel_id=1, source_target_pairs={{0,48},{1,17},{16,0},{17,33},{32,16},{33,49},{48,32},{49,1},{2,50}... | collective-permute-start | bytes 1572872 | tf_op jit(solution)/shard_map/ppermute | solution.py:117
  68.4 11.0 %collective-permute-start.4 = (bf16[16,2,64,128]{3,2,1,0:T(8,128)(2,1)S(1)}, bf16[16,2,64,128]{3,2,1,0:T(8,128)(2,1)}, u32[]{:S(2)}, u32[]{:S(2)}) collective-permute-start(bf16[16,2,64,128]{3,2,1,0:T(8,128)(2,1)S(1)} %collective-permute-done.refs_1_), channel_id=1, source_target_pairs={{0,1},{1,0},{2,3},{3,2},{4,5},{5,4},{6,7},{7,6},{8,9},{9,8},{10,11... | collective-permute-start | bytes 1572872 | tf_op jit(solution)/shard_map/ppermute | solution.py:111
  77.5 4.4 %collective-permute-start.7 = (bf16[16,2,64,128]{3,2,1,0:T(8,128)(2,1)S(1)}, bf16[16,2,64,128]{3,2,1,0:T(8,128)(2,1)}, u32[]{:S(2)}, u32[]{:S(2)}) collective-permute-start(bf16[16,2,64,128]{3,2,1,0:T(8,128)(2,1)S(1)} %collective-permute-done.5.refs_3_), channel_id=1, source_target_pairs={{0,1},{1,0},{2,3},{3,2},{4,5},{5,4},{6,7},{7,6},{8,9},{9,8},{10,11... | collective-permute-start | bytes 1572872 | tf_op jit(solution)/shard_map/ppermute | solution.py:111
  79.5 4.1 %collective-permute-start.6 = (bf16[16,2,64,128]{3,2,1,0:T(8,128)(2,1)S(1)}, bf16[16,2,64,128]{3,2,1,0:T(8,128)(2,1)}, u32[]{:S(2)}, u32[]{:S(2)}) collective-permute-start(bf16[16,2,64,128]{3,2,1,0:T(8,128)(2,1)S(1)} %collective-permute-done.2.refs_2_), channel_id=1, source_target_pairs={{0,1},{1,0},{2,3},{3,2},{4,5},{5,4},{6,7},{7,6},{8,9},{9,8},{10,11... | collective-permute-start | bytes 1572872 | tf_op jit(solution)/shard_map/ppermute | solution.py:111

commit v9 on v7

--- a/solution.py
+++ b/solution.py
@@ -18,13 +18,15 @@
 ODD = 3
 NEGATIVE = -1e30
 FACTOR = math.log2(math.e) / math.sqrt(HEAD_SIZE)
-Z, X, YLO, YHI, CORE = "z", "x", "ylo", "yhi", "core"
-RING = (YLO, YHI)
+Z2, Z1, Z0, X, Y0, Y2, Y1, CORE = AXES = ("z2", "z1", "z0", "x", "y0", "y2", "y1", "core")
+Z = (Z2, Z1, Z0)
+Z_RING = (Z0, Z1, Z2)
+Y_RING = (Y0, Y1, Y2)
 
 
 def attend(core_ref, entries, q_ref, *refs):
     columns = refs[:8]
-    out_ref, table, keys, values, scores, weights, sems = refs[8:]
+    out_ref, table, keys, values, scores, peaks, weights, sems = refs[8:]
     core = core_ref[0]
     evens = table.shape[1] - ODD
     per_column = evens // 4
@@ -57,35 +59,44 @@
                 span = pl.ds(e * BLOCK_POSITIONS + rc * HALF, HALF)
                 keys[span, :] = table[rc, t, 0]
                 values[span, :] = table[rc, t, 1]
-        peaks = []
-        for strip in range(2):
-            q = jnp.concatenate(
-                [q_ref[2 * b + strip, :, h * HEAD_SIZE : (h + 1) * HEAD_SIZE] for h in range(GROUP)], axis=0
+        place = b // 2 * 4 + b % 2
+        q = jnp.concatenate(
+            [
+                q_ref[place + 2 * strip, :, h * HEAD_SIZE : (h + 1) * HEAD_SIZE]
+                for strip in range(2)
+                for h in range(GROUP)
+            ],
+            axis=0,
+        )
+        for g in range(MAXB // 2):
+            s = lax.dot_general(
+                q,
+                keys[g * 256 : (g + 1) * 256, :],
+                (((1,), (1,)), ((), ())),
+                preferred_element_type=jnp.float32,
             )
-            peak = None
-            for g in range(MAXB // 2):
-                s = lax.dot_general(
-                    q,
-                    keys[g * 256 : (g + 1) * 256, :],
-                    (((1,), (1,)), ((), ())),
-                    preferred_element_type=jnp.float32,
-                )
+            for strip in range(2):
+                parts = []
                 for e in (2 * g, 2 * g + 1):
-                    part = s[:, (e % 2) * 128 : (e % 2 + 1) * 128]
+                    part = s[strip * ROWS : (strip + 1) * ROWS, (e % 2) * 128 : (e % 2 + 1) * 128]
                     part = jnp.where(ahead <= strip * HALF if e == 0 else e < count, part, NEGATIVE)
                     scores[strip, e] = part
-                    peak = part if peak is None else jnp.maximum(peak, part)
-            peaks.append(jnp.max(peak, axis=1, keepdims=True) * FACTOR)
+                    parts.append(part)
+                peak = jnp.maximum(*parts)
+                peaks[strip] = peak if g == 0 else jnp.maximum(peaks[strip], peak)
         for strip in range(2):
+            top = jnp.max(peaks[strip], axis=1, keepdims=True) * FACTOR
             total = jnp.zeros((ROWS, BLOCK_POSITIONS), jnp.float32)
             for e in range(MAXB):
-                w = jnp.exp2(scores[strip, e] * FACTOR - peaks[strip])
+                w = jnp.exp2(scores[strip, e] * FACTOR - top)
                 total = total + w
                 weights[strip, :, e * 128 : (e + 1) * 128] = w.astype(jnp.bfloat16)
             numerator = jnp.dot(weights[strip], values[...], preferred_element_type=jnp.float32)
             result = (numerator / jnp.sum(total, axis=1, keepdims=True)).astype(jnp.bfloat16)
             for h in range(GROUP):
-                out_ref[2 * b + strip, :, h * HEAD_SIZE : (h + 1) * HEAD_SIZE] = result[h * STRIP : (h + 1) * STRIP]
+                out_ref[place + 2 * strip, :, h * HEAD_SIZE : (h + 1) * HEAD_SIZE] = result[
+                    h * STRIP : (h + 1) * STRIP
+                ]
         return carry
 
     lax.fori_loop(0, 4, one_block, 0)
@@ -106,6 +117,7 @@
             pltpu.VMEM((KEYS, HEAD_SIZE), jnp.bfloat16),
             pltpu.VMEM((KEYS, HEAD_SIZE), jnp.bfloat16),
             pltpu.VMEM((2, MAXB, ROWS, BLOCK_POSITIONS), jnp.float32),
+            pltpu.VMEM((2, ROWS, BLOCK_POSITIONS), jnp.float32),
             pltpu.VMEM((2, ROWS, KEYS), jnp.bfloat16),
             pltpu.SemaphoreType.DMA((10,)),
         ],
@@ -118,7 +130,8 @@
 def table_entries(z, x, listed, evens):
     j = listed[:, :MAXB]
     relative = jnp.bitwise_and(j // 4 - x, 3)
-    even_row = relative * (evens // 4) + j // 16 * 2 + (j // 2) % 2
+    layer = j // 64 + j // 32 % 2 * 2 + j // 16 % 2 * 4
+    even_row = relative * (evens // 4) + layer * 2 + (j // 2) % 2
     odd_row = evens + jnp.clip((j - 4 * (z * 4 + x) + 1) // 2, 0, ODD - 1)
     return jnp.concatenate([jnp.where(j % 2 == 0, even_row, odd_row), listed[:, MAXB:]], axis=1)
 
@@ -135,27 +148,27 @@
 
 def body(queries, keyvals, block_index, block_count):
     z, x, core = (lax.axis_index(a).astype(jnp.int32) for a in (Z, X, CORE))
-    heads = lax.axis_size(RING)
+    heads = lax.axis_size(Y_RING)
 
-    lists = jnp.concatenate([block_index, block_count[:, None]], axis=1).reshape(1, -1).astype(jnp.bfloat16)
-    lists = jnp.pad(lists, ((0, 15), (0, HEAD_SIZE - lists.shape[1])))
+    lists = jnp.concatenate([block_index, block_count[:, None]], axis=1)
+    lists = jnp.pad(lists, ((0, 16 - lists.shape[0]), (0, HEAD_SIZE - lists.shape[1]))).astype(jnp.bfloat16)
     sent = keyvals.reshape(2 * STRIP, heads, HEAD_SIZE).transpose(1, 0, 2)
     sent = jnp.concatenate([sent, jnp.broadcast_to(lists[None], (heads,) + lists.shape)], axis=1)
-    received = lax.all_to_all(sent, RING, split_axis=0, concat_axis=0, tiled=True)
-    local = received[:, : 2 * STRIP].reshape(4, 2, 2, STRIP, HEAD_SIZE).transpose(0, 2, 1, 3, 4)
+    received = lax.all_to_all(sent, Y_RING, split_axis=0, concat_axis=0, tiled=True)
+    local = received[:, : 2 * STRIP].reshape(2, 2, 2, 2, STRIP, HEAD_SIZE).transpose(0, 2, 3, 1, 4, 5)
     local = local.reshape(4, 2, HALF, HEAD_SIZE)
 
     summary = jnp.stack([local[0], local[2]])
     copies = jnp.broadcast_to(summary[None], (lax.axis_size(Z),) + summary.shape)
-    column = lax.all_to_all(copies, Z, split_axis=0, concat_axis=0, tiled=True)
+    column = lax.all_to_all(copies, Z_RING, split_axis=0, concat_axis=0, tiled=True)
     column = column.reshape((-1,) + summary.shape[1:])
     column, queries, odd = lax.optimization_barrier((column, queries, local[1::2]))
 
     first = around(column, X, 1)
     sent_q = queries.reshape(STRIP, heads, GROUP * HEAD_SIZE).transpose(1, 0, 2)
-    q = lax.all_to_all(sent_q, RING, split_axis=0, concat_axis=0, tiled=True)
-    pairs = lax.axis_size((Z, X))
-    before = lax.ppermute(odd[1], (Z, X), [(i, i + 1) for i in range(pairs - 1)])
+    q = lax.all_to_all(sent_q, Y_RING, split_axis=0, concat_axis=0, tiled=True)
+    pairs = lax.axis_size(Z + (X,))
+    before = lax.ppermute(odd[1], Z + (X,), [(i, i + 1) for i in range(pairs - 1)])
     first, column, before = lax.optimization_barrier((first, column, before))
 
     far = around(first, X, 1)
@@ -163,22 +176,20 @@
     own = jnp.concatenate([column, before[None], odd])
     own_swapped = swap(own, CORE)
     first_swapped = swap(first, CORE)
-    listed = received[:: heads // 2, 2 * STRIP, : 2 * MAXB + 2].astype(jnp.int32).reshape(4, MAXB + 1)
+    listed = received[:: heads // 2, 2 * STRIP : 2 * STRIP + 2, : MAXB + 1].astype(jnp.int32).reshape(4, MAXB + 1)
     entries = table_entries(z, x, listed, 4 * column.shape[0])
     second, q, entries, own_swapped, first_swapped = lax.optimization_barrier(
         (second, q, entries, own_swapped, first_swapped)
     )
     columns = [own, first, second, far, own_swapped, first_swapped, swap(second, CORE), swap(far, CORE)]
     result = attention(core[None], entries, q, columns)
-    result = lax.all_to_all(result, RING, split_axis=0, concat_axis=0, tiled=True)
+    result = lax.all_to_all(result, Y_RING, split_axis=0, concat_axis=0, tiled=True)
     return result.transpose(1, 0, 2).reshape(STRIP, heads * GROUP * HEAD_SIZE)
 
 
 def solution(mesh):
-    pb, kv, ha = mesh.devices.shape
-    fine = Mesh(mesh.devices.reshape(pb, kv // 2, 2, ha // 2, 2), (Z, X, YLO, YHI, CORE))
-    rows = (Z, X, YLO, YHI, CORE)
-    shard = (Z, X, YLO)
+    rows, shard = AXES, AXES[:5]
+    fine = Mesh(mesh.devices.reshape(2, 2, 2, -1, 2, 2, 2, 2), AXES)
     return jax.shard_map(
         body,
         mesh=fine,

time: 119 us -> 117 us (0.983)
  the two profiles are of different devices: /device:TPU:72 before, /device:TPU:81 now
where the time goes in v9:
time: 117 us
  starting transfers between devices  41.6 us (36%)
  blocking collectives  36.4 us (31%)
  waiting for transfers between devices  22.7 us (19%)
  Pallas kernels  10.8 us (9%)
  local copies, waits for them, and re-layouts  3.77 us (3%)
    all_to_all x1, blocking collectives, body(): lax.all_to_all(result, Y_RING, split_axis=0, concat_axis=0, tiled=True)  22.3 us
    ppermute x4, starting transfers between devices, swap(): return lax.ppermute(array, axis, [(0, 1), (1, 0)])  16.9 us
    all_to_all x1, blocking collectives, body(): lax.all_to_all(sent, Y_RING, split_axis=0, concat_axis=0, tiled=True)  14.1 us
    all_to_all x1, waiting for transfers between devices, body(): lax.all_to_all(copies, Z_RING, split_axis=0, concat_axis=0, tiled=True)  11.8 us
    pallas_call x1, Pallas kernels, attention(): pl.pallas_call(attend, out_shape=jax.ShapeDtypeStruct(q.shape, q.dtype),...  10.8 us
    ppermute x3, starting transfers between devices, around(): return lax.ppermute(array, (axis, CORE), pairs)  9.66 us
    all_to_all x1, starting transfers between devices, body(): lax.all_to_all(copies, Z_RING, split_axis=0, concat_axis=0, tiled=True)  9.54 us
    ppermute x1, waiting for transfers between devices, body(): lax.ppermute(odd[1], Z + (X,), [(i, i + 1) for i in range(pairs - 1)])  4.94 us
  transfers between devices with their start and end apart: 10, of which 4 were waited for; matrix products, arithmetic and copies ran while one was open for 1% of the time, Pallas kernels for 0%

profile of v9, /device:TPU:81, one launch (start us, length us, event | category | flops | bytes accessed | tf_op | source)
XLA Modules:
  0.0 116.5 jit_solution(16186149118850780102)
XLA Ops:
  0.0 0.7 convert.10
  0.7 0.1 copy.9
  0.8 0.9 copy.15
  1.9 14.1 %all_to_all.20 = bf16[8,80,128]{2,1,0:T(8,128)(2,1)S(1)} all-to-all(bf16[8,80,128]{2,1,0:T(8,128)(2,1)S(1)} %pad_maximum_fusion.1), channel_id=1, replica_groups=mesh['z2'=2,'z1'=2,'z0'=2,'x'=4,'y0'=2,'y2'=2,'y1'=2,'core'=2] {'y0','y1..., dimensions={0} | all-to-all | bytes 327680 | tf_op jit(solution)/shard_map/all_to_all | solution.py:157
  16.0 0.9 broadcast_in_dim.25
  16.9 9.5 %all-to-all-start.1 = ((bf16[8,2,2,64,128]{4,3,2,1,0:T(8,128)(2,1)}), bf16[8,2,2,64,128]{4,3,2,1,0:T(8,128)(2,1)S(1)}, u32[]{:S(2)}, u32[]{:S(2)}) async-start(bf16[8,2,2,64,128]{4,3,2,1,0:T(8,128)(2,1)} %broadcast_in_dim.25), calls=%async_computation.1 | async-start | bytes 1048576 | tf_op jit(solution)/shard_map/all_to_all | solution.py:163
  26.5 11.8 %all-to-all-done.1 = bf16[8,2,2,64,128]{4,3,2,1,0:T(8,128)(2,1)S(1)} async-done(((bf16[8,2,2,64,128]{4,3,2,1,0:T(8,128)(2,1)}), bf16[8,2,2,64,128]{4,3,2,1,0:T(8,128)(2,1)S(1)}, u32[]{:S(2)}, u32[]{:S(2)}) %all-to-all-start.1) | async-done | bytes 524320 | tf_op jit(solution)/shard_map/all_to_all | solution.py:163
  38.3 4.4 %collective-permute-start = (bf16[16,2,64,128]{3,2,1,0:T(8,128)(2,1)S(1)}, bf16[16,2,64,128]{3,2,1,0:T(8,128)(2,1)S(1)}, u32[]{:S(2)}, u32[]{:S(2)}) collective-permute-start(bf16[16,2,64,128]{3,2,1,0:T(8,128)(2,1)S(1)} %bitcast.29), channel_id=1, source_target_pairs={{0,16},{1,49},{16,32},{17,1},{32,48},{33,17},{48,0},{49,33},{2,18}... | collective-permute-start | bytes 1572872 | tf_op jit(solution)/shard_map/ppermute | solution.py:146
  42.7 0.8 copy.18
  43.6 3.6 %all-to-all-start.2 = ((bf16[8,32,1024]{2,1,0:T(8,128)(2,1)}), bf16[8,32,1024]{2,1,0:T(8,128)(2,1)S(1)}, u32[]{:S(2)}, u32[]{:S(2)}) async-start(bf16[8,32,1024]{2,1,0:T(8,128)(2,1)} %bitcast.27), calls=%async_computation.2 | async-start | bytes 1048576 | tf_op jit(solution)/shard_map/all_to_all | solution.py:169
  47.2 1.9 %collective-permute-start.1 = (bf16[2,64,128]{2,1,0:T(8,128)(2,1)S(1)}, bf16[2,64,128]{2,1,0:T(8,128)(2,1)S(1)}, u32[]{:S(2)}, u32[]{:S(2)}) collective-permute-start(bf16[2,64,128]{2,1,0:T(8,128)(2,1)S(1)} %slice_bitcast_fusion), channel_id=1, source_target_pairs={{0,16},{16,32},{32,48},{48,64},{64,80},{80,96},{96,112},{112,128},... | collective-permute-start | bytes 98312 | tf_op jit(solution)/shard_map/ppermute | solution.py:171
  49.1 4.9 %collective-permute-done.1 = bf16[2,64,128]{2,1,0:T(8,128)(2,1)S(1)} collective-permute-done((bf16[2,64,128]{2,1,0:T(8,128)(2,1)S(1)}, bf16[2,64,128]{2,1,0:T(8,128)(2,1)S(1)}, u32[]{:S(2)}, u32[]{:S(2)}) %collective-permute-start.1) | collective-permute-done | bytes 32800 | tf_op jit(solution)/shard_map/ppermute | solution.py:171
  54.1 0.1 pad_maximum_fusion.refs_0_
  54.1 6.4 %collective-permute-start.3 = (bf16[19,2,64,128]{3,2,1,0:T(8,128)(2,1)S(1)}, bf16[19,2,64,128]{3,2,1,0:T(8,128)(2,1)S(1)}, u32[]{:S(2)}, u32[]{:S(2)}) collective-permute-start(bf16[19,2,64,128]{3,2,1,0:T(8,128)(2,1)S(1)} %pad_maximum_fusion.refs_0_), channel_id=1, source_target_pairs={{0,1},{1,0},{2,3},{3,2},{4,5},{5,4},{6,7},{7,6},{8,9},{9,8},{10,11... | collective-permute-start | bytes 1867784 | tf_op jit(solution)/shard_map/ppermute | solution.py:140
  60.6 2.0 %collective-permute-start.5 = (bf16[16,2,64,128]{3,2,1,0:T(8,128)(2,1)S(1)}, bf16[16,2,64,128]{3,2,1,0:T(8,128)(2,1)S(1)}, u32[]{:S(2)}, u32[]{:S(2)}) collective-permute-start(bf16[16,2,64,128]{3,2,1,0:T(8,128)(2,1)S(1)} %collective-permute-done.refs_1_), channel_id=1, source_target_pairs={{0,16},{1,49},{16,32},{17,1},{32,48},{33,17},{48,0},{49,33},{2,18}... | collective-permute-start | bytes 1572872 | tf_op jit(solution)/shard_map/ppermute | solution.py:146
  62.6 3.3 %collective-permute-start.2 = (bf16[16,2,64,128]{3,2,1,0:T(8,128)(2,1)}, bf16[16,2,64,128]{3,2,1,0:T(8,128)(2,1)S(1)}, u32[]{:S(2)}, u32[]{:S(2)}) collective-permute-start(bf16[16,2,64,128]{3,2,1,0:T(8,128)(2,1)} %bitcast.31), channel_id=1, source_target_pairs={{0,48},{1,17},{16,0},{17,33},{32,16},{33,49},{48,32},{49,1},{2,50}... | collective-permute-start | bytes 1572872 | tf_op jit(solution)/shard_map/ppermute | solution.py:146
  65.9 3.7 %collective-permute-start.4 = (bf16[16,2,64,128]{3,2,1,0:T(8,128)(2,1)S(1)}, bf16[16,2,64,128]{3,2,1,0:T(8,128)(2,1)}, u32[]{:S(2)}, u32[]{:S(2)}) collective-permute-start(bf16[16,2,64,128]{3,2,1,0:T(8,128)(2,1)S(1)} %collective-permute-done.refs_1_), channel_id=1, source_target_pairs={{0,1},{1,0},{2,3},{3,2},{4,5},{5,4},{6,7},{7,6},{8,9},{9,8},{10,11... | collective-permute-start | bytes 1572872 | tf_op jit(solution)/shard_map/ppermute | solution.py:140
  69.8 3.9 %collective-permute-done.5.refs_3_ = bf16[16,2,64,128]{3,2,1,0:T(8,128)(2,1)S(1)} collective-permute-done((bf16[16,2,64,128]{3,2,1,0:T(8,128)(2,1)S(1)}, bf16[16,2,64,128]{3,2,1,0:T(8,128)(2,1)S(1)}, u32[]{:S(2)}, u32[]{:S(2)}) %collective-permute-start.5) | collective-permute-done | bytes 524320 | tf_op jit(solution)/shard_map/ppermute | solution.py:146
  73.7 4.8 %collective-permute-start.7 = (bf16[16,2,64,128]{3,2,1,0:T(8,128)(2,1)S(1)}, bf16[16,2,64,128]{3,2,1,0:T(8,128)(2,1)}, u32[]{:S(2)}, u32[]{:S(2)}) collective-permute-start(bf16[16,2,64,128]{3,2,1,0:T(8,128)(2,1)S(1)} %collective-permute-done.5.refs_3_), channel_id=1, source_target_pairs={{0,1},{1,0},{2,3},{3,2},{4,5},{5,4},{6,7},{7,6},{8,9},{9,8},{10,11... | collective-permute-start | bytes 1572872 | tf_op jit(solution)/shard_map/ppermute | solution.py:140
  78.6 1.9 %collective-permute-start.6 = (bf16[16,2,64,128]{3,2,1,0:T(8,128)(2,1)S(1)}, bf16[16,2,64,128]{3,2,1,0:T(8,128)(2,1)}, u32[]{:S(2)}, u32[]{:S(2)}) collective-permute-start(bf16[16,2,64,128]{3,2,1,0:T(8,128)(2,1)S(1)} %collective-permute-done.2.refs_2_), channel_id=1, source_target_pairs={{0,1},{1,0},{2,3},{3,2},{4,5},{5,4},{6,7},{7,6},{8,9},{9,8},{10,11... | collective-permute-start | bytes 1572872 | tf_op jit(solution)/shard_map/ppermute | solution.py:140
  80.6 2.0 %collective-permute-done.6.refs_6_ = bf16[16,2,64,128]{3,2,1,0:T(8,128)(2,1)} collective-permute-done((bf16[16,2,64,128]{3,2,1,0:T(8,128)(2,1)S(1)}, bf16[16,2,64,128]{3,2,1,0:T(8,128)(2,1)}, u32[]{:S(2)}, u32[]{:S(2)}) %collective-permute-start.6) | collective-permute-done | bytes 524320 | tf_op jit(solution)/shard_map/ppermute | solution.py:140
  82.5 10.8 %shard_map.46 = bf16[8,32,1024]{2,1,0:T(8,128)(2,1)S(1)} custom-call(s32[1]{0:T(128)} %bitcast.core_ref, s32[4,17]{1,0:T(4,128)S(1)} %pad_add_fusion.entries, bf16[8,32,1024]{2,1,0:T(8,128)(2,1)S(1)} %all-to-all-done.2.q_ref, bf16[19,2,64,128]{3,2,1,0:T(8,128)(2,1)S(1)} %pad_maximum_fusion.refs_0_, ...), custom_call_target="tpu_custom_call" | custom-call | flops 2147483648 | bytes 8388608 | tf_op jit(solution)/shard_map/pallas_call | solution.py:110
  93.4 22.3 %all_to_all.21 = bf16[8,32,1024]{2,1,0:T(8,128)(2,1)S(1)} all-to-all(bf16[8,32,1024]{2,1,0:T(8,128)(2,1)S(1)} %shard_map.46), channel_id=1, replica_groups=mesh['z2'=2,'z1'=2,'z0'=2,'x'=4,'y0'=2,'y2'=2,'y1'=2,'core'=2] {'y0','y1..., dimensions={0} | all-to-all | bytes 1048576 | tf_op jit(solution)/shard_map/all_to_all | solution.py:186
  115.7 0.8 copy.14
  (28 shorter events, 0.4 us)
Async XLA Ops:
  0.0 0.7 copy-start.2
  16.9 25.8 %copy-start.1 = (bf16[32,8192]{1,0:T(8,128)(2,1)S(1)}, bf16[32,8192]{1,0:T(8,128)(2,1)}, u32[]{:S(2)}) copy-start(bf16[32,8192]{1,0:T(8,128)(2,1)} %param.4) | copy-start | bytes 1572868
  16.9 21.4 %all-to-all-start.1 = ((bf16[8,2,2,64,128]{4,3,2,1,0:T(8,128)(2,1)}), bf16[8,2,2,64,128]{4,3,2,1,0:T(8,128)(2,1)S(1)}, u32[]{:S(2)}, u32[]{:S(2)}) async-start(bf16[8,2,2,64,128]{4,3,2,1,0:T(8,128)(2,1)} %broadcast_in_dim.25), calls=%async_computation.1 | async-start | bytes 1048576 | tf_op jit(solution)/shard_map/all_to_all | solution.py:163
  38.3 15.7 %copy-start = (bf16[8,2,2,64,128]{4,3,2,1,0:T(8,128)(2,1)}, bf16[8,2,2,64,128]{4,3,2,1,0:T(8,128)(2,1)S(1)}, u32[]{:S(2)}) copy-start(bf16[8,2,2,64,128]{4,3,2,1,0:T(8,128)(2,1)S(1)} %all-to-all-done.1) | copy-start | bytes 1572868
  38.3 15.7 %collective-permute-start = (bf16[16,2,64,128]{3,2,1,0:T(8,128)(2,1)S(1)}, bf16[16,2,64,128]{3,2,1,0:T(8,128)(2,1)S(1)}, u32[]{:S(2)}, u32[]{:S(2)}) collective-permute-start(bf16[16,2,64,128]{3,2,1,0:T(8,128)(2,1)S(1)} %bitcast.29), channel_id=1, source_target_pairs={{0,16},{1,49},{16,32},{17,1},{32,48},{33,17},{48,0},{49,33},{2,18}... | collective-permute-start | bytes 1572872 | tf_op jit(solution)/shard_map/ppermute | solution.py:146
  43.6 35.0 %all-to-all-start.2 = ((bf16[8,32,1024]{2,1,0:T(8,128)(2,1)}), bf16[8,32,1024]{2,1,0:T(8,128)(2,1)S(1)}, u32[]{:S(2)}, u32[]{:S(2)}) async-start(bf16[8,32,1024]{2,1,0:T(8,128)(2,1)} %bitcast.27), calls=%async_computation.2 | async-start | bytes 1048576 | tf_op jit(solution)/shard_map/all_to_all | solution.py:169
  47.2 6.9 %collective-permute-start.1 = (bf16[2,64,128]{2,1,0:T(8,128)(2,1)S(1)}, bf16[2,64,128]{2,1,0:T(8,128)(2,1)S(1)}, u32[]{:S(2)}, u32[]{:S(2)}) collective-permute-start(bf16[2,64,128]{2,1,0:T(8,128)(2,1)S(1)} %slice_bitcast_fusion), channel_id=1, source_target_pairs={{0,16},{16,32},{32,48},{48,64},{64,80},{80,96},{96,112},{112,128},... | collective-permute-start | bytes 98312 | tf_op jit(solution)/shard_map/ppermute | solution.py:171
  54.1 24.5 %collective-permute-start.3 = (bf16[19,2,64,128]{3,2,1,0:T(8,128)(2,1)S(1)}, bf16[19,2,64,128]{3,2,1,0:T(8,128)(2,1)S(1)}, u32[]{:S(2)}, u32[]{:S(2)}) collective-permute-start(bf16[19,2,64,128]{3,2,1,0:T(8,128)(2,1)S(1)} %pad_maximum_fusion.refs_0_), channel_id=1, source_target_pairs={{0,1},{1,0},{2,3},{3,2},{4,5},{5,4},{6,7},{7,6},{8,9},{9,8},{10,11... | collective-permute-start | bytes 1867784 | tf_op jit(solution)/shard_map/ppermute | solution.py:140
  60.6 13.2 %collective-permute-start.5 = (bf16[16,2,64,128]{3,2,1,0:T(8,128)(2,1)S(1)}, bf16[16,2,64,128]{3,2,1,0:T(8,128)(2,1)S(1)}, u32[]{:S(2)}, u32[]{:S(2)}) collective-permute-start(bf16[16,2,64,128]{3,2,1,0:T(8,128)(2,1)S(1)} %collective-permute-done.refs_1_), channel_id=1, source_target_pairs={{0,16},{1,49},{16,32},{17,1},{32,48},{33,17},{48,0},{49,33},{2,18}... | collective-permute-start | bytes 1572872 | tf_op jit(solution)/shard_map/ppermute | solution.py:146
  62.6 16.0 %collective-permute-start.2 = (bf16[16,2,64,128]{3,2,1,0:T(8,128)(2,1)}, bf16[16,2,64,128]{3,2,1,0:T(8,128)(2,1)S(1)}, u32[]{:S(2)}, u32[]{:S(2)}) collective-permute-start(bf16[16,2,64,128]{3,2,1,0:T(8,128)(2,1)} %bitcast.31), channel_id=1, source_target_pairs={{0,48},{1,17},{16,0},{17,33},{32,16},{33,49},{48,32},{49,1},{2,50}... | collective-permute-start | bytes 1572872 | tf_op jit(solution)/shard_map/ppermute | solution.py:146
  65.9 12.7 %collective-permute-start.4 = (bf16[16,2,64,128]{3,2,1,0:T(8,128)(2,1)S(1)}, bf16[16,2,64,128]{3,2,1,0:T(8,128)(2,1)}, u32[]{:S(2)}, u32[]{:S(2)}) collective-permute-start(bf16[16,2,64,128]{3,2,1,0:T(8,128)(2,1)S(1)} %collective-permute-done.refs_1_), channel_id=1, source_target_pairs={{0,1},{1,0},{2,3},{3,2},{4,5},{5,4},{6,7},{7,6},{8,9},{9,8},{10,11... | collective-permute-start | bytes 1572872 | tf_op jit(solution)/shard_map/ppermute | solution.py:140
  73.7 6.8 %collective-permute-start.7 = (bf16[16,2,64,128]{3,2,1,0:T(8,128)(2,1)S(1)}, bf16[16,2,64,128]{3,2,1,0:T(8,128)(2,1)}, u32[]{:S(2)}, u32[]{:S(2)}) collective-permute-start(bf16[16,2,64,128]{3,2,1,0:T(8,128)(2,1)S(1)} %collective-permute-done.5.refs_3_), channel_id=1, source_target_pairs={{0,1},{1,0},{2,3},{3,2},{4,5},{5,4},{6,7},{7,6},{8,9},{9,8},{10,11... | collective-permute-start | bytes 1572872 | tf_op jit(solution)/shard_map/ppermute | solution.py:140
  78.6 3.9 %collective-permute-start.6 = (bf16[16,2,64,128]{3,2,1,0:T(8,128)(2,1)S(1)}, bf16[16,2,64,128]{3,2,1,0:T(8,128)(2,1)}, u32[]{:S(2)}, u32[]{:S(2)}) collective-permute-start(bf16[16,2,64,128]{3,2,1,0:T(8,128)(2,1)S(1)} %collective-permute-done.2.refs_2_), channel_id=1, source_target_pairs={{0,1},{1,0},{2,3},{3,2},{4,5},{5,4},{6,7},{7,6},{8,9},{9,8},{10,11... | collective-permute-start | bytes 1572872 | tf_op jit(solution)/shard_map/ppermute | solution.py:140

commit v10 on v9

--- a/solution.py
+++ b/solution.py
@@ -155,6 +155,7 @@
     sent = keyvals.reshape(2 * STRIP, heads, HEAD_SIZE).transpose(1, 0, 2)
     sent = jnp.concatenate([sent, jnp.broadcast_to(lists[None], (heads,) + lists.shape)], axis=1)
     received = lax.all_to_all(sent, Y_RING, split_axis=0, concat_axis=0, tiled=True)
+    received, queries = lax.optimization_barrier((received, queries))
     local = received[:, : 2 * STRIP].reshape(2, 2, 2, 2, STRIP, HEAD_SIZE).transpose(0, 2, 3, 1, 4, 5)
     local = local.reshape(4, 2, HALF, HEAD_SIZE)
 
@@ -162,14 +163,14 @@
     copies = jnp.broadcast_to(summary[None], (lax.axis_size(Z),) + summary.shape)
     column = lax.all_to_all(copies, Z_RING, split_axis=0, concat_axis=0, tiled=True)
     column = column.reshape((-1,) + summary.shape[1:])
-    column, queries, odd = lax.optimization_barrier((column, queries, local[1::2]))
+    sent_q = queries.reshape(STRIP, heads, GROUP * HEAD_SIZE).transpose(1, 0, 2)
+    column, sent_q, odd = lax.optimization_barrier((column, sent_q, local[1::2]))
 
     first = around(column, X, 1)
-    sent_q = queries.reshape(STRIP, heads, GROUP * HEAD_SIZE).transpose(1, 0, 2)
     q = lax.all_to_all(sent_q, Y_RING, split_axis=0, concat_axis=0, tiled=True)
     pairs = lax.axis_size(Z + (X,))
     before = lax.ppermute(odd[1], Z + (X,), [(i, i + 1) for i in range(pairs - 1)])
-    first, column, before = lax.optimization_barrier((first, column, before))
+    first, column = lax.optimization_barrier((first, column))
 
     far = around(first, X, 1)
     second = around(column, X, -1)

time: 117 us -> 116 us (level)
  transfers between devices with their start and end apart: 10 -> 10, of which waited for: 4 -> 5; matrix products, arithmetic and copies ran while one was open for 1% -> 1% of each run, Pallas kernels for 0% -> 0%
where the time goes in v10:
time: 116 us
  starting transfers between devices  41.6 us (36%)
  blocking collectives  36.4 us (31%)
  waiting for transfers between devices  21.9 us (19%)
  Pallas kernels  10.8 us (9%)
  local copies, waits for them, and re-layouts  3.76 us (3%)
    all_to_all x1, blocking collectives, body(): lax.all_to_all(result, Y_RING, split_axis=0, concat_axis=0, tiled=True)  22.3 us
    ppermute x4, starting transfers between devices, swap(): return lax.ppermute(array, axis, [(0, 1), (1, 0)])  16.9 us
    all_to_all x1, blocking collectives, body(): lax.all_to_all(sent, Y_RING, split_axis=0, concat_axis=0, tiled=True)  14.1 us
    all_to_all x1, waiting for transfers between devices, body(): lax.all_to_all(copies, Z_RING, split_axis=0, concat_axis=0, tiled=True)  11 us
    pallas_call x1, Pallas kernels, attention(): pl.pallas_call(attend, out_shape=jax.ShapeDtypeStruct(q.shape, q.dtype),...  10.8 us
    ppermute x3, starting transfers between devices, around(): return lax.ppermute(array, (axis, CORE), pairs)  9.66 us
    all_to_all x1, starting transfers between devices, body(): lax.all_to_all(copies, Z_RING, split_axis=0, concat_axis=0, tiled=True)  9.54 us
    ppermute x3, waiting for transfers between devices, around(): return lax.ppermute(array, (axis, CORE), pairs)  4.48 us
  transfers between devices with their start and end apart: 10, of which 5 were waited for; matrix products, arithmetic and copies ran while one was open for 1% of the time, Pallas kernels for 0%

profile of v10, /device:TPU:81, one launch (start us, length us, event | category | flops | bytes accessed | tf_op | source)
XLA Modules:
  0.0 115.7 jit_solution(5507103251846869848)
XLA Ops:
  0.0 0.7 convert.10
  0.7 0.1 copy.9
  0.8 0.9 copy.15
  1.9 14.1 %all_to_all.20 = bf16[8,80,128]{2,1,0:T(8,128)(2,1)S(1)} all-to-all(bf16[8,80,128]{2,1,0:T(8,128)(2,1)S(1)} %pad_maximum_fusion.1), channel_id=1, replica_groups=mesh['z2'=2,'z1'=2,'z0'=2,'x'=4,'y0'=2,'y2'=2,'y1'=2,'core'=2] {'y0','y1..., dimensions={0} | all-to-all | bytes 327680 | tf_op jit(solution)/shard_map/all_to_all | solution.py:157
  16.0 0.9 broadcast_in_dim.25
  16.9 9.5 %all-to-all-start.1 = ((bf16[8,2,2,64,128]{4,3,2,1,0:T(8,128)(2,1)}), bf16[8,2,2,64,128]{4,3,2,1,0:T(8,128)(2,1)S(1)}, u32[]{:S(2)}, u32[]{:S(2)}) async-start(bf16[8,2,2,64,128]{4,3,2,1,0:T(8,128)(2,1)} %broadcast_in_dim.25), calls=%async_computation.1 | async-start | bytes 1048576 | tf_op jit(solution)/shard_map/all_to_all | solution.py:164
  26.5 0.8 copy.18
  27.3 11.0 %all-to-all-done.1 = bf16[8,2,2,64,128]{4,3,2,1,0:T(8,128)(2,1)S(1)} async-done(((bf16[8,2,2,64,128]{4,3,2,1,0:T(8,128)(2,1)}), bf16[8,2,2,64,128]{4,3,2,1,0:T(8,128)(2,1)S(1)}, u32[]{:S(2)}, u32[]{:S(2)}) %all-to-all-start.1) | async-done | bytes 524320 | tf_op jit(solution)/shard_map/all_to_all | solution.py:164
  38.3 4.4 %collective-permute-start = (bf16[16,2,64,128]{3,2,1,0:T(8,128)(2,1)S(1)}, bf16[16,2,64,128]{3,2,1,0:T(8,128)(2,1)S(1)}, u32[]{:S(2)}, u32[]{:S(2)}) collective-permute-start(bf16[16,2,64,128]{3,2,1,0:T(8,128)(2,1)S(1)} %bitcast.29), channel_id=1, source_target_pairs={{0,16},{1,49},{16,32},{17,1},{32,48},{33,17},{48,0},{49,33},{2,18}... | collective-permute-start | bytes 1572872 | tf_op jit(solution)/shard_map/ppermute | solution.py:146
  42.7 3.6 %all-to-all-start.2 = ((bf16[8,32,1024]{2,1,0:T(8,128)(2,1)}), bf16[8,32,1024]{2,1,0:T(8,128)(2,1)S(1)}, u32[]{:S(2)}, u32[]{:S(2)}) async-start(bf16[8,32,1024]{2,1,0:T(8,128)(2,1)} %bitcast.27), calls=%async_computation.2 | async-start | bytes 1048576 | tf_op jit(solution)/shard_map/all_to_all | solution.py:170
  46.4 1.9 %collective-permute-start.2 = (bf16[2,64,128]{2,1,0:T(8,128)(2,1)S(1)}, bf16[2,64,128]{2,1,0:T(8,128)(2,1)S(1)}, u32[]{:S(2)}, u32[]{:S(2)}) collective-permute-start(bf16[2,64,128]{2,1,0:T(8,128)(2,1)S(1)} %slice_bitcast_fusion), channel_id=1, source_target_pairs={{0,16},{16,32},{32,48},{48,64},{64,80},{80,96},{96,112},{112,128},... | collective-permute-start | bytes 98312 | tf_op jit(solution)/shard_map/ppermute | solution.py:172
  48.3 0.5 collective-permute-done.refs_1_
  48.8 4.4 %collective-permute-done.2 = bf16[2,64,128]{2,1,0:T(8,128)(2,1)S(1)} collective-permute-done((bf16[2,64,128]{2,1,0:T(8,128)(2,1)S(1)}, bf16[2,64,128]{2,1,0:T(8,128)(2,1)S(1)}, u32[]{:S(2)}, u32[]{:S(2)}) %collective-permute-start.2) | collective-permute-done | bytes 32800 | tf_op jit(solution)/shard_map/ppermute | solution.py:172
  53.3 6.4 %collective-permute-start.3 = (bf16[19,2,64,128]{3,2,1,0:T(8,128)(2,1)S(1)}, bf16[19,2,64,128]{3,2,1,0:T(8,128)(2,1)S(1)}, u32[]{:S(2)}, u32[]{:S(2)}) collective-permute-start(bf16[19,2,64,128]{3,2,1,0:T(8,128)(2,1)S(1)} %pad_maximum_fusion.refs_0_), channel_id=1, source_target_pairs={{0,1},{1,0},{2,3},{3,2},{4,5},{5,4},{6,7},{7,6},{8,9},{9,8},{10,11... | collective-permute-start | bytes 1867784 | tf_op jit(solution)/shard_map/ppermute | solution.py:140
  59.7 2.0 %collective-permute-start.5 = (bf16[16,2,64,128]{3,2,1,0:T(8,128)(2,1)S(1)}, bf16[16,2,64,128]{3,2,1,0:T(8,128)(2,1)S(1)}, u32[]{:S(2)}, u32[]{:S(2)}) collective-permute-start(bf16[16,2,64,128]{3,2,1,0:T(8,128)(2,1)S(1)} %collective-permute-done.refs_1_), channel_id=1, source_target_pairs={{0,16},{1,49},{16,32},{17,1},{32,48},{33,17},{48,0},{49,33},{2,18}... | collective-permute-start | bytes 1572872 | tf_op jit(solution)/shard_map/ppermute | solution.py:146
  61.7 3.3 %collective-permute-start.1 = (bf16[16,2,64,128]{3,2,1,0:T(8,128)(2,1)}, bf16[16,2,64,128]{3,2,1,0:T(8,128)(2,1)S(1)}, u32[]{:S(2)}, u32[]{:S(2)}) collective-permute-start(bf16[16,2,64,128]{3,2,1,0:T(8,128)(2,1)} %bitcast.31), channel_id=1, source_target_pairs={{0,48},{1,17},{16,0},{17,33},{32,16},{33,49},{48,32},{49,1},{2,50}... | collective-permute-start | bytes 1572872 | tf_op jit(solution)/shard_map/ppermute | solution.py:146
  65.0 3.7 %collective-permute-start.4 = (bf16[16,2,64,128]{3,2,1,0:T(8,128)(2,1)S(1)}, bf16[16,2,64,128]{3,2,1,0:T(8,128)(2,1)}, u32[]{:S(2)}, u32[]{:S(2)}) collective-permute-start(bf16[16,2,64,128]{3,2,1,0:T(8,128)(2,1)S(1)} %collective-permute-done.refs_1_), channel_id=1, source_target_pairs={{0,1},{1,0},{2,3},{3,2},{4,5},{5,4},{6,7},{7,6},{8,9},{9,8},{10,11... | collective-permute-start | bytes 1572872 | tf_op jit(solution)/shard_map/ppermute | solution.py:140
  68.9 3.9 %collective-permute-done.5.refs_3_ = bf16[16,2,64,128]{3,2,1,0:T(8,128)(2,1)S(1)} collective-permute-done((bf16[16,2,64,128]{3,2,1,0:T(8,128)(2,1)S(1)}, bf16[16,2,64,128]{3,2,1,0:T(8,128)(2,1)S(1)}, u32[]{:S(2)}, u32[]{:S(2)}) %collective-permute-start.5) | collective-permute-done | bytes 524320 | tf_op jit(solution)/shard_map/ppermute | solution.py:146
  72.9 4.8 %collective-permute-start.7 = (bf16[16,2,64,128]{3,2,1,0:T(8,128)(2,1)S(1)}, bf16[16,2,64,128]{3,2,1,0:T(8,128)(2,1)}, u32[]{:S(2)}, u32[]{:S(2)}) collective-permute-start(bf16[16,2,64,128]{3,2,1,0:T(8,128)(2,1)S(1)} %collective-permute-done.5.refs_3_), channel_id=1, source_target_pairs={{0,1},{1,0},{2,3},{3,2},{4,5},{5,4},{6,7},{7,6},{8,9},{9,8},{10,11... | collective-permute-start | bytes 1572872 | tf_op jit(solution)/shard_map/ppermute | solution.py:140
  77.8 1.9 %collective-permute-start.6 = (bf16[16,2,64,128]{3,2,1,0:T(8,128)(2,1)S(1)}, bf16[16,2,64,128]{3,2,1,0:T(8,128)(2,1)}, u32[]{:S(2)}, u32[]{:S(2)}) collective-permute-start(bf16[16,2,64,128]{3,2,1,0:T(8,128)(2,1)S(1)} %collective-permute-done.1.refs_2_), channel_id=1, source_target_pairs={{0,1},{1,0},{2,3},{3,2},{4,5},{5,4},{6,7},{7,6},{8,9},{9,8},{10,11... | collective-permute-start | bytes 1572872 | tf_op jit(solution)/shard_map/ppermute | solution.py:140
  79.7 2.0 %collective-permute-done.6.refs_6_ = bf16[16,2,64,128]{3,2,1,0:T(8,128)(2,1)} collective-permute-done((bf16[16,2,64,128]{3,2,1,0:T(8,128)(2,1)S(1)}, bf16[16,2,64,128]{3,2,1,0:T(8,128)(2,1)}, u32[]{:S(2)}, u32[]{:S(2)}) %collective-permute-start.6) | collective-permute-done | bytes 524320 | tf_op jit(solution)/shard_map/ppermute | solution.py:140
  81.7 10.8 %shard_map.46 = bf16[8,32,1024]{2,1,0:T(8,128)(2,1)S(1)} custom-call(s32[1]{0:T(128)} %bitcast.core_ref, s32[4,17]{1,0:T(4,128)S(1)} %pad_add_fusion.entries, bf16[8,32,1024]{2,1,0:T(8,128)(2,1)S(1)} %all-to-all-done.2.q_ref, bf16[19,2,64,128]{3,2,1,0:T(8,128)(2,1)S(1)} %pad_maximum_fusion.refs_0_, ...), custom_call_target="tpu_custom_call" | custom-call | flops 2147483648 | bytes 8388608 | tf_op jit(solution)/shard_map/pallas_call | solution.py:110
  92.6 22.3 %all_to_all.21 = bf16[8,32,1024]{2,1,0:T(8,128)(2,1)S(1)} all-to-all(bf16[8,32,1024]{2,1,0:T(8,128)(2,1)S(1)} %shard_map.46), channel_id=1, replica_groups=mesh['z2'=2,'z1'=2,'z0'=2,'x'=4,'y0'=2,'y2'=2,'y1'=2,'core'=2] {'y0','y1..., dimensions={0} | all-to-all | bytes 1048576 | tf_op jit(solution)/shard_map/all_to_all | solution.py:187
  114.9 0.8 copy.14
  (28 shorter events, 0.5 us)
Async XLA Ops:
  0.0 0.7 copy-start.2
  16.9 9.6 %copy-start.1 = (bf16[32,8192]{1,0:T(8,128)(2,1)S(1)}, bf16[32,8192]{1,0:T(8,128)(2,1)}, u32[]{:S(2)}) copy-start(bf16[32,8192]{1,0:T(8,128)(2,1)} %param.4) | copy-start | bytes 1572868
  16.9 21.4 %all-to-all-start.1 = ((bf16[8,2,2,64,128]{4,3,2,1,0:T(8,128)(2,1)}), bf16[8,2,2,64,128]{4,3,2,1,0:T(8,128)(2,1)S(1)}, u32[]{:S(2)}, u32[]{:S(2)}) async-start(bf16[8,2,2,64,128]{4,3,2,1,0:T(8,128)(2,1)} %broadcast_in_dim.25), calls=%async_computation.1 | async-start | bytes 1048576 | tf_op jit(solution)/shard_map/all_to_all | solution.py:164
  38.3 14.9 %copy-start = (bf16[8,2,2,64,128]{4,3,2,1,0:T(8,128)(2,1)}, bf16[8,2,2,64,128]{4,3,2,1,0:T(8,128)(2,1)S(1)}, u32[]{:S(2)}) copy-start(bf16[8,2,2,64,128]{4,3,2,1,0:T(8,128)(2,1)S(1)} %all-to-all-done.1) | copy-start | bytes 1572868
  38.3 10.5 %collective-permute-start = (bf16[16,2,64,128]{3,2,1,0:T(8,128)(2,1)S(1)}, bf16[16,2,64,128]{3,2,1,0:T(8,128)(2,1)S(1)}, u32[]{:S(2)}, u32[]{:S(2)}) collective-permute-start(bf16[16,2,64,128]{3,2,1,0:T(8,128)(2,1)S(1)} %bitcast.29), channel_id=1, source_target_pairs={{0,16},{1,49},{16,32},{17,1},{32,48},{33,17},{48,0},{49,33},{2,18}... | collective-permute-start | bytes 1572872 | tf_op jit(solution)/shard_map/ppermute | solution.py:146
  42.7 35.0 %all-to-all-start.2 = ((bf16[8,32,1024]{2,1,0:T(8,128)(2,1)}), bf16[8,32,1024]{2,1,0:T(8,128)(2,1)S(1)}, u32[]{:S(2)}, u32[]{:S(2)}) async-start(bf16[8,32,1024]{2,1,0:T(8,128)(2,1)} %bitcast.27), calls=%async_computation.2 | async-start | bytes 1048576 | tf_op jit(solution)/shard_map/all_to_all | solution.py:170
  46.4 6.9 %collective-permute-start.2 = (bf16[2,64,128]{2,1,0:T(8,128)(2,1)S(1)}, bf16[2,64,128]{2,1,0:T(8,128)(2,1)S(1)}, u32[]{:S(2)}, u32[]{:S(2)}) collective-permute-start(bf16[2,64,128]{2,1,0:T(8,128)(2,1)S(1)} %slice_bitcast_fusion), channel_id=1, source_target_pairs={{0,16},{16,32},{32,48},{48,64},{64,80},{80,96},{96,112},{112,128},... | collective-permute-start | bytes 98312 | tf_op jit(solution)/shard_map/ppermute | solution.py:172
  53.3 24.5 %collective-permute-start.3 = (bf16[19,2,64,128]{3,2,1,0:T(8,128)(2,1)S(1)}, bf16[19,2,64,128]{3,2,1,0:T(8,128)(2,1)S(1)}, u32[]{:S(2)}, u32[]{:S(2)}) collective-permute-start(bf16[19,2,64,128]{3,2,1,0:T(8,128)(2,1)S(1)} %pad_maximum_fusion.refs_0_), channel_id=1, source_target_pairs={{0,1},{1,0},{2,3},{3,2},{4,5},{5,4},{6,7},{7,6},{8,9},{9,8},{10,11... | collective-permute-start | bytes 1867784 | tf_op jit(solution)/shard_map/ppermute | solution.py:140
  59.7 13.2 %collective-permute-start.5 = (bf16[16,2,64,128]{3,2,1,0:T(8,128)(2,1)S(1)}, bf16[16,2,64,128]{3,2,1,0:T(8,128)(2,1)S(1)}, u32[]{:S(2)}, u32[]{:S(2)}) collective-permute-start(bf16[16,2,64,128]{3,2,1,0:T(8,128)(2,1)S(1)} %collective-permute-done.refs_1_), channel_id=1, source_target_pairs={{0,16},{1,49},{16,32},{17,1},{32,48},{33,17},{48,0},{49,33},{2,18}... | collective-permute-start | bytes 1572872 | tf_op jit(solution)/shard_map/ppermute | solution.py:146
  61.7 16.0 %collective-permute-start.1 = (bf16[16,2,64,128]{3,2,1,0:T(8,128)(2,1)}, bf16[16,2,64,128]{3,2,1,0:T(8,128)(2,1)S(1)}, u32[]{:S(2)}, u32[]{:S(2)}) collective-permute-start(bf16[16,2,64,128]{3,2,1,0:T(8,128)(2,1)} %bitcast.31), channel_id=1, source_target_pairs={{0,48},{1,17},{16,0},{17,33},{32,16},{33,49},{48,32},{49,1},{2,50}... | collective-permute-start | bytes 1572872 | tf_op jit(solution)/shard_map/ppermute | solution.py:146
  65.0 12.7 %collective-permute-start.4 = (bf16[16,2,64,128]{3,2,1,0:T(8,128)(2,1)S(1)}, bf16[16,2,64,128]{3,2,1,0:T(8,128)(2,1)}, u32[]{:S(2)}, u32[]{:S(2)}) collective-permute-start(bf16[16,2,64,128]{3,2,1,0:T(8,128)(2,1)S(1)} %collective-permute-done.refs_1_), channel_id=1, source_target_pairs={{0,1},{1,0},{2,3},{3,2},{4,5},{5,4},{6,7},{7,6},{8,9},{9,8},{10,11... | collective-permute-start | bytes 1572872 | tf_op jit(solution)/shard_map/ppermute | solution.py:140
  72.9 6.8 %collective-permute-start.7 = (bf16[16,2,64,128]{3,2,1,0:T(8,128)(2,1)S(1)}, bf16[16,2,64,128]{3,2,1,0:T(8,128)(2,1)}, u32[]{:S(2)}, u32[]{:S(2)}) collective-permute-start(bf16[16,2,64,128]{3,2,1,0:T(8,128)(2,1)S(1)} %collective-permute-done.5.refs_3_), channel_id=1, source_target_pairs={{0,1},{1,0},{2,3},{3,2},{4,5},{5,4},{6,7},{7,6},{8,9},{9,8},{10,11... | collective-permute-start | bytes 1572872 | tf_op jit(solution)/shard_map/ppermute | solution.py:140
  77.8 3.9 %collective-permute-start.6 = (bf16[16,2,64,128]{3,2,1,0:T(8,128)(2,1)S(1)}, bf16[16,2,64,128]{3,2,1,0:T(8,128)(2,1)}, u32[]{:S(2)}, u32[]{:S(2)}) collective-permute-start(bf16[16,2,64,128]{3,2,1,0:T(8,128)(2,1)S(1)} %collective-permute-done.1.refs_2_), channel_id=1, source_target_pairs={{0,1},{1,0},{2,3},{3,2},{4,5},{5,4},{6,7},{7,6},{8,9},{9,8},{10,11... | collective-permute-start | bytes 1572872 | tf_op jit(solution)/shard_map/ppermute | solution.py:140

commit v11 on v10

--- a/solution.py
+++ b/solution.py
@@ -25,8 +25,8 @@
 
 
 def attend(core_ref, entries, q_ref, *refs):
-    columns = refs[:8]
-    out_ref, table, keys, values, scores, peaks, weights, sems = refs[8:]
+    columns, odds = refs[:8], refs[8:10]
+    out_ref, table, keys, values, scores, peaks, weights, sems = refs[10:]
     core = core_ref[0]
     evens = table.shape[1] - ODD
     per_column = evens // 4
@@ -40,8 +40,8 @@
     for rc in range(2):
         side = jnp.bitwise_xor(core, rc)
         for source, relative in zip(columns[rc * 4 : rc * 4 + 4], (0, 3 - 2 * side, 1 + 2 * side, 2)):
-            bring(source.at[pl.ds(0, per_column)], table.at[rc, pl.ds(relative * per_column, per_column)])
-        bring(columns[rc * 4].at[pl.ds(per_column, ODD)], table.at[rc, pl.ds(evens, ODD)])
+            bring(source, table.at[rc, pl.ds(relative * per_column, per_column)])
+        bring(odds[rc], table.at[rc, pl.ds(evens, ODD)])
     for copy in copies:
         copy.wait()
 
@@ -102,7 +102,7 @@
     lax.fori_loop(0, 4, one_block, 0)
 
 
-def attention(core, entries, q, columns, interpret=False):
+def attention(core, entries, q, columns, odds, interpret=False):
     evens = 4 * columns[1].shape[0]
     smem = pl.BlockSpec(memory_space=pltpu.SMEM)
     vmem = pl.BlockSpec(memory_space=pltpu.VMEM)
@@ -110,7 +110,7 @@
     return pl.pallas_call(
         attend,
         out_shape=jax.ShapeDtypeStruct(q.shape, q.dtype),
-        in_specs=[smem, smem, vmem] + [hbm] * 8,
+        in_specs=[smem, smem, vmem] + [hbm] * 10,
         out_specs=vmem,
         scratch_shapes=[
             pltpu.VMEM((2, evens + ODD, 2, HALF, HEAD_SIZE), jnp.bfloat16),
@@ -124,7 +124,7 @@
         compiler_params=pltpu.CompilerParams(vmem_limit_bytes=40 * 2**20),
         cost_estimate=pl.CostEstimate(flops=2**31, bytes_accessed=8 * 2**20, transcendentals=2**22),
         interpret=interpret,
-    )(core, entries, q, *columns)
+    )(core, entries, q, *columns, *odds)
 
 
 def table_entries(z, x, listed, evens):
@@ -174,16 +174,13 @@
 
     far = around(first, X, 1)
     second = around(column, X, -1)
-    own = jnp.concatenate([column, before[None], odd])
-    own_swapped = swap(own, CORE)
-    first_swapped = swap(first, CORE)
     listed = received[:: heads // 2, 2 * STRIP : 2 * STRIP + 2, : MAXB + 1].astype(jnp.int32).reshape(4, MAXB + 1)
     entries = table_entries(z, x, listed, 4 * column.shape[0])
-    second, q, entries, own_swapped, first_swapped = lax.optimization_barrier(
-        (second, q, entries, own_swapped, first_swapped)
-    )
-    columns = [own, first, second, far, own_swapped, first_swapped, swap(second, CORE), swap(far, CORE)]
-    result = attention(core[None], entries, q, columns)
+    odd = jnp.concatenate([before[None], odd])
+    second, q, entries, other_odd = lax.optimization_barrier((second, q, entries, swap(odd, CORE)))
+    columns = [column, first, second, far]
+    columns += [swap(piece, CORE) for piece in columns]
+    result = attention(core[None], entries, q, columns, [odd, other_odd])
     result = lax.all_to_all(result, Y_RING, split_axis=0, concat_axis=0, tiled=True)
     return result.transpose(1, 0, 2).reshape(STRIP, heads * GROUP * HEAD_SIZE)
 

time: 116 us -> 113 us (0.974)
  the two profiles are of different devices: /device:TPU:81 before, /device:TPU:23 now
where the time goes in v11:
time: 113 us; the launch traced here: 112 us
  starting transfers between devices  40.2 us (36%)
  blocking collectives  33.4 us (30%)
  waiting for transfers between devices  22.8 us (20%)
  Pallas kernels  10.8 us (10%)
  local copies, waits for them, and re-layouts  3.76 us (3%)
    all_to_all x1, blocking collectives, body(): lax.all_to_all(result, Y_RING, split_axis=0, concat_axis=0, tiled=True)  19.3 us
    ppermute x5, starting transfers between devices, swap(): return lax.ppermute(array, axis, [(0, 1), (1, 0)])  16 us
    all_to_all x1, blocking collectives, body(): lax.all_to_all(sent, Y_RING, split_axis=0, concat_axis=0, tiled=True)  14.1 us
    all_to_all x1, waiting for transfers between devices, body(): lax.all_to_all(copies, Z_RING, split_axis=0, concat_axis=0, tiled=True)  12.7 us
    pallas_call x1, Pallas kernels, attention(): pl.pallas_call(attend, out_shape=jax.ShapeDtypeStruct(q.shape, q.dtype),...  10.8 us
    all_to_all x1, starting transfers between devices, body(): lax.all_to_all(copies, Z_RING, split_axis=0, concat_axis=0, tiled=True)  10.2 us
    ppermute x3, starting transfers between devices, around(): return lax.ppermute(array, (axis, CORE), pairs)  7.72 us
    ppermute x3, waiting for transfers between devices, around(): return lax.ppermute(array, (axis, CORE), pairs)  5.01 us
  transfers between devices with their start and end apart: 11, of which 4 were waited for; matrix products, arithmetic and copies ran while one was open for 1% of the time, Pallas kernels for 0%

profile of v11, /device:TPU:23, one launch (start us, length us, event | category | flops | bytes accessed | tf_op | source)
XLA Modules:
  0.0 112.1 jit_solution(4451291090514431239)
XLA Ops:
  0.0 0.7 convert.10
  0.7 0.1 copy.9
  0.8 0.9 copy.15
  1.9 14.1 %all_to_all.20 = bf16[8,80,128]{2,1,0:T(8,128)(2,1)S(1)} all-to-all(bf16[8,80,128]{2,1,0:T(8,128)(2,1)S(1)} %pad_maximum_fusion), channel_id=1, replica_groups=mesh['z2'=2,'z1'=2,'z0'=2,'x'=4,'y0'=2,'y2'=2,'y1'=2,'core'=2] {'y0','y1..., dimensions={0} | all-to-all | bytes 327680 | tf_op jit(solution)/shard_map/all_to_all | solution.py:157
  16.0 0.9 broadcast_in_dim.25
  16.9 10.2 %all-to-all-start.1 = ((bf16[8,2,2,64,128]{4,3,2,1,0:T(8,128)(2,1)}), bf16[8,2,2,64,128]{4,3,2,1,0:T(8,128)(2,1)S(1)}, u32[]{:S(2)}, u32[]{:S(2)}) async-start(bf16[8,2,2,64,128]{4,3,2,1,0:T(8,128)(2,1)} %broadcast_in_dim.25), calls=%async_computation.1 | async-start | bytes 1048576 | tf_op jit(solution)/shard_map/all_to_all | solution.py:164
  27.1 0.8 copy.18
  28.0 12.7 %all-to-all-done.1 = bf16[8,2,2,64,128]{4,3,2,1,0:T(8,128)(2,1)S(1)} async-done(((bf16[8,2,2,64,128]{4,3,2,1,0:T(8,128)(2,1)}), bf16[8,2,2,64,128]{4,3,2,1,0:T(8,128)(2,1)S(1)}, u32[]{:S(2)}, u32[]{:S(2)}) %all-to-all-start.1) | async-done | bytes 524320 | tf_op jit(solution)/shard_map/all_to_all | solution.py:164
  40.7 2.4 %collective-permute-start = (bf16[16,2,64,128]{3,2,1,0:T(8,128)(2,1)S(1)}, bf16[16,2,64,128]{3,2,1,0:T(8,128)(2,1)S(1)}, u32[]{:S(2)}, u32[]{:S(2)}) collective-permute-start(bf16[16,2,64,128]{3,2,1,0:T(8,128)(2,1)S(1)} %bitcast.29), channel_id=1, source_target_pairs={{0,16},{1,49},{16,32},{17,1},{32,48},{33,17},{48,0},{49,33},{2,18}... | collective-permute-start | bytes 1572872 | tf_op jit(solution)/shard_map/ppermute | solution.py:146
  43.1 3.6 %all-to-all-start.2 = ((bf16[8,32,1024]{2,1,0:T(8,128)(2,1)}), bf16[8,32,1024]{2,1,0:T(8,128)(2,1)S(1)}, u32[]{:S(2)}, u32[]{:S(2)}) async-start(bf16[8,32,1024]{2,1,0:T(8,128)(2,1)} %bitcast.27), calls=%async_computation.2 | async-start | bytes 1048576 | tf_op jit(solution)/shard_map/all_to_all | solution.py:170
  46.8 5.0 %collective-permute-done.refs_1_ = bf16[16,2,64,128]{3,2,1,0:T(8,128)(2,1)S(1)} collective-permute-done((bf16[16,2,64,128]{3,2,1,0:T(8,128)(2,1)S(1)}, bf16[16,2,64,128]{3,2,1,0:T(8,128)(2,1)S(1)}, u32[]{:S(2)}, u32[]{:S(2)}) %collective-permute-start) | collective-permute-done | bytes 524320 | tf_op jit(solution)/shard_map/ppermute | solution.py:146
  51.8 1.9 %collective-permute-start.1 = (bf16[16,2,64,128]{3,2,1,0:T(8,128)(2,1)S(1)}, bf16[16,2,64,128]{3,2,1,0:T(8,128)(2,1)S(1)}, u32[]{:S(2)}, u32[]{:S(2)}) collective-permute-start(bf16[16,2,64,128]{3,2,1,0:T(8,128)(2,1)S(1)} %bitcast.30), channel_id=1, source_target_pairs={{0,48},{1,17},{16,0},{17,33},{32,16},{33,49},{48,32},{49,1},{2,50}... | collective-permute-start | bytes 1572872 | tf_op jit(solution)/shard_map/ppermute | solution.py:146
  53.7 3.4 %collective-permute-start.4 = (bf16[16,2,64,128]{3,2,1,0:T(8,128)(2,1)S(1)}, bf16[16,2,64,128]{3,2,1,0:T(8,128)(2,1)S(1)}, u32[]{:S(2)}, u32[]{:S(2)}) collective-permute-start(bf16[16,2,64,128]{3,2,1,0:T(8,128)(2,1)S(1)} %collective-permute-done.refs_1_), channel_id=1, source_target_pairs={{0,16},{1,49},{16,32},{17,1},{32,48},{33,17},{48,0},{49,33},{2,18}... | collective-permute-start | bytes 1572872 | tf_op jit(solution)/shard_map/ppermute | solution.py:146
  57.1 2.6 %collective-permute-start.2 = (bf16[2,64,128]{2,1,0:T(8,128)(2,1)S(1)}, bf16[2,64,128]{2,1,0:T(8,128)(2,1)S(1)}, u32[]{:S(2)}, u32[]{:S(2)}) collective-permute-start(bf16[2,64,128]{2,1,0:T(8,128)(2,1)S(1)} %slice_bitcast_fusion), channel_id=1, source_target_pairs={{0,16},{16,32},{32,48},{48,64},{64,80},{80,96},{96,112},{112,128},... | collective-permute-start | bytes 98312 | tf_op jit(solution)/shard_map/ppermute | solution.py:172
  59.8 3.4 %collective-permute-done.2 = bf16[2,64,128]{2,1,0:T(8,128)(2,1)S(1)} collective-permute-done((bf16[2,64,128]{2,1,0:T(8,128)(2,1)S(1)}, bf16[2,64,128]{2,1,0:T(8,128)(2,1)S(1)}, u32[]{:S(2)}, u32[]{:S(2)}) %collective-permute-start.2) | collective-permute-done | bytes 32800 | tf_op jit(solution)/shard_map/ppermute | solution.py:172
  63.2 7.4 %collective-permute-start.3 = (bf16[3,2,64,128]{3,2,1,0:T(8,128)(2,1)S(1)}, bf16[3,2,64,128]{3,2,1,0:T(8,128)(2,1)S(1)}, u32[]{:S(2)}, u32[]{:S(2)}) collective-permute-start(bf16[3,2,64,128]{3,2,1,0:T(8,128)(2,1)S(1)} %pad_maximum_fusion.1.refs_8_), channel_id=1, source_target_pairs={{0,1},{1,0},{2,3},{3,2},{4,5},{5,4},{6,7},{7,6},{8,9},{9,8},{10,11... | collective-permute-start | bytes 294920 | tf_op jit(solution)/shard_map/ppermute | solution.py:140
  70.7 1.9 %collective-permute-start.5 = (bf16[16,2,64,128]{3,2,1,0:T(8,128)(2,1)S(1)}, bf16[16,2,64,128]{3,2,1,0:T(8,128)(2,1)S(1)}, u32[]{:S(2)}, u32[]{:S(2)}) collective-permute-start(bf16[16,2,64,128]{3,2,1,0:T(8,128)(2,1)S(1)} %bitcast.31), channel_id=1, source_target_pairs={{0,1},{1,0},{2,3},{3,2},{4,5},{5,4},{6,7},{7,6},{8,9},{9,8},{10,11... | collective-permute-start | bytes 1572872 | tf_op jit(solution)/shard_map/ppermute | solution.py:140
  72.6 2.4 %collective-permute-start.6 = (bf16[16,2,64,128]{3,2,1,0:T(8,128)(2,1)S(1)}, bf16[16,2,64,128]{3,2,1,0:T(8,128)(2,1)}, u32[]{:S(2)}, u32[]{:S(2)}) collective-permute-start(bf16[16,2,64,128]{3,2,1,0:T(8,128)(2,1)S(1)} %collective-permute-done.refs_1_), channel_id=1, source_target_pairs={{0,1},{1,0},{2,3},{3,2},{4,5},{5,4},{6,7},{7,6},{8,9},{9,8},{10,11... | collective-permute-start | bytes 1572872 | tf_op jit(solution)/shard_map/ppermute | solution.py:140
  75.1 1.9 %collective-permute-start.7 = (bf16[16,2,64,128]{3,2,1,0:T(8,128)(2,1)S(1)}, bf16[16,2,64,128]{3,2,1,0:T(8,128)(2,1)}, u32[]{:S(2)}, u32[]{:S(2)}) collective-permute-start(bf16[16,2,64,128]{3,2,1,0:T(8,128)(2,1)S(1)} %collective-permute-done.1.refs_2_), channel_id=1, source_target_pairs={{0,1},{1,0},{2,3},{3,2},{4,5},{5,4},{6,7},{7,6},{8,9},{9,8},{10,11... | collective-permute-start | bytes 1572872 | tf_op jit(solution)/shard_map/ppermute | solution.py:140
  77.0 2.4 %collective-permute-start.8 = (bf16[16,2,64,128]{3,2,1,0:T(8,128)(2,1)S(1)}, bf16[16,2,64,128]{3,2,1,0:T(8,128)(2,1)}, u32[]{:S(2)}, u32[]{:S(2)}) collective-permute-start(bf16[16,2,64,128]{3,2,1,0:T(8,128)(2,1)S(1)} %collective-permute-done.4.refs_3_), channel_id=1, source_target_pairs={{0,1},{1,0},{2,3},{3,2},{4,5},{5,4},{6,7},{7,6},{8,9},{9,8},{10,11... | collective-permute-start | bytes 1572872 | tf_op jit(solution)/shard_map/ppermute | solution.py:140
  79.5 1.6 %collective-permute-done.8.refs_7_ = bf16[16,2,64,128]{3,2,1,0:T(8,128)(2,1)} collective-permute-done((bf16[16,2,64,128]{3,2,1,0:T(8,128)(2,1)S(1)}, bf16[16,2,64,128]{3,2,1,0:T(8,128)(2,1)}, u32[]{:S(2)}, u32[]{:S(2)}) %collective-permute-start.8) | collective-permute-done | bytes 524320 | tf_op jit(solution)/shard_map/ppermute | solution.py:140
  81.1 10.8 %shard_map.46 = bf16[8,32,1024]{2,1,0:T(8,128)(2,1)S(1)} custom-call(s32[1]{0:T(128)} %bitcast.core_ref, s32[4,17]{1,0:T(4,128)S(1)} %pad_add_fusion.entries, bf16[8,32,1024]{2,1,0:T(8,128)(2,1)S(1)} %all-to-all-done.2.q_ref, bf16[16,2,64,128]{3,2,1,0:T(8,128)(2,1)S(1)} %bitcast.32, bf16[16,2,64,128]{3,2,1,0:T(8,128)(2,1)S(1)} %collective-permute-done.refs_1_, ...), custom_call_target="tpu_custom_call" | custom-call | flops 2147483648 | bytes 8388608 | tf_op jit(solution)/shard_map/pallas_call | solution.py:110
  91.9 19.3 %all_to_all.21 = bf16[8,32,1024]{2,1,0:T(8,128)(2,1)S(1)} all-to-all(bf16[8,32,1024]{2,1,0:T(8,128)(2,1)S(1)} %shard_map.46), channel_id=1, replica_groups=mesh['z2'=2,'z1'=2,'z0'=2,'x'=4,'y0'=2,'y2'=2,'y1'=2,'core'=2] {'y0','y1..., dimensions={0} | all-to-all | bytes 1048576 | tf_op jit(solution)/shard_map/all_to_all | solution.py:184
  111.2 0.8 copy.14
  (28 shorter events, 0.4 us)
Async XLA Ops:
  0.0 0.7 copy-start.1
  16.9 10.2 %copy-start = (bf16[32,8192]{1,0:T(8,128)(2,1)S(1)}, bf16[32,8192]{1,0:T(8,128)(2,1)}, u32[]{:S(2)}) copy-start(bf16[32,8192]{1,0:T(8,128)(2,1)} %param.4) | copy-start | bytes 1572868
  16.9 23.7 %all-to-all-start.1 = ((bf16[8,2,2,64,128]{4,3,2,1,0:T(8,128)(2,1)}), bf16[8,2,2,64,128]{4,3,2,1,0:T(8,128)(2,1)S(1)}, u32[]{:S(2)}, u32[]{:S(2)}) async-start(bf16[8,2,2,64,128]{4,3,2,1,0:T(8,128)(2,1)} %broadcast_in_dim.25), calls=%async_computation.1 | async-start | bytes 1048576 | tf_op jit(solution)/shard_map/all_to_all | solution.py:164
  40.7 11.1 %collective-permute-start = (bf16[16,2,64,128]{3,2,1,0:T(8,128)(2,1)S(1)}, bf16[16,2,64,128]{3,2,1,0:T(8,128)(2,1)S(1)}, u32[]{:S(2)}, u32[]{:S(2)}) collective-permute-start(bf16[16,2,64,128]{3,2,1,0:T(8,128)(2,1)S(1)} %bitcast.29), channel_id=1, source_target_pairs={{0,16},{1,49},{16,32},{17,1},{32,48},{33,17},{48,0},{49,33},{2,18}... | collective-permute-start | bytes 1572872 | tf_op jit(solution)/shard_map/ppermute | solution.py:146
  43.1 31.9 %all-to-all-start.2 = ((bf16[8,32,1024]{2,1,0:T(8,128)(2,1)}), bf16[8,32,1024]{2,1,0:T(8,128)(2,1)S(1)}, u32[]{:S(2)}, u32[]{:S(2)}) async-start(bf16[8,32,1024]{2,1,0:T(8,128)(2,1)} %bitcast.27), calls=%async_computation.2 | async-start | bytes 1048576 | tf_op jit(solution)/shard_map/all_to_all | solution.py:170
  51.8 23.3 %collective-permute-start.1 = (bf16[16,2,64,128]{3,2,1,0:T(8,128)(2,1)S(1)}, bf16[16,2,64,128]{3,2,1,0:T(8,128)(2,1)S(1)}, u32[]{:S(2)}, u32[]{:S(2)}) collective-permute-start(bf16[16,2,64,128]{3,2,1,0:T(8,128)(2,1)S(1)} %bitcast.30), channel_id=1, source_target_pairs={{0,48},{1,17},{16,0},{17,33},{32,16},{33,49},{48,32},{49,1},{2,50}... | collective-permute-start | bytes 1572872 | tf_op jit(solution)/shard_map/ppermute | solution.py:146
  53.7 23.3 %collective-permute-start.4 = (bf16[16,2,64,128]{3,2,1,0:T(8,128)(2,1)S(1)}, bf16[16,2,64,128]{3,2,1,0:T(8,128)(2,1)S(1)}, u32[]{:S(2)}, u32[]{:S(2)}) collective-permute-start(bf16[16,2,64,128]{3,2,1,0:T(8,128)(2,1)S(1)} %collective-permute-done.refs_1_), channel_id=1, source_target_pairs={{0,16},{1,49},{16,32},{17,1},{32,48},{33,17},{48,0},{49,33},{2,18}... | collective-permute-start | bytes 1572872 | tf_op jit(solution)/shard_map/ppermute | solution.py:146
  57.1 6.1 %collective-permute-start.2 = (bf16[2,64,128]{2,1,0:T(8,128)(2,1)S(1)}, bf16[2,64,128]{2,1,0:T(8,128)(2,1)S(1)}, u32[]{:S(2)}, u32[]{:S(2)}) collective-permute-start(bf16[2,64,128]{2,1,0:T(8,128)(2,1)S(1)} %slice_bitcast_fusion), channel_id=1, source_target_pairs={{0,16},{16,32},{32,48},{48,64},{64,80},{80,96},{96,112},{112,128},... | collective-permute-start | bytes 98312 | tf_op jit(solution)/shard_map/ppermute | solution.py:172
  63.2 11.8 %collective-permute-start.3 = (bf16[3,2,64,128]{3,2,1,0:T(8,128)(2,1)S(1)}, bf16[3,2,64,128]{3,2,1,0:T(8,128)(2,1)S(1)}, u32[]{:S(2)}, u32[]{:S(2)}) collective-permute-start(bf16[3,2,64,128]{3,2,1,0:T(8,128)(2,1)S(1)} %pad_maximum_fusion.1.refs_8_), channel_id=1, source_target_pairs={{0,1},{1,0},{2,3},{3,2},{4,5},{5,4},{6,7},{7,6},{8,9},{9,8},{10,11... | collective-permute-start | bytes 294920 | tf_op jit(solution)/shard_map/ppermute | solution.py:140
  70.7 8.7 %collective-permute-start.5 = (bf16[16,2,64,128]{3,2,1,0:T(8,128)(2,1)S(1)}, bf16[16,2,64,128]{3,2,1,0:T(8,128)(2,1)S(1)}, u32[]{:S(2)}, u32[]{:S(2)}) collective-permute-start(bf16[16,2,64,128]{3,2,1,0:T(8,128)(2,1)S(1)} %bitcast.31), channel_id=1, source_target_pairs={{0,1},{1,0},{2,3},{3,2},{4,5},{5,4},{6,7},{7,6},{8,9},{9,8},{10,11... | collective-permute-start | bytes 1572872 | tf_op jit(solution)/shard_map/ppermute | solution.py:140
  72.6 6.8 %collective-permute-start.6 = (bf16[16,2,64,128]{3,2,1,0:T(8,128)(2,1)S(1)}, bf16[16,2,64,128]{3,2,1,0:T(8,128)(2,1)}, u32[]{:S(2)}, u32[]{:S(2)}) collective-permute-start(bf16[16,2,64,128]{3,2,1,0:T(8,128)(2,1)S(1)} %collective-permute-done.refs_1_), channel_id=1, source_target_pairs={{0,1},{1,0},{2,3},{3,2},{4,5},{5,4},{6,7},{7,6},{8,9},{9,8},{10,11... | collective-permute-start | bytes 1572872 | tf_op jit(solution)/shard_map/ppermute | solution.py:140
  75.1 4.4 %collective-permute-start.7 = (bf16[16,2,64,128]{3,2,1,0:T(8,128)(2,1)S(1)}, bf16[16,2,64,128]{3,2,1,0:T(8,128)(2,1)}, u32[]{:S(2)}, u32[]{:S(2)}) collective-permute-start(bf16[16,2,64,128]{3,2,1,0:T(8,128)(2,1)S(1)} %collective-permute-done.1.refs_2_), channel_id=1, source_target_pairs={{0,1},{1,0},{2,3},{3,2},{4,5},{5,4},{6,7},{7,6},{8,9},{9,8},{10,11... | collective-permute-start | bytes 1572872 | tf_op jit(solution)/shard_map/ppermute | solution.py:140
  77.0 4.1 %collective-permute-start.8 = (bf16[16,2,64,128]{3,2,1,0:T(8,128)(2,1)S(1)}, bf16[16,2,64,128]{3,2,1,0:T(8,128)(2,1)}, u32[]{:S(2)}, u32[]{:S(2)}) collective-permute-start(bf16[16,2,64,128]{3,2,1,0:T(8,128)(2,1)S(1)} %collective-permute-done.4.refs_3_), channel_id=1, source_target_pairs={{0,1},{1,0},{2,3},{3,2},{4,5},{5,4},{6,7},{7,6},{8,9},{9,8},{10,11... | collective-permute-start | bytes 1572872 | tf_op jit(solution)/shard_map/ppermute | solution.py:140

commit v12 on v11

--- a/solution.py
+++ b/solution.py
@@ -170,7 +170,7 @@
     q = lax.all_to_all(sent_q, Y_RING, split_axis=0, concat_axis=0, tiled=True)
     pairs = lax.axis_size(Z + (X,))
     before = lax.ppermute(odd[1], Z + (X,), [(i, i + 1) for i in range(pairs - 1)])
-    first, column = lax.optimization_barrier((first, column))
+    first, column, before = lax.optimization_barrier((first, column, before))
 
     far = around(first, X, 1)
     second = around(column, X, -1)

time: 113 us -> 114 us (level)
  the two profiles are of different devices: /device:TPU:23 before, /device:TPU:145 now
where the time goes in v12:
time: 114 us
  starting transfers between devices  40.2 us (35%)
  blocking collectives  36.4 us (32%)
  waiting for transfers between devices  21.3 us (19%)
  Pallas kernels  10.8 us (9%)
  local copies, waits for them, and re-layouts  3.76 us (3%)
    all_to_all x1, blocking collectives, body(): lax.all_to_all(result, Y_RING, split_axis=0, concat_axis=0, tiled=True)  22.3 us
    ppermute x5, starting transfers between devices, swap(): return lax.ppermute(array, axis, [(0, 1), (1, 0)])  15.2 us
    all_to_all x1, waiting for transfers between devices, body(): lax.all_to_all(copies, Z_RING, split_axis=0, concat_axis=0, tiled=True)  14.1 us
    all_to_all x1, blocking collectives, body(): lax.all_to_all(sent, Y_RING, split_axis=0, concat_axis=0, tiled=True)  14.1 us
    ppermute x3, starting transfers between devices, around(): return lax.ppermute(array, (axis, CORE), pairs)  10.9 us
    pallas_call x1, Pallas kernels, attention(): pl.pallas_call(attend, out_shape=jax.ShapeDtypeStruct(q.shape, q.dtype),...  10.8 us
    all_to_all x1, starting transfers between devices, body(): lax.all_to_all(copies, Z_RING, split_axis=0, concat_axis=0, tiled=True)  8.63 us
    ppermute x1, waiting for transfers between devices, body(): lax.ppermute(odd[1], Z + (X,), [(i, i + 1) for i in range(pairs - 1)])  5.13 us
  transfers between devices with their start and end apart: 11, of which 3 were waited for; matrix products, arithmetic and copies ran while one was open for 1% of the time, Pallas kernels for 0%

profile of v12, /device:TPU:145, one launch (start us, length us, event | category | flops | bytes accessed | tf_op | source)
XLA Modules:
  0.0 113.6 jit_solution(3150755569089868454)
XLA Ops:
  0.0 0.7 convert.10
  0.7 0.1 copy.9
  0.8 0.9 copy.15
  1.8 0.1 fusion.5
  1.9 14.1 %all_to_all.20 = bf16[8,80,128]{2,1,0:T(8,128)(2,1)S(1)} all-to-all(bf16[8,80,128]{2,1,0:T(8,128)(2,1)S(1)} %pad_maximum_fusion), channel_id=1, replica_groups=mesh['z2'=2,'z1'=2,'z0'=2,'x'=4,'y0'=2,'y2'=2,'y1'=2,'core'=2] {'y0','y1..., dimensions={0} | all-to-all | bytes 327680 | tf_op jit(solution)/shard_map/all_to_all | solution.py:157
  16.0 0.9 broadcast_in_dim.25
  16.9 8.6 %all-to-all-start.1 = ((bf16[8,2,2,64,128]{4,3,2,1,0:T(8,128)(2,1)}), bf16[8,2,2,64,128]{4,3,2,1,0:T(8,128)(2,1)S(1)}, u32[]{:S(2)}, u32[]{:S(2)}) async-start(bf16[8,2,2,64,128]{4,3,2,1,0:T(8,128)(2,1)} %broadcast_in_dim.25), calls=%async_computation.1 | async-start | bytes 1048576 | tf_op jit(solution)/shard_map/all_to_all | solution.py:164
  25.6 0.8 copy.18
  26.4 14.1 %all-to-all-done.1 = bf16[8,2,2,64,128]{4,3,2,1,0:T(8,128)(2,1)S(1)} async-done(((bf16[8,2,2,64,128]{4,3,2,1,0:T(8,128)(2,1)}), bf16[8,2,2,64,128]{4,3,2,1,0:T(8,128)(2,1)S(1)}, u32[]{:S(2)}, u32[]{:S(2)}) %all-to-all-start.1) | async-done | bytes 524320 | tf_op jit(solution)/shard_map/all_to_all | solution.py:164
  40.5 4.4 %collective-permute-start = (bf16[16,2,64,128]{3,2,1,0:T(8,128)(2,1)S(1)}, bf16[16,2,64,128]{3,2,1,0:T(8,128)(2,1)S(1)}, u32[]{:S(2)}, u32[]{:S(2)}) collective-permute-start(bf16[16,2,64,128]{3,2,1,0:T(8,128)(2,1)S(1)} %bitcast.29), channel_id=1, source_target_pairs={{0,16},{1,49},{16,32},{17,1},{32,48},{33,17},{48,0},{49,33},{2,18}... | collective-permute-start | bytes 1572872 | tf_op jit(solution)/shard_map/ppermute | solution.py:146
  44.9 3.6 %all-to-all-start.2 = ((bf16[8,32,1024]{2,1,0:T(8,128)(2,1)}), bf16[8,32,1024]{2,1,0:T(8,128)(2,1)S(1)}, u32[]{:S(2)}, u32[]{:S(2)}) async-start(bf16[8,32,1024]{2,1,0:T(8,128)(2,1)} %bitcast.27), calls=%async_computation.2 | async-start | bytes 1048576 | tf_op jit(solution)/shard_map/all_to_all | solution.py:170
  48.6 1.9 %collective-permute-start.1 = (bf16[2,64,128]{2,1,0:T(8,128)(2,1)S(1)}, bf16[2,64,128]{2,1,0:T(8,128)(2,1)S(1)}, u32[]{:S(2)}, u32[]{:S(2)}) collective-permute-start(bf16[2,64,128]{2,1,0:T(8,128)(2,1)S(1)} %slice_bitcast_fusion), channel_id=1, source_target_pairs={{0,16},{16,32},{32,48},{48,64},{64,80},{80,96},{96,112},{112,128},... | collective-permute-start | bytes 98312 | tf_op jit(solution)/shard_map/ppermute | solution.py:172
  50.5 5.1 %collective-permute-done.1 = bf16[2,64,128]{2,1,0:T(8,128)(2,1)S(1)} collective-permute-done((bf16[2,64,128]{2,1,0:T(8,128)(2,1)S(1)}, bf16[2,64,128]{2,1,0:T(8,128)(2,1)S(1)}, u32[]{:S(2)}, u32[]{:S(2)}) %collective-permute-start.1) | collective-permute-done | bytes 32800 | tf_op jit(solution)/shard_map/ppermute | solution.py:172
  55.6 1.9 %collective-permute-start.2 = (bf16[16,2,64,128]{3,2,1,0:T(8,128)(2,1)S(1)}, bf16[16,2,64,128]{3,2,1,0:T(8,128)(2,1)S(1)}, u32[]{:S(2)}, u32[]{:S(2)}) collective-permute-start(bf16[16,2,64,128]{3,2,1,0:T(8,128)(2,1)S(1)} %bitcast.30), channel_id=1, source_target_pairs={{0,48},{1,17},{16,0},{17,33},{32,16},{33,49},{48,32},{49,1},{2,50}... | collective-permute-start | bytes 1572872 | tf_op jit(solution)/shard_map/ppermute | solution.py:146
  57.6 4.6 %collective-permute-start.4 = (bf16[16,2,64,128]{3,2,1,0:T(8,128)(2,1)S(1)}, bf16[16,2,64,128]{3,2,1,0:T(8,128)(2,1)S(1)}, u32[]{:S(2)}, u32[]{:S(2)}) collective-permute-start(bf16[16,2,64,128]{3,2,1,0:T(8,128)(2,1)S(1)} %collective-permute-done.refs_1_), channel_id=1, source_target_pairs={{0,16},{1,49},{16,32},{17,1},{32,48},{33,17},{48,0},{49,33},{2,18}... | collective-permute-start | bytes 1572872 | tf_op jit(solution)/shard_map/ppermute | solution.py:146
  62.3 3.1 %collective-permute-start.3 = (bf16[3,2,64,128]{3,2,1,0:T(8,128)(2,1)S(1)}, bf16[3,2,64,128]{3,2,1,0:T(8,128)(2,1)S(1)}, u32[]{:S(2)}, u32[]{:S(2)}) collective-permute-start(bf16[3,2,64,128]{3,2,1,0:T(8,128)(2,1)S(1)} %pad_maximum_fusion.1.refs_8_), channel_id=1, source_target_pairs={{0,1},{1,0},{2,3},{3,2},{4,5},{5,4},{6,7},{7,6},{8,9},{9,8},{10,11... | collective-permute-start | bytes 294920 | tf_op jit(solution)/shard_map/ppermute | solution.py:140
  65.5 1.9 %collective-permute-start.5 = (bf16[16,2,64,128]{3,2,1,0:T(8,128)(2,1)S(1)}, bf16[16,2,64,128]{3,2,1,0:T(8,128)(2,1)S(1)}, u32[]{:S(2)}, u32[]{:S(2)}) collective-permute-start(bf16[16,2,64,128]{3,2,1,0:T(8,128)(2,1)S(1)} %bitcast.31), channel_id=1, source_target_pairs={{0,1},{1,0},{2,3},{3,2},{4,5},{5,4},{6,7},{7,6},{8,9},{9,8},{10,11... | collective-permute-start | bytes 1572872 | tf_op jit(solution)/shard_map/ppermute | solution.py:140
  67.4 2.4 %collective-permute-start.6 = (bf16[16,2,64,128]{3,2,1,0:T(8,128)(2,1)S(1)}, bf16[16,2,64,128]{3,2,1,0:T(8,128)(2,1)}, u32[]{:S(2)}, u32[]{:S(2)}) collective-permute-start(bf16[16,2,64,128]{3,2,1,0:T(8,128)(2,1)S(1)} %collective-permute-done.refs_1_), channel_id=1, source_target_pairs={{0,1},{1,0},{2,3},{3,2},{4,5},{5,4},{6,7},{7,6},{8,9},{9,8},{10,11... | collective-permute-start | bytes 1572872 | tf_op jit(solution)/shard_map/ppermute | solution.py:140
  69.8 5.9 %collective-permute-start.7 = (bf16[16,2,64,128]{3,2,1,0:T(8,128)(2,1)S(1)}, bf16[16,2,64,128]{3,2,1,0:T(8,128)(2,1)}, u32[]{:S(2)}, u32[]{:S(2)}) collective-permute-start(bf16[16,2,64,128]{3,2,1,0:T(8,128)(2,1)S(1)} %collective-permute-done.2.refs_2_), channel_id=1, source_target_pairs={{0,1},{1,0},{2,3},{3,2},{4,5},{5,4},{6,7},{7,6},{8,9},{9,8},{10,11... | collective-permute-start | bytes 1572872 | tf_op jit(solution)/shard_map/ppermute | solution.py:140
  75.7 1.9 %collective-permute-start.8 = (bf16[16,2,64,128]{3,2,1,0:T(8,128)(2,1)S(1)}, bf16[16,2,64,128]{3,2,1,0:T(8,128)(2,1)}, u32[]{:S(2)}, u32[]{:S(2)}) collective-permute-start(bf16[16,2,64,128]{3,2,1,0:T(8,128)(2,1)S(1)} %collective-permute-done.4.refs_3_), channel_id=1, source_target_pairs={{0,1},{1,0},{2,3},{3,2},{4,5},{5,4},{6,7},{7,6},{8,9},{9,8},{10,11... | collective-permute-start | bytes 1572872 | tf_op jit(solution)/shard_map/ppermute | solution.py:140
  77.7 2.0 %collective-permute-done.8.refs_7_ = bf16[16,2,64,128]{3,2,1,0:T(8,128)(2,1)} collective-permute-done((bf16[16,2,64,128]{3,2,1,0:T(8,128)(2,1)S(1)}, bf16[16,2,64,128]{3,2,1,0:T(8,128)(2,1)}, u32[]{:S(2)}, u32[]{:S(2)}) %collective-permute-start.8) | collective-permute-done | bytes 524320 | tf_op jit(solution)/shard_map/ppermute | solution.py:140
  79.6 10.8 %shard_map.46 = bf16[8,32,1024]{2,1,0:T(8,128)(2,1)S(1)} custom-call(s32[1]{0:T(128)} %bitcast.core_ref, s32[4,17]{1,0:T(4,128)S(1)} %pad_add_fusion.entries, bf16[8,32,1024]{2,1,0:T(8,128)(2,1)S(1)} %all-to-all-done.2.q_ref, bf16[16,2,64,128]{3,2,1,0:T(8,128)(2,1)S(1)} %bitcast.32, bf16[16,2,64,128]{3,2,1,0:T(8,128)(2,1)S(1)} %collective-permute-done.refs_1_, ...), custom_call_target="tpu_custom_call" | custom-call | flops 2147483648 | bytes 8388608 | tf_op jit(solution)/shard_map/pallas_call | solution.py:110
  90.5 22.3 %all_to_all.21 = bf16[8,32,1024]{2,1,0:T(8,128)(2,1)S(1)} all-to-all(bf16[8,32,1024]{2,1,0:T(8,128)(2,1)S(1)} %shard_map.46), channel_id=1, replica_groups=mesh['z2'=2,'z1'=2,'z0'=2,'x'=4,'y0'=2,'y2'=2,'y1'=2,'core'=2] {'y0','y1..., dimensions={0} | all-to-all | bytes 1048576 | tf_op jit(solution)/shard_map/all_to_all | solution.py:184
  112.8 0.8 copy.14
  (28 shorter events, 0.3 us)
Async XLA Ops:
  0.0 0.7 copy-start.1
  16.9 8.6 %copy-start = (bf16[32,8192]{1,0:T(8,128)(2,1)S(1)}, bf16[32,8192]{1,0:T(8,128)(2,1)}, u32[]{:S(2)}) copy-start(bf16[32,8192]{1,0:T(8,128)(2,1)} %param.4) | copy-start | bytes 1572868
  16.9 23.6 %all-to-all-start.1 = ((bf16[8,2,2,64,128]{4,3,2,1,0:T(8,128)(2,1)}), bf16[8,2,2,64,128]{4,3,2,1,0:T(8,128)(2,1)S(1)}, u32[]{:S(2)}, u32[]{:S(2)}) async-start(bf16[8,2,2,64,128]{4,3,2,1,0:T(8,128)(2,1)} %broadcast_in_dim.25), calls=%async_computation.1 | async-start | bytes 1048576 | tf_op jit(solution)/shard_map/all_to_all | solution.py:164
  40.5 15.1 %collective-permute-start = (bf16[16,2,64,128]{3,2,1,0:T(8,128)(2,1)S(1)}, bf16[16,2,64,128]{3,2,1,0:T(8,128)(2,1)S(1)}, u32[]{:S(2)}, u32[]{:S(2)}) collective-permute-start(bf16[16,2,64,128]{3,2,1,0:T(8,128)(2,1)S(1)} %bitcast.29), channel_id=1, source_target_pairs={{0,16},{1,49},{16,32},{17,1},{32,48},{33,17},{48,0},{49,33},{2,18}... | collective-permute-start | bytes 1572872 | tf_op jit(solution)/shard_map/ppermute | solution.py:146
  44.9 24.9 %all-to-all-start.2 = ((bf16[8,32,1024]{2,1,0:T(8,128)(2,1)}), bf16[8,32,1024]{2,1,0:T(8,128)(2,1)S(1)}, u32[]{:S(2)}, u32[]{:S(2)}) async-start(bf16[8,32,1024]{2,1,0:T(8,128)(2,1)} %bitcast.27), calls=%async_computation.2 | async-start | bytes 1048576 | tf_op jit(solution)/shard_map/all_to_all | solution.py:170
  48.6 7.1 %collective-permute-start.1 = (bf16[2,64,128]{2,1,0:T(8,128)(2,1)S(1)}, bf16[2,64,128]{2,1,0:T(8,128)(2,1)S(1)}, u32[]{:S(2)}, u32[]{:S(2)}) collective-permute-start(bf16[2,64,128]{2,1,0:T(8,128)(2,1)S(1)} %slice_bitcast_fusion), channel_id=1, source_target_pairs={{0,16},{16,32},{32,48},{48,64},{64,80},{80,96},{96,112},{112,128},... | collective-permute-start | bytes 98312 | tf_op jit(solution)/shard_map/ppermute | solution.py:172
  55.6 14.2 %collective-permute-start.2 = (bf16[16,2,64,128]{3,2,1,0:T(8,128)(2,1)S(1)}, bf16[16,2,64,128]{3,2,1,0:T(8,128)(2,1)S(1)}, u32[]{:S(2)}, u32[]{:S(2)}) collective-permute-start(bf16[16,2,64,128]{3,2,1,0:T(8,128)(2,1)S(1)} %bitcast.30), channel_id=1, source_target_pairs={{0,48},{1,17},{16,0},{17,33},{32,16},{33,49},{48,32},{49,1},{2,50}... | collective-permute-start | bytes 1572872 | tf_op jit(solution)/shard_map/ppermute | solution.py:146
  57.6 18.1 %collective-permute-start.4 = (bf16[16,2,64,128]{3,2,1,0:T(8,128)(2,1)S(1)}, bf16[16,2,64,128]{3,2,1,0:T(8,128)(2,1)S(1)}, u32[]{:S(2)}, u32[]{:S(2)}) collective-permute-start(bf16[16,2,64,128]{3,2,1,0:T(8,128)(2,1)S(1)} %collective-permute-done.refs_1_), channel_id=1, source_target_pairs={{0,16},{1,49},{16,32},{17,1},{32,48},{33,17},{48,0},{49,33},{2,18}... | collective-permute-start | bytes 1572872 | tf_op jit(solution)/shard_map/ppermute | solution.py:146
  62.3 7.5 %collective-permute-start.3 = (bf16[3,2,64,128]{3,2,1,0:T(8,128)(2,1)S(1)}, bf16[3,2,64,128]{3,2,1,0:T(8,128)(2,1)S(1)}, u32[]{:S(2)}, u32[]{:S(2)}) collective-permute-start(bf16[3,2,64,128]{3,2,1,0:T(8,128)(2,1)S(1)} %pad_maximum_fusion.1.refs_8_), channel_id=1, source_target_pairs={{0,1},{1,0},{2,3},{3,2},{4,5},{5,4},{6,7},{7,6},{8,9},{9,8},{10,11... | collective-permute-start | bytes 294920 | tf_op jit(solution)/shard_map/ppermute | solution.py:140
  65.5 12.2 %collective-permute-start.5 = (bf16[16,2,64,128]{3,2,1,0:T(8,128)(2,1)S(1)}, bf16[16,2,64,128]{3,2,1,0:T(8,128)(2,1)S(1)}, u32[]{:S(2)}, u32[]{:S(2)}) collective-permute-start(bf16[16,2,64,128]{3,2,1,0:T(8,128)(2,1)S(1)} %bitcast.31), channel_id=1, source_target_pairs={{0,1},{1,0},{2,3},{3,2},{4,5},{5,4},{6,7},{7,6},{8,9},{9,8},{10,11... | collective-permute-start | bytes 1572872 | tf_op jit(solution)/shard_map/ppermute | solution.py:140
  67.4 10.3 %collective-permute-start.6 = (bf16[16,2,64,128]{3,2,1,0:T(8,128)(2,1)S(1)}, bf16[16,2,64,128]{3,2,1,0:T(8,128)(2,1)}, u32[]{:S(2)}, u32[]{:S(2)}) collective-permute-start(bf16[16,2,64,128]{3,2,1,0:T(8,128)(2,1)S(1)} %collective-permute-done.refs_1_), channel_id=1, source_target_pairs={{0,1},{1,0},{2,3},{3,2},{4,5},{5,4},{6,7},{7,6},{8,9},{9,8},{10,11... | collective-permute-start | bytes 1572872 | tf_op jit(solution)/shard_map/ppermute | solution.py:140
  69.8 7.8 %collective-permute-start.7 = (bf16[16,2,64,128]{3,2,1,0:T(8,128)(2,1)S(1)}, bf16[16,2,64,128]{3,2,1,0:T(8,128)(2,1)}, u32[]{:S(2)}, u32[]{:S(2)}) collective-permute-start(bf16[16,2,64,128]{3,2,1,0:T(8,128)(2,1)S(1)} %collective-permute-done.2.refs_2_), channel_id=1, source_target_pairs={{0,1},{1,0},{2,3},{3,2},{4,5},{5,4},{6,7},{7,6},{8,9},{9,8},{10,11... | collective-permute-start | bytes 1572872 | tf_op jit(solution)/shard_map/ppermute | solution.py:140
  75.7 3.9 %collective-permute-start.8 = (bf16[16,2,64,128]{3,2,1,0:T(8,128)(2,1)S(1)}, bf16[16,2,64,128]{3,2,1,0:T(8,128)(2,1)}, u32[]{:S(2)}, u32[]{:S(2)}) collective-permute-start(bf16[16,2,64,128]{3,2,1,0:T(8,128)(2,1)S(1)} %collective-permute-done.4.refs_3_), channel_id=1, source_target_pairs={{0,1},{1,0},{2,3},{3,2},{4,5},{5,4},{6,7},{7,6},{8,9},{9,8},{10,11... | collective-permute-start | bytes 1572872 | tf_op jit(solution)/shard_map/ppermute | solution.py:140
